TPU v7x, 32 devices: a whole 2x2x4 slice. The times are simulated.
32 devices in a mesh: blk: 4 (over y, x), band: 8 (over z, core).
Axes of the slice: x: 2, y: 2, z: 4, core: 2. Of those that a mesh axis runs over, the one named last changes fastest.
Arguments:
- fine_blocks: float32 [128, 64, 256], P(('blk', 'band')), may hold values from -3 to 3
- source_group: int32 [128, 4], P(('blk', 'band')), may hold values from 0 to 3, all different within a row; in each aligned block of 4 rows (0 to 3, 4 to 7, ...) at most 4 rows name the same one
- source_row: int32 [128, 4], P(('blk', 'band')), may hold values from 0 to 3
- prolong_blocks: float32 [128, 64, 128], P(('blk', 'band')), may hold values from -0.75 to 0.75
- prolong_code: int32 [128, 2], P(('blk', 'band')), may hold values from 0 to 2
Outputs:
- coarse_rows: float32 [2048, 1280], P(('blk', 'band'))
Inputs may be any that keep to these rules, and one draw needn't show every extreme that they name: `source_group`: each fine block row names 4 different groups; among the rows of one device no group is named more than 4 times, and some device names one group exactly 4 times.
All inputs are finite; a program needn't handle non-finite values.
Results may differ from a plain program's by a relative error of at most 0.0003.
Values sent between devices are 32-bit elements; how exact they have to be, the bound alone decides.
No kernel may reach another device: no remote copies, remote signals or barrier semaphores. Data moves between devices by JAX's collectives and lax.ppermute only.
A program may use at most 64 MiB of HBM per device.

v0:
```python
import jax
import jax.numpy as jnp
from jax import lax
from jax.sharding import PartitionSpec as P

CB = 1


precise = lax.Precision.HIGHEST


def with_halo(cells, sides, width):
    for axis, dim in sides:
        count = lax.axis_size(axis)
        head = lax.slice_in_dim(cells, 0, width, axis=dim)
        tail = lax.slice_in_dim(cells, cells.shape[dim] - width, cells.shape[dim], axis=dim)
        cells = jnp.concatenate(
            [
                lax.ppermute(tail, axis, [(i, (i + 1) % count) for i in range(count)]),
                cells,
                lax.ppermute(head, axis, [((i + 1) % count, i) for i in range(count)]),
            ],
            axis=dim,
        )
    return cells


def expand_codes(blocks, code_rows, slot_total):
    block_width = blocks.shape[-2]
    code_total = code_rows.shape[-1]
    shaped = blocks.reshape(blocks.shape[:-1] + (code_total, block_width))
    picker = (code_rows[..., None] == jnp.arange(slot_total, dtype=jnp.int32)).astype(jnp.float32)
    placed = jnp.einsum("...anx,...nj->...ajx", shaped, picker, precision=precise)
    return placed.reshape(blocks.shape[:-1] + (slot_total * block_width,))


def body(fine_blocks, source_group, source_row, prolong_blocks, prolong_code):
    block_width = prolong_blocks.shape[1]
    fine_rows = prolong_blocks.shape[0]
    per_row = fine_blocks.shape[2] // block_width
    slot_total = 3 * CB
    window = slot_total * block_width
    groups = lax.axis_size("blk")
    bucket_depth = min(fine_rows, 2 * fine_rows * per_row // groups)
    total_blocks = fine_rows * per_row
    blocks_flat = fine_blocks.reshape(fine_rows, block_width, per_row, block_width).transpose(
        0, 2, 1, 3
    )
    blocks_flat = blocks_flat.reshape(total_blocks, block_width, block_width)
    group_flat = source_group.reshape(total_blocks)
    row_flat = source_row.reshape(total_blocks)
    target_row = jnp.arange(total_blocks, dtype=jnp.int32) // per_row
    member = (group_flat[None, :] == jnp.arange(groups, dtype=jnp.int32)[:, None]).astype(jnp.int32)
    position = jnp.cumsum(member, axis=1) - 1
    depth_range = jnp.arange(bucket_depth, dtype=jnp.int32)
    matched = (member[:, None, :] == 1) & (position[:, None, :] == depth_range[None, :, None])
    block_range = jnp.arange(total_blocks, dtype=jnp.int32)
    bucket_block = jnp.sum(jnp.where(matched, block_range[None, None, :], 0), axis=2)
    bucket_on = jnp.any(matched, axis=2).astype(jnp.float32)
    own_window = expand_codes(prolong_blocks, prolong_code, slot_total)
    restrict = own_window.reshape(fine_rows * block_width, window)
    portion_blocks = lax.all_gather(prolong_blocks, "blk", axis=0, tiled=True)
    portion_code = lax.all_gather(prolong_code, "blk", axis=0, tiled=True)
    span_groups = portion_blocks.shape[0] // fine_rows
    local_row = (
        jnp.arange(span_groups, dtype=jnp.int32)[:, None] * fine_rows + row_flat[bucket_block]
    )
    gathered = expand_codes(portion_blocks[local_row], portion_code[local_row], slot_total)
    picked = blocks_flat[bucket_block] * bucket_on[..., None, None]
    product = jnp.einsum("qsab,qsby->qsay", picked, gathered, precision=precise)
    landing = (
        target_row[bucket_block][..., None] == jnp.arange(fine_rows, dtype=jnp.int32)
    ).astype(jnp.float32)
    applied = jnp.einsum("qsi,qsay->qiay", landing, product, precision=precise)
    applied = applied.reshape(applied.shape[0], fine_rows * block_width, window)
    collected = jnp.einsum("rj,qry->qjy", restrict, applied, precision=precise)
    coarse_height = CB * block_width
    band_width = groups * CB * block_width
    partial_value = collected.reshape(groups, 3, coarse_height, 3, CB, block_width).transpose(
        1, 2, 3, 0, 4, 5
    )
    partial_value = partial_value.reshape(3, coarse_height, 3 * band_width)
    padded = with_halo(partial_value, (("band", 0),), 1)
    lower = padded[0].reshape(coarse_height, 3, band_width)
    middle = padded[2].reshape(coarse_height, 3, band_width)
    upper = padded[4].reshape(coarse_height, 3, band_width)
    summed = jnp.pad(lower, ((0, 0), (0, 2), (0, 0))) + jnp.pad(middle, ((0, 0), (1, 1), (0, 0)))
    summed = summed + jnp.pad(upper, ((0, 0), (2, 0), (0, 0)))
    return summed.reshape(coarse_height, 5 * band_width)


def solution(mesh):
    return jax.shard_map(
        body,
        mesh=mesh,
        in_specs=(
            P(("blk", "band"), None, None),
            P(("blk", "band"), None),
            P(("blk", "band"), None),
            P(("blk", "band"), None, None),
            P(("blk", "band"), None),
        ),
        out_specs=P(("blk", "band"), None),
        check_vma=False,
    )
```

profile of v0, /device:TPU:0, one launch (start us, length us, event | category | flops | bytes accessed | tf_op | source)
XLA Modules:
  0.0 51.8 jit_solution(6710563241196859554)
XLA Ops:
  0.0 0.8 %eq.86 = s32[16]{0:T(128)S(1)} reshape(s32[4,4]{1,0:T(4,128)} %param.6) | data formatting | bytes 128 | tf_op jit(solution)/shard_map/eq | solution.py:53
  0.8 0.2 reduce_window_sum.11
  1.3 11.8 %all_gather.7 = f32[16,64,128]{2,1,0:T(8,128)S(1)} all-gather(f32[4,64,128]{2,1,0:T(8,128)} %param.8), channel_id=1, replica_groups=mesh['blk'=4,'band'=8] {'blk'}, dimensions={0}, use_global_device_ids=true | all-gather | bytes 655360 | tf_op jit(solution)/shard_map/all_gather | solution.py:62
  13.1 1.1 %reshape.143 = f32[4,64,2,64]{3,2,1,0:T(2,128)S(1)} reshape(f32[4,64,128]{2,1,0:T(8,128)} %param.8) | data formatting | bytes 262144 | tf_op jit(solution)/shard_map/reshape | solution.py:31
  14.2 0.8 %reshape.139 = s32[16]{0:T(128)S(1)} reshape(s32[4,4]{1,0:T(4,128)} %param.7) | data formatting | bytes 128 | tf_op jit(solution)/shard_map/reshape | solution.py:51
  15.1 0.7 %gather_fusion.2 = s32[16]{0:T(128)S(1)} fusion(s32[16]{0:T(128)S(1)} %reshape.139, s32[1024]{0:T(1024)S(1)} %pad_clamp_fusion.1), kind=kCustom, calls=%fused_computation.2 | custom fusion | bytes 192 | tf_op jit(solution)/shard_map/gather | solution.py:66
  16.0 0.6 %gather_fusion.4 = f32[16,64,128]{2,1,0:T(8,128)S(1)} fusion(f32[16,64,128]{2,1,0:T(8,128)S(1)} %all_gather.7, s32[1024]{0:T(1024)S(1)} %pad_clamp_fusion), kind=kCustom, calls=%fused_computation.4 | custom fusion | bytes 1048640 | tf_op jit(solution)/shard_map/gather | solution.py:68
  16.6 0.6 %reshape.140 = f32[4,4,64,2,64]{4,3,2,1,0:T(2,128)S(1)} reshape(f32[16,64,128]{2,1,0:T(8,128)S(1)} %gather_fusion.4) | data formatting | bytes 1048576 | tf_op jit(solution)/shard_map/reshape | solution.py:31
  17.3 7.7 %all-gather = s32[4,4,2]{1,2,0:T(2,128)S(1)} all-gather(s32[1,4,2]{1,2,0:T(2,128)S(1)} %bitcast.59), channel_id=1, replica_groups=mesh['blk'=4,'band'=8] {'blk'}, dimensions={0}, use_global_device_ids=true | all-gather | bytes 160 | tf_op jit(solution)/shard_map/all_gather | solution.py:63
  25.1 0.6 %gather_fusion.3 = s32[16,2]{1,0:T(8,128)S(1)} fusion(s32[16,2]{1,0:T(8,128)S(1)} %bitcast.57, s32[1024]{0:T(1024)S(1)} %pad_clamp_fusion), kind=kCustom, calls=%fused_computation.3 | custom fusion | bytes 320 | tf_op jit(solution)/shard_map/gather | solution.py:68
  25.7 2.8 %convolution_bitcast_fusion = f32[4,4,64,3,64]{4,3,2,1,0:T(4,128)S(1)} fusion(f32[4,4,64,2,64]{4,3,2,1,0:T(2,128)S(1)} %reshape.140, s32[4,4,2]{2,1,0:T(4,128)S(1)} %bitcast.58), kind=kOutput, calls=%fused_computation.5 | convolution fusion | flops 4718688 | bytes 1310848 | tf_op jit(solution)/shard_map/...anx,...nj->...ajx/dot_general | solution.py:33
  28.5 1.6 %copy.46 = f32[4,4,64,3,64]{2,4,3,1,0:T(8,128)} copy(f32[4,4,64,3,64]{4,3,2,1,0:T(4,128)S(1)} %convolution_bitcast_fusion) | data formatting | bytes 1572864 | tf_op jit(solution)/shard_map/...anx,...nj->...ajx/transpose | solution.py:33
  30.3 0.6 %gather_fusion.1 = f32[16,64,64]{2,1,0:T(8,128)S(1)} fusion(f32[16,64,64]{2,1,0:T(8,128)S(1)} %bitcast.54, s32[1024]{0:T(1024)S(1)} %pad_clamp_fusion.1), kind=kCustom, calls=%fused_computation.1 | custom fusion | bytes 524352 | tf_op jit(solution)/shard_map/gather | solution.py:69
  30.9 0.7 %gather_fusion = s32[16]{0:T(128)S(1)} fusion(s32[16]{0:T(128)S(1)} %and_select_fusion, s32[1024]{0:T(1024)S(1)} %pad_clamp_fusion.1), kind=kCustom, calls=%fused_computation | custom fusion | bytes 192 | tf_op jit(solution)/shard_map/gather | solution.py:72
  31.7 3.2 %fusion.2 = f32[4,4,64,192]{3,2,1,0:T(8,128)S(1)} fusion(f32[4,4,64,192]{2,3,1,0:T(8,128)S(1)} %bitcast.51, f32[4,4,64,64]{3,2,1,0:T(8,128)S(1)} %bitcast.56, f32[4,4]{1,0:T(4,128)S(1)} %convert_element_type.28), kind=kOutput, calls=%fused_computation.12 | convolution fusion | flops 151060480 | bytes 1835072 | tf_op jit(solution)/shard_map/qsab,qsby->qsay/dot_general | solution.py:70
  34.9 1.7 %fusion = f32[4,4,64,192]{3,1,2,0:T(4,128)S(1)} fusion(f32[4,4,64,192]{3,2,1,0:T(8,128)S(1)} %fusion.2, s32[4,4]{1,0:T(4,128)S(1)} %reshape.147), kind=kOutput, calls=%fused_computation.8 | convolution fusion | flops 9437248 | bytes 1572928 | tf_op jit(solution)/shard_map/qsi,qsay->qiay/dot_general | solution.py:74
  36.7 0.8 %convolution_bitcast_fusion.2 = f32[4,64,3,64]{3,2,1,0:T(4,128)S(1)} fusion(f32[4,64,2,64]{3,2,1,0:T(2,128)S(1)} %reshape.143, s32[4,2]{1,0:T(4,128)S(1)} %copy.50), kind=kOutput, calls=%fused_computation.7 | convolution fusion | flops 1179672 | bytes 327712 | tf_op jit(solution)/shard_map/...anx,...nj->...ajx/dot_general | solution.py:33
  37.6 0.3 reshape.199
  37.9 1.8 %convolution_bitcast_fusion.1 = f32[4,192,192]{1,2,0:T(8,128)S(1)} fusion(f32[4,256,192]{2,1,0:T(8,128)S(1)} %bitcast.53, f32[256,192]{1,0:T(8,128)S(1)} %reshape.199), kind=kOutput, calls=%fused_computation.6 | convolution fusion | flops 452984832 | bytes 1572864 | tf_op jit(solution)/shard_map/rj,qry->qjy/dot_general | solution.py:76
  39.7 0.3 copy.53
  40.0 0.5 reshape.144
  40.5 0.3 fusion.20
  40.8 0.3 copy.57
  41.0 0.3 slice.36
  41.4 0.3 copy.54
  41.6 0.3 slice.33
  41.9 0.5 %collective-permute-start = (f32[1,64,768]{2,1,0:T(8,128)S(1)}, f32[1,64,768]{2,1,0:T(8,128)S(1)}, u32[]{:S(2)}, u32[]{:S(2)}) collective-permute-start(f32[1,64,768]{2,1,0:T(8,128)S(1)} %slice.33), channel_id=1, source_target_pairs={{0,1},{1,2},{2,3},{3,4},{4,5},{5,6},{6,7},{7,0},{8,9},{9,10},{10,1... | collective-permute-start | bytes 589832 | tf_op jit(solution)/shard_map/ppermute | solution.py:19
  42.4 0.3 copy.66
  42.7 0.3 reshape.200
  43.0 2.0 %collective-permute-done.1 = f32[1,64,768]{2,1,0:T(8,128)S(1)} collective-permute-done((f32[1,64,768]{2,1,0:T(8,128)S(1)}, f32[1,64,768]{2,1,0:T(8,128)S(1)}, u32[]{:S(2)}, u32[]{:S(2)}) %collective-permute-start.1) | collective-permute-done | bytes 196640 | tf_op jit(solution)/shard_map/ppermute | solution.py:21
  45.1 5.6 %collective-permute-done = f32[1,64,768]{2,1,0:T(8,128)S(1)} collective-permute-done((f32[1,64,768]{2,1,0:T(8,128)S(1)}, f32[1,64,768]{2,1,0:T(8,128)S(1)}, u32[]{:S(2)}, u32[]{:S(2)}) %collective-permute-start) | collective-permute-done | bytes 196640 | tf_op jit(solution)/shard_map/ppermute | solution.py:19
  51.0 0.8 %copy.69 = f32[8,8,5,256]{3,1,2,0:T(8,128)} copy(f32[8,8,5,256]{3,2,1,0:T(8,128)S(1)} %bitcast.55) | data formatting | bytes 655360
  (30 shorter events, 1.8 us)
Async XLA Ops:
  15.8 1.5 %copy-start.2 = (s32[4,2]{0,1:T(2,128)S(1)}, s32[4,2]{0,1:T(2,128)}, u32[]{:S(2)}) copy-start(s32[4,2]{0,1:T(2,128)} %param.9) | copy-start | bytes 100
  28.5 1.6 %copy-start.1 = (f32[4,64,256]{2,1,0:T(8,128)S(1)}, f32[4,64,256]{2,1,0:T(8,128)}, u32[]{:S(2)}) copy-start(f32[4,64,256]{2,1,0:T(8,128)} %param.5) | copy-start | bytes 786436
  30.3 1.4 %copy-start = (f32[4,4,64,3,64]{2,4,3,1,0:T(8,128)S(1)}, f32[4,4,64,3,64]{2,4,3,1,0:T(8,128)}, u32[]{:S(2)}) copy-start(f32[4,4,64,3,64]{2,4,3,1,0:T(8,128)} %copy.46) | copy-start | bytes 2359300
  41.3 3.7 %collective-permute-start.1 = (f32[1,64,768]{2,1,0:T(8,128)S(1)}, f32[1,64,768]{2,1,0:T(8,128)S(1)}, u32[]{:S(2)}, u32[]{:S(2)}) collective-permute-start(f32[1,64,768]{2,1,0:T(8,128)S(1)} %slice.36), channel_id=1, source_target_pairs={{1,0},{2,1},{3,2},{4,3},{5,4},{6,5},{7,6},{0,7},{9,8},{10,9},{11,1... | collective-permute-start | bytes 589832 | tf_op jit(solution)/shard_map/ppermute | solution.py:21
  41.9 8.8 %collective-permute-start = (f32[1,64,768]{2,1,0:T(8,128)S(1)}, f32[1,64,768]{2,1,0:T(8,128)S(1)}, u32[]{:S(2)}, u32[]{:S(2)}) collective-permute-start(f32[1,64,768]{2,1,0:T(8,128)S(1)} %slice.33), channel_id=1, source_target_pairs={{0,1},{1,2},{2,3},{3,4},{4,5},{5,6},{6,7},{7,0},{8,9},{9,10},{10,1... | collective-permute-start | bytes 589832 | tf_op jit(solution)/shard_map/ppermute | solution.py:19
where the time goes:
time: 52.1 us; the launch traced here: 51.8 us
  blocking collectives  19.5 us (37%)
  local copies, waits for them, and re-layouts  12.8 us (25%)
  matrix products  10.2 us (20%)
  waiting for transfers between devices  7.61 us (15%)
  other arithmetic  0.82 us (2%)
  starting transfers between devices  0.6 us (1%)
    all_gather x1, blocking collectives, body(): portion_blocks = lax.all_gather(prolong_blocks, 'blk', axis=0, tiled=True)  11.8 us
    all_gather x1, blocking collectives, body(): portion_code = lax.all_gather(prolong_code, 'blk', axis=0, tiled=True)  7.69 us
    ppermute x1, waiting for transfers between devices, with_halo(): lax.ppermute(tail, axis, [(i, (i + 1) % count) for i in range(count)])  5.61 us
    dot_general x2, matrix products, expand_codes(): jnp.einsum('...anx,...nj->...ajx', shaped, picker, precision=precise)  3.61 us
    dot_general x1, matrix products, body(): product = jnp.einsum('qsab,qsby->qsay', picked, gathered, precision=precise)  3.16 us
    ppermute x1, waiting for transfers between devices, with_halo(): lax.ppermute(head, axis, [((i + 1) % count, i) for i in range(count)])  2 us
    dot_general x1, matrix products, body(): collected = jnp.einsum('rj,qry->qjy', restrict, applied, precision=precise)  1.81 us
    reshape x2, local copies, waits for them, and re-layouts, expand_codes(): shaped = blocks.reshape(blocks.shape[:-1] + (code_total, block_width))  1.7 us
  transfers between devices with their start and end apart: 2, of which 2 were waited for; matrix products, arithmetic and copies ran while one was open for 2% of the time, Pallas kernels for 0%

commit v1 on v0

v1 whole, which is shorter than its diff:
```python
import functools

import jax
import jax.numpy as jnp
from jax import lax
from jax.experimental import pallas as pl
from jax.experimental.pallas import tpu as pltpu
from jax.sharding import PartitionSpec as P

SHIFTS = 3


def vmem():
    return pl.BlockSpec(memory_space=pltpu.VMEM)


def smem():
    return pl.BlockSpec(memory_space=pltpu.SMEM)


def split(x):
    hi = x.astype(jnp.bfloat16)
    return hi, (x - hi.astype(jnp.float32)).astype(jnp.bfloat16)


def dot(a, b):
    return lax.dot_general(a, b, (((1,), (0,)), ((), ())), preferred_element_type=jnp.float32)


def dot3(a_hi, a_lo, b_hi, b_lo):
    return dot(a_hi, b_hi) + (dot(a_hi, b_lo) + dot(a_lo, b_hi))


def pack_kernel(width, code_ref, p_ref, out_ref):
    rows = p_ref.shape[0]
    for i in range(rows):
        out_ref[i * width : (i + 1) * width, :] = p_ref[i]
    lane = lax.broadcasted_iota(jnp.int32, (1, 2 * width), 1)
    left = lane < width
    masks = []
    for i in range(rows):
        c0, c1 = code_ref[i, 0], code_ref[i, 1]
        straight = jnp.where(left, c0, c1)
        crossed = jnp.where(left, c1, c0)
        near = jnp.where(left, 0, 1)
        far = jnp.where(left, 2, -1)
        masks += [straight == near, crossed == near, straight == far, crossed == far]
    out_ref[rows * width :, :] = jnp.concatenate([m.astype(jnp.float32) for m in masks], axis=0)


def left_kernel(width, groups, group_ref, code_ref, a_ref, p_ref, hi_ref, lo_ref):
    rows, per_row = group_ref.shape
    me = lax.axis_index("blk")
    odd = lax.axis_index("band") % 2
    pair = 2 * width
    wide = rows * width
    pt = p_ref[...].reshape(wide, pair).T
    row_of = lax.broadcasted_iota(jnp.int32, (1, wide), 1) // width
    codes = []
    for n in range(2):
        c = jnp.full((1, wide), code_ref[0, n], jnp.int32)
        for i in range(1, rows):
            c = jnp.where(row_of == i, code_ref[i, n], c)
        codes.append(c)
    blocks = []
    for dest in (1, 2 - 2 * odd, 2 * odd):
        blocks.append(
            jnp.where(codes[0] == dest, pt[:width], 0.0) + jnp.where(codes[1] == dest, pt[width:], 0.0)
        )
    rt_hi, rt_lo = split(jnp.concatenate(blocks, axis=0))
    half = lax.broadcasted_iota(jnp.int32, (width, pair), 1) // width
    for p in range(rows // 2):
        tops = []
        for h in range(2):
            i = 2 * p + h
            cells = []
            for k in range(per_row):
                x = a_ref[i, :, (k // 2) * pair : (k // 2 + 1) * pair]
                if k % 2 != h:
                    x = pltpu.roll(x, width, 1)
                cells.append(jnp.where(half == h, x, 0.0))
            tops.append(cells)
        lanes = slice(p * pair, (p + 1) * pair)
        for j in range(groups):
            g = me ^ j
            parts = []
            for h in range(2):
                x = jnp.zeros((width, pair), jnp.float32)
                for k in range(per_row):
                    x = jnp.where(group_ref[2 * p + h, k] == g, tops[h][k], x)
                parts.append(x)
            b_hi, b_lo = split(jnp.concatenate(parts, axis=0))
            left = dot3(rt_hi[:, lanes], rt_lo[:, lanes], b_hi, b_lo)
            l_hi, l_lo = split(left)
            hi_ref[j, :, lanes] = l_hi
            lo_ref[j, :, lanes] = l_lo


def right_kernel(width, groups, group_ref, row_ref, hi_ref, lo_ref, *refs):
    sources, (own_ref, chip_ref, far_ref) = refs[:groups], refs[groups:]
    rows, per_row = group_ref.shape
    me = lax.axis_index("blk")
    pair = 2 * width
    right_half = lax.broadcasted_iota(jnp.int32, (width, pair), 1) >= width
    for q in range(groups // 2):
        found = []
        for j in (2 * q, 2 * q + 1):
            g = me ^ j
            src = sources[j]
            near, far = [], []
            for i in range(rows):
                s = jnp.int32(0)
                for k in range(per_row):
                    s = jnp.where(group_ref[i, k] == g, row_ref[i, k], s)
                x = src[pl.ds(pl.multiple_of(s * width, width), width), :]
                y = pltpu.roll(x, width, 1)
                m = [src[pl.ds(rows * width + 4 * s + t, 1), :] for t in range(4)]
                near.append(x * m[0] + y * m[1])
                far.append(x * m[2] + y * m[3])
            w = jnp.concatenate([jnp.concatenate(near, axis=0), jnp.concatenate(far, axis=0)], axis=1)
            w_hi, w_lo = split(w)
            found.append(dot3(hi_ref[j], lo_ref[j], w_hi, w_lo))
        swap = me % 2 == 1
        base = ((me ^ (2 * q)) // 2) * pair
        for t, out_ref in enumerate((own_ref, chip_ref, far_ref)):
            a, b = (f[t * width : (t + 1) * width] for f in found)
            first = jnp.where(swap, b, a)
            second = jnp.where(swap, a, b)
            for e in range(SHIFTS):
                tile = slice((e // 2) * pair, (e // 2 + 1) * pair)
                u, v = first[:, tile], second[:, tile]
                if e % 2 == 0:
                    v = pltpu.roll(v, width, 1)
                else:
                    u = pltpu.roll(u, width, 1)
                place = pl.multiple_of(e * groups * width + base, pair)
                out_ref[:, pl.ds(place, pair)] = jnp.where(right_half, v, u)


def add_kernel(step, own_ref, chip_ref, far_ref, out_ref):
    odd = lax.axis_index("band") % 2 == 1
    upper = lambda t: jnp.where(odd, far_ref[:, t], chip_ref[:, t])
    lower = lambda t: jnp.where(odd, chip_ref[:, t], far_ref[:, t])
    at = [slice(e * step, (e + 1) * step) for e in range(5)]
    out_ref[:, at[0]] = lower(at[0])
    out_ref[:, at[1]] = lower(at[1]) + own_ref[:, at[0]]
    out_ref[:, at[2]] = lower(at[2]) + own_ref[:, at[1]] + upper(at[0])
    out_ref[:, at[3]] = own_ref[:, at[2]] + upper(at[1])
    out_ref[:, at[4]] = upper(at[2])


def body(fine_blocks, source_group, source_row, prolong_blocks, prolong_code):
    rows, width, pair = prolong_blocks.shape
    groups = lax.axis_size("blk")
    bands = lax.axis_size("band")
    f32 = jnp.float32
    packed_rows = rows * width + 4 * rows
    packed = pl.pallas_call(
        functools.partial(pack_kernel, width),
        out_shape=jax.ShapeDtypeStruct((packed_rows, pair), f32),
        in_specs=[smem(), vmem()],
        out_specs=vmem(),
        name="pack",
    )(prolong_code, prolong_blocks)
    arrived = [packed] + [
        lax.ppermute(packed, "blk", [(i, i ^ j) for i in range(groups)]) for j in range(1, groups)
    ]
    height = SHIFTS * width
    deep = rows * width
    hi, lo = pl.pallas_call(
        functools.partial(left_kernel, width, groups),
        out_shape=[jax.ShapeDtypeStruct((groups, height, deep), jnp.bfloat16)] * 2,
        in_specs=[smem(), smem(), vmem(), vmem()],
        out_specs=[vmem()] * 2,
        cost_estimate=pl.CostEstimate(flops=2 * 3 * groups * height * 128 * deep, bytes_accessed=2000000, transcendentals=0),
        name="left",
    )(source_group, prolong_code, fine_blocks, prolong_blocks)
    own, chip, far = pl.pallas_call(
        functools.partial(right_kernel, width, groups),
        out_shape=[jax.ShapeDtypeStruct((width, SHIFTS * groups * width), f32)] * 3,
        in_specs=[smem()] * 2 + [vmem()] * (2 + groups),
        out_specs=[vmem()] * 3,
        name="right",
    )(source_group, source_row, hi, lo, *arrived)
    chip = lax.ppermute(chip, "band", [(i, i ^ 1) for i in range(bands)])
    far = lax.ppermute(far, "band", [(i, (i + 1 if i % 2 else i - 1) % bands) for i in range(bands)])
    return pl.pallas_call(
        functools.partial(add_kernel, groups * width),
        out_shape=jax.ShapeDtypeStruct((width, 5 * groups * width), f32),
        in_specs=[vmem()] * 3,
        out_specs=vmem(),
        name="add",
    )(own, chip, far)


def solution(mesh):
    return jax.shard_map(
        body,
        mesh=mesh,
        in_specs=(
            P(("blk", "band"), None, None),
            P(("blk", "band"), None),
            P(("blk", "band"), None),
            P(("blk", "band"), None, None),
            P(("blk", "band"), None),
        ),
        out_specs=P(("blk", "band"), None),
        check_vma=False,
    )
```

time: 52.1 us -> 28.8 us (0.55)
  blocking collectives: 19.5 us -> 0 us
  matrix products: 10.2 us -> 0 us
  local copies, waits for them, and re-layouts: 12.8 us -> 2.65 us
  Pallas kernels: 0 us -> 8.8 us
  starting transfers between devices: 0.6 us -> 8.18 us
  waiting for transfers between devices: 7.61 us -> 8.99 us
  other arithmetic: 0.82 us -> 0 us
    all_gather x2 -> x0, blocking collectives: 19.5 us -> none  [the longest x1 11.8 us: body(): portion_blocks = lax.all_gather(prolong_blocks, 'blk', axis=0, tiled=True)]
    dot_general x5 -> x0, matrix products: 10.2 us -> none  [the longest x2 3.61 us: expand_codes(): jnp.einsum('...anx,...nj->...ajx', shaped, picker, precision=precise)]
    pallas_call x0 -> x4, Pallas kernels: none -> 8.8 us  [the longest x1 2.8 us: body(): pl.pallas_call(functools.partial(right_kernel, width, groups), out_shape=...]
    ppermute x2 -> x5, starting transfers between devices: 0.6 us -> 8.18 us  [the longest x3 4.46 us: body(): lax.ppermute(packed, 'blk', [(i, i ^ j) for i in range(groups)])]
    gather x7 -> x0, local copies, waits for them, and re-layouts: 3.21 us -> none  [the longest x2 0.74 us: body(): target_row[bucket_block][..., None]]
    reshape x4 -> x0, local copies, waits for them, and re-layouts: 2.93 us -> none  [the longest x2 1.7 us: expand_codes(): shaped = blocks.reshape(blocks.shape[:-1] + (code_total, block_width))]
    transpose x2 -> x0, local copies, waits for them, and re-layouts: 1.92 us -> none  [the longest x1 1.61 us: expand_codes(): jnp.einsum('...anx,...nj->...ajx', shaped, picker, precision=precise)]
    unnamed x9 -> x11, local copies, waits for them, and re-layouts: 1.1 us -> 2.65 us
  transfers between devices with their start and end apart: 2 -> 5, of which waited for: 2 -> 4; matrix products, arithmetic and copies ran while one was open for 2% -> 0% of each run, Pallas kernels for 0% -> 9%
where the time goes in v1:
time: 28.8 us; the launch traced here: 28.6 us
  waiting for transfers between devices  8.99 us (31%)
  Pallas kernels  8.8 us (31%)
  starting transfers between devices  8.18 us (28%)
  local copies, waits for them, and re-layouts  2.65 us (9%)
    ppermute x1, waiting for transfers between devices, body(): lax.ppermute(far, 'band', [(i, (i + 1 if i % 2 else i - 1) % bands) for i...  4.96 us
    ppermute x3, starting transfers between devices, body(): lax.ppermute(packed, 'blk', [(i, i ^ j) for i in range(groups)])  4.46 us
    ppermute x3, waiting for transfers between devices, body(): lax.ppermute(packed, 'blk', [(i, i ^ j) for i in range(groups)])  4.03 us
    ppermute x1, starting transfers between devices, body(): lax.ppermute(far, 'band', [(i, (i + 1 if i % 2 else i - 1) % bands) for i...  3.71 us
    pallas_call x1, Pallas kernels, body(): pl.pallas_call(functools.partial(right_kernel, width, groups), out_shape=...  2.8 us
    unnamed x11, local copies, waits for them, and re-layouts  2.65 us
    pallas_call x1, Pallas kernels, body(): pl.pallas_call(functools.partial(left_kernel, width, groups), out_shape=[...  2.52 us
    pallas_call x1, Pallas kernels, body(): pl.pallas_call(functools.partial(add_kernel, groups * width), out_shape=j...  1.88 us
  transfers between devices with their start and end apart: 5, of which 4 were waited for; matrix products, arithmetic and copies ran while one was open for 0% of the time, Pallas kernels for 9%

profile of v1, /device:TPU:0, one launch (start us, length us, event | category | flops | bytes accessed | tf_op | source)
XLA Modules:
  0.0 28.6 jit_solution(15113210569468099830)
XLA Ops:
  0.0 1.3 %copy.6.code_ref = s32[4,2]{1,0:T(4,128)} copy(s32[4,2]{0,1:T(2,128)} %param.9) | data formatting | bytes 64 | tf_op args[4]
  1.3 1.6 %pack.1.refs_0_ = f32[272,128]{1,0:T(8,128)} custom-call(s32[4,2]{1,0:T(4,128)} %copy.6.code_ref, f32[4,64,128]{2,1,0:T(8,128)} %p_ref.3), custom_call_target="tpu_custom_call" | custom-call | tf_op jit(solution)/shard_map/pack/pallas_call | solution.py:158
  2.9 3.9 %collective-permute-start.2 = (f32[272,128]{1,0:T(8,128)}, f32[272,128]{1,0:T(8,128)S(1)}, u32[]{:S(2)}, u32[]{:S(2)}) collective-permute-start(f32[272,128]{1,0:T(8,128)} %pack.1.refs_0_), channel_id=1, source_target_pairs={{0,24},{8,16},{16,8},{24,0},{1,25},{9,17},{17,9},{25,1},{2,26},{10... | collective-permute-start | bytes 417800 | tf_op jit(solution)/shard_map/ppermute | solution.py:166
  6.8 0.5 %collective-permute-start.1 = (f32[272,128]{1,0:T(8,128)}, f32[272,128]{1,0:T(8,128)S(1)}, u32[]{:S(2)}, u32[]{:S(2)}) collective-permute-start(f32[272,128]{1,0:T(8,128)} %pack.1.refs_0_), channel_id=1, source_target_pairs={{0,16},{8,24},{16,0},{24,8},{1,17},{9,25},{17,1},{25,9},{2,18},{10... | collective-permute-start | bytes 417800 | tf_op jit(solution)/shard_map/ppermute | solution.py:166
  7.3 0.1 collective-permute-start
  7.4 2.5 %left.1 = (bf16[4,192,256]{2,1,0:T(8,128)(2,1)}, bf16[4,192,256]{2,1,0:T(8,128)(2,1)}) custom-call(s32[4,4]{1,0:T(4,128)} %group_ref.3, s32[4,2]{1,0:T(4,128)} %copy.6.code_ref, f32[4,64,256]{2,1,0:T(8,128)} %a_ref.1, f32[4,64,128]{2,1,0:T(8,128)} %p_ref.3), custom_call_target="tpu_custom_call" | custom-call | flops 150994944 | bytes 2000000 | tf_op jit(solution)/shard_map/left/pallas_call | solution.py:170
  9.9 1.3 %collective-permute-done.2.refs_3_ = f32[272,128]{1,0:T(8,128)S(1)} collective-permute-done((f32[272,128]{1,0:T(8,128)}, f32[272,128]{1,0:T(8,128)S(1)}, u32[]{:S(2)}, u32[]{:S(2)}) %collective-permute-start.2) | collective-permute-done | bytes 139296 | tf_op jit(solution)/shard_map/ppermute | solution.py:166
  11.2 0.0 copy-start.2
  11.2 2.5 %collective-permute-done.1.refs_2_ = f32[272,128]{1,0:T(8,128)S(1)} collective-permute-done((f32[272,128]{1,0:T(8,128)}, f32[272,128]{1,0:T(8,128)S(1)}, u32[]{:S(2)}, u32[]{:S(2)}) %collective-permute-start.1) | collective-permute-done | bytes 139296 | tf_op jit(solution)/shard_map/ppermute | solution.py:166
  13.7 0.0 copy-start.3
  13.7 0.3 collective-permute-done.refs_1_
  14.0 0.0 copy-start.4
  14.0 0.0 copy-done.2
  14.0 0.4 %copy-done.3 = f32[272,128]{1,0:T(8,128)} copy-done((f32[272,128]{1,0:T(8,128)}, f32[272,128]{1,0:T(8,128)S(1)}, u32[]{:S(2)}) %copy-start.3) | copy-done | bytes 139288
  14.4 0.2 copy-done.4
  14.6 2.8 %right.1 = (f32[64,768]{1,0:T(8,128)}, f32[64,768]{1,0:T(8,128)}, f32[64,768]{1,0:T(8,128)}) custom-call(s32[4,4]{1,0:T(4,128)} %group_ref.3, s32[4,4]{1,0:T(4,128)} %row_ref.1, bf16[4,192,256]{2,1,0:T(8,128)(2,1)} %get-tuple-element.10.hi_ref, bf16[4,192,256]{2,1,0:T(8,128)(2,1)} %get-tuple-element.11.lo_ref, f32[272,128]{1,0:T(8,128)} %pack.1.refs_0_, ...), custom_call_target="tpu_custom_call" | custom-call | tf_op jit(solution)/shard_map/right/pallas_call | solution.py:178
  17.4 0.0 collective-permute-start.3
  17.4 3.7 %collective-permute-start.4 = (f32[64,768]{1,0:T(8,128)}, f32[64,768]{1,0:T(8,128)S(1)}, u32[]{:S(2)}, u32[]{:S(2)}) collective-permute-start(f32[64,768]{1,0:T(8,128)} %get-tuple-element.14), channel_id=1, source_target_pairs={{0,7},{1,2},{2,1},{3,4},{4,3},{5,6},{6,5},{7,0},{8,15},{9,10},{10,... | collective-permute-start | bytes 589832 | tf_op jit(solution)/shard_map/ppermute | solution.py:186
  21.1 0.0 collective-permute-done.3.chip_ref
  21.1 0.0 copy-start
  21.1 5.0 %collective-permute-done.4.far_ref = f32[64,768]{1,0:T(8,128)S(1)} collective-permute-done((f32[64,768]{1,0:T(8,128)}, f32[64,768]{1,0:T(8,128)S(1)}, u32[]{:S(2)}, u32[]{:S(2)}) %collective-permute-start.4) | collective-permute-done | bytes 196640 | tf_op jit(solution)/shard_map/ppermute | solution.py:186
  26.1 0.0 copy-start.1
  26.1 0.0 copy-done
  26.1 0.7 %copy-done.1 = f32[64,768]{1,0:T(8,128)} copy-done((f32[64,768]{1,0:T(8,128)}, f32[64,768]{1,0:T(8,128)S(1)}, u32[]{:S(2)}) %copy-start.1) | copy-done | bytes 196632
  26.7 1.9 %add.1 = f32[64,1280]{1,0:T(8,128)} custom-call(f32[64,768]{1,0:T(8,128)} %get-tuple-element.12.own_ref, f32[64,768]{1,0:T(8,128)} %copy-done, f32[64,768]{1,0:T(8,128)} %copy-done.1), custom_call_target="tpu_custom_call" | custom-call | tf_op jit(solution)/shard_map/add/pallas_call | solution.py:187
Async XLA Ops:
  2.9 8.3 %collective-permute-start.2 = (f32[272,128]{1,0:T(8,128)}, f32[272,128]{1,0:T(8,128)S(1)}, u32[]{:S(2)}, u32[]{:S(2)}) collective-permute-start(f32[272,128]{1,0:T(8,128)} %pack.1.refs_0_), channel_id=1, source_target_pairs={{0,24},{8,16},{16,8},{24,0},{1,25},{9,17},{17,9},{25,1},{2,26},{10... | collective-permute-start | bytes 417800 | tf_op jit(solution)/shard_map/ppermute | solution.py:166
  6.8 6.9 %collective-permute-start.1 = (f32[272,128]{1,0:T(8,128)}, f32[272,128]{1,0:T(8,128)S(1)}, u32[]{:S(2)}, u32[]{:S(2)}) collective-permute-start(f32[272,128]{1,0:T(8,128)} %pack.1.refs_0_), channel_id=1, source_target_pairs={{0,16},{8,24},{16,0},{24,8},{1,17},{9,25},{17,1},{25,9},{2,18},{10... | collective-permute-start | bytes 417800 | tf_op jit(solution)/shard_map/ppermute | solution.py:166
  7.3 6.6 %collective-permute-start = (f32[272,128]{1,0:T(8,128)}, f32[272,128]{1,0:T(8,128)S(1)}, u32[]{:S(2)}, u32[]{:S(2)}) collective-permute-start(f32[272,128]{1,0:T(8,128)} %pack.1.refs_0_), channel_id=1, source_target_pairs={{0,8},{8,0},{16,24},{24,16},{1,9},{9,1},{17,25},{25,17},{2,10},{10... | collective-permute-start | bytes 417800 | tf_op jit(solution)/shard_map/ppermute | solution.py:166
  11.2 2.7 %copy-start.2 = (f32[272,128]{1,0:T(8,128)}, f32[272,128]{1,0:T(8,128)S(1)}, u32[]{:S(2)}) copy-start(f32[272,128]{1,0:T(8,128)S(1)} %collective-permute-done.2.refs_3_) | copy-start | bytes 417796
  13.7 0.7 %copy-start.3 = (f32[272,128]{1,0:T(8,128)}, f32[272,128]{1,0:T(8,128)S(1)}, u32[]{:S(2)}) copy-start(f32[272,128]{1,0:T(8,128)S(1)} %collective-permute-done.1.refs_2_) | copy-start | bytes 417796
  14.0 0.6 %copy-start.4 = (f32[272,128]{1,0:T(8,128)}, f32[272,128]{1,0:T(8,128)S(1)}, u32[]{:S(2)}) copy-start(f32[272,128]{1,0:T(8,128)S(1)} %collective-permute-done.refs_1_) | copy-start | bytes 417796
  17.4 3.7 %collective-permute-start.3 = (f32[64,768]{1,0:T(8,128)}, f32[64,768]{1,0:T(8,128)S(1)}, u32[]{:S(2)}, u32[]{:S(2)}) collective-permute-start(f32[64,768]{1,0:T(8,128)} %get-tuple-element.13), channel_id=1, source_target_pairs={{0,1},{1,0},{2,3},{3,2},{4,5},{5,4},{6,7},{7,6},{8,9},{9,8},{10,11... | collective-permute-start | bytes 589832 | tf_op jit(solution)/shard_map/ppermute | solution.py:185
  17.4 8.7 %collective-permute-start.4 = (f32[64,768]{1,0:T(8,128)}, f32[64,768]{1,0:T(8,128)S(1)}, u32[]{:S(2)}, u32[]{:S(2)}) collective-permute-start(f32[64,768]{1,0:T(8,128)} %get-tuple-element.14), channel_id=1, source_target_pairs={{0,7},{1,2},{2,1},{3,4},{4,3},{5,6},{6,5},{7,0},{8,15},{9,10},{10,... | collective-permute-start | bytes 589832 | tf_op jit(solution)/shard_map/ppermute | solution.py:186
  21.1 5.0 %copy-start = (f32[64,768]{1,0:T(8,128)}, f32[64,768]{1,0:T(8,128)S(1)}, u32[]{:S(2)}) copy-start(f32[64,768]{1,0:T(8,128)S(1)} %collective-permute-done.3.chip_ref) | copy-start | bytes 589828
  26.1 0.7 %copy-start.1 = (f32[64,768]{1,0:T(8,128)}, f32[64,768]{1,0:T(8,128)S(1)}, u32[]{:S(2)}) copy-start(f32[64,768]{1,0:T(8,128)S(1)} %collective-permute-done.4.far_ref) | copy-start | bytes 589828

commit v2 on v1

--- a/solution.py
+++ b/solution.py
@@ -8,6 +8,7 @@
 from jax.sharding import PartitionSpec as P
 
 SHIFTS = 3
+PARAMS = pltpu.CompilerParams(vmem_limit_bytes=24 * 1024 * 1024)
 
 
 def vmem():
@@ -39,7 +40,7 @@
     left = lane < width
     masks = []
     for i in range(rows):
-        c0, c1 = code_ref[i, 0], code_ref[i, 1]
+        c0, c1 = code_ref[0, i], code_ref[1, i]
         straight = jnp.where(left, c0, c1)
         crossed = jnp.where(left, c1, c0)
         near = jnp.where(left, 0, 1)
@@ -58,9 +59,9 @@
     row_of = lax.broadcasted_iota(jnp.int32, (1, wide), 1) // width
     codes = []
     for n in range(2):
-        c = jnp.full((1, wide), code_ref[0, n], jnp.int32)
+        c = jnp.full((1, wide), code_ref[n, 0], jnp.int32)
         for i in range(1, rows):
-            c = jnp.where(row_of == i, code_ref[i, n], c)
+            c = jnp.where(row_of == i, code_ref[n, i], c)
         codes.append(c)
     blocks = []
     for dest in (1, 2 - 2 * odd, 2 * odd):
@@ -154,12 +155,14 @@
     groups = lax.axis_size("blk")
     bands = lax.axis_size("band")
     f32 = jnp.float32
+    prolong_code = prolong_code.T
     packed_rows = rows * width + 4 * rows
     packed = pl.pallas_call(
         functools.partial(pack_kernel, width),
         out_shape=jax.ShapeDtypeStruct((packed_rows, pair), f32),
         in_specs=[smem(), vmem()],
         out_specs=vmem(),
+        compiler_params=PARAMS,
         name="pack",
     )(prolong_code, prolong_blocks)
     arrived = [packed] + [
@@ -173,6 +176,7 @@
         in_specs=[smem(), smem(), vmem(), vmem()],
         out_specs=[vmem()] * 2,
         cost_estimate=pl.CostEstimate(flops=2 * 3 * groups * height * 128 * deep, bytes_accessed=2000000, transcendentals=0),
+        compiler_params=PARAMS,
         name="left",
     )(source_group, prolong_code, fine_blocks, prolong_blocks)
     own, chip, far = pl.pallas_call(
@@ -180,6 +184,7 @@
         out_shape=[jax.ShapeDtypeStruct((width, SHIFTS * groups * width), f32)] * 3,
         in_specs=[smem()] * 2 + [vmem()] * (2 + groups),
         out_specs=[vmem()] * 3,
+        compiler_params=PARAMS,
         name="right",
     )(source_group, source_row, hi, lo, *arrived)
     chip = lax.ppermute(chip, "band", [(i, i ^ 1) for i in range(bands)])
@@ -189,6 +194,7 @@
         out_shape=jax.ShapeDtypeStruct((width, 5 * groups * width), f32),
         in_specs=[vmem()] * 3,
         out_specs=vmem(),
+        compiler_params=PARAMS,
         name="add",
     )(own, chip, far)
 

time: 28.8 us -> 23.9 us (0.83)
  Pallas kernels: 8.8 us -> 3.89 us
    pallas_call x1, Pallas kernels: 2.8 us -> 1.34 us  [body(): pl.pallas_call(functools.partial(right_kernel, width, groups), out_shape=...]
    pallas_call x1, Pallas kernels: 2.52 us -> 1.21 us  [body(): pl.pallas_call(functools.partial(left_kernel, width, groups), out_shape=[...]
    pallas_call x1, Pallas kernels: 1.88 us -> 0.78 us  [body(): pl.pallas_call(functools.partial(add_kernel, groups * width), out_shape=j...]
    pallas_call x1, Pallas kernels: 1.6 us -> 0.57 us  [body(): pl.pallas_call(functools.partial(pack_kernel, width), out_shape=jax.Shape...]
    unnamed x11 -> x12, local copies, waits for them, and re-layouts: 2.65 us -> 2.55 us
  transfers between devices with their start and end apart: 5 -> 5, of which waited for: 4 -> 4; matrix products, arithmetic and copies ran while one was open for 0% -> 0% of each run, Pallas kernels for 9% -> 5%
where the time goes in v2:
time: 23.9 us; the launch traced here: 23.7 us
  waiting for transfers between devices  8.85 us (37%)
  starting transfers between devices  8.38 us (35%)
  Pallas kernels  3.89 us (16%)
  local copies, waits for them, and re-layouts  2.55 us (11%)
    ppermute x1, waiting for transfers between devices, body(): lax.ppermute(far, 'band', [(i, (i + 1 if i % 2 else i - 1) % bands) for i...  4.76 us
    ppermute x3, starting transfers between devices, body(): lax.ppermute(packed, 'blk', [(i, i ^ j) for i in range(groups)])  4.6 us
    ppermute x3, waiting for transfers between devices, body(): lax.ppermute(packed, 'blk', [(i, i ^ j) for i in range(groups)])  4.09 us
    ppermute x1, starting transfers between devices, body(): lax.ppermute(far, 'band', [(i, (i + 1 if i % 2 else i - 1) % bands) for i...  3.71 us
    unnamed x12, local copies, waits for them, and re-layouts  2.55 us
    pallas_call x1, Pallas kernels, body(): pl.pallas_call(functools.partial(right_kernel, width, groups), out_shape=...  1.34 us
    pallas_call x1, Pallas kernels, body(): pl.pallas_call(functools.partial(left_kernel, width, groups), out_shape=[...  1.21 us
    pallas_call x1, Pallas kernels, body(): pl.pallas_call(functools.partial(add_kernel, groups * width), out_shape=j...  0.78 us
  transfers between devices with their start and end apart: 5, of which 4 were waited for; matrix products, arithmetic and copies ran while one was open for 0% of the time, Pallas kernels for 5%

profile of v2, /device:TPU:0, one launch (start us, length us, event | category | flops | bytes accessed | tf_op | source)
XLA Modules:
  0.0 23.7 jit_solution(9877484769926668719)
XLA Ops:
  0.0 0.0 copy-start.4
  0.0 0.7 %copy-done.4 = s32[4,2]{0,1:T(2,128)S(1)} copy-done((s32[4,2]{0,1:T(2,128)S(1)}, s32[4,2]{0,1:T(2,128)}, u32[]{:S(2)}) %copy-start.4) | copy-done | bytes 56
  0.7 0.0 copy-start
  0.7 0.9 %copy-done = f32[4,64,128]{2,1,0:T(8,128)S(1)} copy-done((f32[4,64,128]{2,1,0:T(8,128)S(1)}, f32[4,64,128]{2,1,0:T(8,128)}, u32[]{:S(2)}) %copy-start) | copy-done | bytes 131096
  1.6 0.0 copy-start.1
  1.6 0.0 copy-start.2
  1.6 0.6 %pack.1.refs_0_ = f32[272,128]{1,0:T(8,128)S(1)} custom-call(s32[2,4]{1,0:T(2,128)S(1)} %bitcast.1, f32[4,64,128]{2,1,0:T(8,128)S(1)} %copy-done), custom_call_target="tpu_custom_call" | custom-call | tf_op jit(solution)/shard_map/pack/pallas_call | solution.py:160
  2.2 4.0 %collective-permute-start.2 = (f32[272,128]{1,0:T(8,128)S(1)}, f32[272,128]{1,0:T(8,128)S(1)}, u32[]{:S(2)}, u32[]{:S(2)}) collective-permute-start(f32[272,128]{1,0:T(8,128)S(1)} %pack.1.refs_0_), channel_id=1, source_target_pairs={{0,24},{8,16},{16,8},{24,0},{1,25},{9,17},{17,9},{25,1},{2,26},{10... | collective-permute-start | bytes 417800 | tf_op jit(solution)/shard_map/ppermute | solution.py:169
  6.1 0.5 %collective-permute-start.1 = (f32[272,128]{1,0:T(8,128)S(1)}, f32[272,128]{1,0:T(8,128)S(1)}, u32[]{:S(2)}, u32[]{:S(2)}) collective-permute-start(f32[272,128]{1,0:T(8,128)S(1)} %pack.1.refs_0_), channel_id=1, source_target_pairs={{0,16},{8,24},{16,0},{24,8},{1,17},{9,25},{17,1},{25,9},{2,18},{10... | collective-permute-start | bytes 417800 | tf_op jit(solution)/shard_map/ppermute | solution.py:169
  6.6 0.1 collective-permute-start
  6.8 0.0 copy-done.1
  6.8 0.0 copy-done.2
  6.8 0.0 copy-start.5
  6.8 0.9 %copy-done.5 = f32[4,64,256]{2,1,0:T(8,128)S(1)} copy-done((f32[4,64,256]{2,1,0:T(8,128)S(1)}, f32[4,64,256]{2,1,0:T(8,128)}, u32[]{:S(2)}) %copy-start.5) | copy-done | bytes 262168
  7.7 1.2 %left.1 = (bf16[4,192,256]{2,1,0:T(8,128)(2,1)S(1)}, bf16[4,192,256]{2,1,0:T(8,128)(2,1)S(1)}) custom-call(s32[4,4]{1,0:T(4,128)S(1)} %copy-done.2, s32[2,4]{1,0:T(2,128)S(1)} %bitcast.2, f32[4,64,256]{2,1,0:T(8,128)S(1)} %copy-done.5, f32[4,64,128]{2,1,0:T(8,128)S(1)} %copy-done.1), custom_call_target="tpu_custom_call" | custom-call | flops 150994944 | bytes 2000000 | tf_op jit(solution)/shard_map/left/pallas_call | solution.py:173
  8.9 0.0 copy-start.3
  8.9 1.3 %collective-permute-done.2.refs_3_ = f32[272,128]{1,0:T(8,128)S(1)} collective-permute-done((f32[272,128]{1,0:T(8,128)S(1)}, f32[272,128]{1,0:T(8,128)S(1)}, u32[]{:S(2)}, u32[]{:S(2)}) %collective-permute-start.2) | collective-permute-done | bytes 139296 | tf_op jit(solution)/shard_map/ppermute | solution.py:169
  10.2 2.6 %collective-permute-done.1.refs_2_ = f32[272,128]{1,0:T(8,128)S(1)} collective-permute-done((f32[272,128]{1,0:T(8,128)S(1)}, f32[272,128]{1,0:T(8,128)S(1)}, u32[]{:S(2)}, u32[]{:S(2)}) %collective-permute-start.1) | collective-permute-done | bytes 139296 | tf_op jit(solution)/shard_map/ppermute | solution.py:169
  12.8 0.3 %collective-permute-done.refs_1_ = f32[272,128]{1,0:T(8,128)S(1)} collective-permute-done((f32[272,128]{1,0:T(8,128)S(1)}, f32[272,128]{1,0:T(8,128)S(1)}, u32[]{:S(2)}, u32[]{:S(2)}) %collective-permute-start) | collective-permute-done | bytes 139296 | tf_op jit(solution)/shard_map/ppermute | solution.py:169
  13.0 0.0 copy-done.3
  13.0 1.3 %right.1 = (f32[64,768]{1,0:T(8,128)S(1)}, f32[64,768]{1,0:T(8,128)S(1)}, f32[64,768]{1,0:T(8,128)S(1)}) custom-call(s32[4,4]{1,0:T(4,128)S(1)} %copy-done.2, s32[4,4]{1,0:T(4,128)S(1)} %copy-done.3, bf16[4,192,256]{2,1,0:T(8,128)(2,1)S(1)} %get-tuple-element.10.hi_ref, bf16[4,192,256]{2,1,0:T(8,128)(2,1)S(1)} %get-tuple-element.11.lo_ref, ...), custom_call_target="tpu_custom_call" | custom-call | tf_op jit(solution)/shard_map/right/pallas_call | solution.py:182
  14.4 0.1 collective-permute-start.3
  14.5 3.7 %collective-permute-start.4 = (f32[64,768]{1,0:T(8,128)S(1)}, f32[64,768]{1,0:T(8,128)S(1)}, u32[]{:S(2)}, u32[]{:S(2)}) collective-permute-start(f32[64,768]{1,0:T(8,128)S(1)} %get-tuple-element.14), channel_id=1, source_target_pairs={{0,7},{1,2},{2,1},{3,4},{4,3},{5,6},{6,5},{7,0},{8,15},{9,10},{10,... | collective-permute-start | bytes 589832 | tf_op jit(solution)/shard_map/ppermute | solution.py:191
  18.2 0.0 collective-permute-done.3.chip_ref
  18.2 4.8 %collective-permute-done.4.far_ref = f32[64,768]{1,0:T(8,128)S(1)} collective-permute-done((f32[64,768]{1,0:T(8,128)S(1)}, f32[64,768]{1,0:T(8,128)S(1)}, u32[]{:S(2)}, u32[]{:S(2)}) %collective-permute-start.4) | collective-permute-done | bytes 196640 | tf_op jit(solution)/shard_map/ppermute | solution.py:191
  22.9 0.8 %add.1 = f32[64,1280]{1,0:T(8,128)} custom-call(f32[64,768]{1,0:T(8,128)S(1)} %get-tuple-element.12.own_ref, f32[64,768]{1,0:T(8,128)S(1)} %collective-permute-done.3.chip_ref, f32[64,768]{1,0:T(8,128)S(1)} %collective-permute-done.4.far_ref), custom_call_target="tpu_custom_call" | custom-call | tf_op jit(solution)/shard_map/add/pallas_call | solution.py:192
Async XLA Ops:
  0.0 0.7 %copy-start.4 = (s32[4,2]{0,1:T(2,128)S(1)}, s32[4,2]{0,1:T(2,128)}, u32[]{:S(2)}) copy-start(s32[4,2]{0,1:T(2,128)} %param.9) | copy-start | bytes 100
  0.7 0.9 %copy-start = (f32[4,64,128]{2,1,0:T(8,128)S(1)}, f32[4,64,128]{2,1,0:T(8,128)}, u32[]{:S(2)}) copy-start(f32[4,64,128]{2,1,0:T(8,128)} %p_ref.3) | copy-start | bytes 393220
  1.6 5.2 %copy-start.1 = (f32[4,64,128]{2,1,0:T(8,128)S(1)}, f32[4,64,128]{2,1,0:T(8,128)}, u32[]{:S(2)}) copy-start(f32[4,64,128]{2,1,0:T(8,128)} %p_ref.3) | copy-start | bytes 393220
  1.6 5.2 %copy-start.2 = (s32[4,4]{1,0:T(4,128)S(1)}, s32[4,4]{1,0:T(4,128)}, u32[]{:S(2)}) copy-start(s32[4,4]{1,0:T(4,128)} %group_ref.3) | copy-start | bytes 196
  2.2 8.0 %collective-permute-start.2 = (f32[272,128]{1,0:T(8,128)S(1)}, f32[272,128]{1,0:T(8,128)S(1)}, u32[]{:S(2)}, u32[]{:S(2)}) collective-permute-start(f32[272,128]{1,0:T(8,128)S(1)} %pack.1.refs_0_), channel_id=1, source_target_pairs={{0,24},{8,16},{16,8},{24,0},{1,25},{9,17},{17,9},{25,1},{2,26},{10... | collective-permute-start | bytes 417800 | tf_op jit(solution)/shard_map/ppermute | solution.py:169
  6.1 6.7 %collective-permute-start.1 = (f32[272,128]{1,0:T(8,128)S(1)}, f32[272,128]{1,0:T(8,128)S(1)}, u32[]{:S(2)}, u32[]{:S(2)}) collective-permute-start(f32[272,128]{1,0:T(8,128)S(1)} %pack.1.refs_0_), channel_id=1, source_target_pairs={{0,16},{8,24},{16,0},{24,8},{1,17},{9,25},{17,1},{25,9},{2,18},{10... | collective-permute-start | bytes 417800 | tf_op jit(solution)/shard_map/ppermute | solution.py:169
  6.6 6.4 %collective-permute-start = (f32[272,128]{1,0:T(8,128)S(1)}, f32[272,128]{1,0:T(8,128)S(1)}, u32[]{:S(2)}, u32[]{:S(2)}) collective-permute-start(f32[272,128]{1,0:T(8,128)S(1)} %pack.1.refs_0_), channel_id=1, source_target_pairs={{0,8},{8,0},{16,24},{24,16},{1,9},{9,1},{17,25},{25,17},{2,10},{10... | collective-permute-start | bytes 417800 | tf_op jit(solution)/shard_map/ppermute | solution.py:169
  6.8 1.0 %copy-start.5 = (f32[4,64,256]{2,1,0:T(8,128)S(1)}, f32[4,64,256]{2,1,0:T(8,128)}, u32[]{:S(2)}) copy-start(f32[4,64,256]{2,1,0:T(8,128)} %a_ref.1) | copy-start | bytes 786436
  8.9 4.1 %copy-start.3 = (s32[4,4]{1,0:T(4,128)S(1)}, s32[4,4]{1,0:T(4,128)}, u32[]{:S(2)}) copy-start(s32[4,4]{1,0:T(4,128)} %row_ref.1) | copy-start | bytes 196
  14.4 3.8 %collective-permute-start.3 = (f32[64,768]{1,0:T(8,128)S(1)}, f32[64,768]{1,0:T(8,128)S(1)}, u32[]{:S(2)}, u32[]{:S(2)}) collective-permute-start(f32[64,768]{1,0:T(8,128)S(1)} %get-tuple-element.13), channel_id=1, source_target_pairs={{0,1},{1,0},{2,3},{3,2},{4,5},{5,4},{6,7},{7,6},{8,9},{9,8},{10,11... | collective-permute-start | bytes 589832 | tf_op jit(solution)/shard_map/ppermute | solution.py:190
  14.5 8.5 %collective-permute-start.4 = (f32[64,768]{1,0:T(8,128)S(1)}, f32[64,768]{1,0:T(8,128)S(1)}, u32[]{:S(2)}, u32[]{:S(2)}) collective-permute-start(f32[64,768]{1,0:T(8,128)S(1)} %get-tuple-element.14), channel_id=1, source_target_pairs={{0,7},{1,2},{2,1},{3,4},{4,3},{5,6},{6,5},{7,0},{8,15},{9,10},{10,... | collective-permute-start | bytes 589832 | tf_op jit(solution)/shard_map/ppermute | solution.py:191

commit v3 on v2

--- a/solution.py
+++ b/solution.py
@@ -8,6 +8,7 @@
 from jax.sharding import PartitionSpec as P
 
 SHIFTS = 3
+CHUNKS = 2
 PARAMS = pltpu.CompilerParams(vmem_limit_bytes=24 * 1024 * 1024)
 
 
@@ -32,10 +33,13 @@
     return dot(a_hi, b_hi) + (dot(a_hi, b_lo) + dot(a_lo, b_hi))
 
 
-def pack_kernel(width, code_ref, p_ref, out_ref):
-    rows = p_ref.shape[0]
-    for i in range(rows):
-        out_ref[i * width : (i + 1) * width, :] = p_ref[i]
+def pack_kernel(width, code_hbm, p_hbm, out_ref, code_ref, sems):
+    rows = code_ref.shape[1]
+    codes = pltpu.make_async_copy(code_hbm, code_ref, sems.at[0])
+    blocks = pltpu.make_async_copy(p_hbm, out_ref.at[0 : rows * width], sems.at[1])
+    codes.start()
+    blocks.start()
+    codes.wait()
     lane = lax.broadcasted_iota(jnp.int32, (1, 2 * width), 1)
     left = lane < width
     masks = []
@@ -47,6 +51,7 @@
         far = jnp.where(left, 2, -1)
         masks += [straight == near, crossed == near, straight == far, crossed == far]
     out_ref[rows * width :, :] = jnp.concatenate([m.astype(jnp.float32) for m in masks], axis=0)
+    blocks.wait()
 
 
 def left_kernel(width, groups, group_ref, code_ref, a_ref, p_ref, hi_ref, lo_ref):
@@ -97,16 +102,17 @@
             lo_ref[j, :, lanes] = l_lo
 
 
-def right_kernel(width, groups, group_ref, row_ref, hi_ref, lo_ref, *refs):
-    sources, (own_ref, chip_ref, far_ref) = refs[:groups], refs[groups:]
+def right_kernel(width, first, earlier_ref, group_ref, row_ref, hi_ref, lo_ref, *refs):
+    sources, (own_ref, chip_ref, far_ref) = refs[:-3], refs[-3:]
     rows, per_row = group_ref.shape
     me = lax.axis_index("blk")
     pair = 2 * width
+    pairs = len(sources) // 2
     right_half = lax.broadcasted_iota(jnp.int32, (width, pair), 1) >= width
-    for q in range(groups // 2):
+    for q in range(pairs):
         found = []
         for j in (2 * q, 2 * q + 1):
-            g = me ^ j
+            g = me ^ (first + j)
             src = sources[j]
             near, far = [], []
             for i in range(rows):
@@ -120,34 +126,43 @@
                 far.append(x * m[2] + y * m[3])
             w = jnp.concatenate([jnp.concatenate(near, axis=0), jnp.concatenate(far, axis=0)], axis=1)
             w_hi, w_lo = split(w)
-            found.append(dot3(hi_ref[j], lo_ref[j], w_hi, w_lo))
+            found.append(dot3(hi_ref[first + j], lo_ref[first + j], w_hi, w_lo))
         swap = me % 2 == 1
-        base = ((me ^ (2 * q)) // 2) * pair
         for t, out_ref in enumerate((own_ref, chip_ref, far_ref)):
             a, b = (f[t * width : (t + 1) * width] for f in found)
-            first = jnp.where(swap, b, a)
-            second = jnp.where(swap, a, b)
+            before = jnp.where(swap, b, a)
+            after = jnp.where(swap, a, b)
             for e in range(SHIFTS):
                 tile = slice((e // 2) * pair, (e // 2 + 1) * pair)
-                u, v = first[:, tile], second[:, tile]
+                u, v = before[:, tile], after[:, tile]
                 if e % 2 == 0:
                     v = pltpu.roll(v, width, 1)
                 else:
                     u = pltpu.roll(u, width, 1)
-                place = pl.multiple_of(e * groups * width + base, pair)
-                out_ref[:, pl.ds(place, pair)] = jnp.where(right_half, v, u)
-
-
-def add_kernel(step, own_ref, chip_ref, far_ref, out_ref):
+                at = (e * pairs + q) * pair
+                out_ref[:, at : at + pair] = jnp.where(right_half, v, u)
+
+
+def add_kernel(groups, *refs):
+    out_ref = refs[-1]
+    me = lax.axis_index("blk")
     odd = lax.axis_index("band") % 2 == 1
-    upper = lambda t: jnp.where(odd, far_ref[:, t], chip_ref[:, t])
-    lower = lambda t: jnp.where(odd, chip_ref[:, t], far_ref[:, t])
-    at = [slice(e * step, (e + 1) * step) for e in range(5)]
-    out_ref[:, at[0]] = lower(at[0])
-    out_ref[:, at[1]] = lower(at[1]) + own_ref[:, at[0]]
-    out_ref[:, at[2]] = lower(at[2]) + own_ref[:, at[1]] + upper(at[0])
-    out_ref[:, at[3]] = own_ref[:, at[2]] + upper(at[1])
-    out_ref[:, at[4]] = upper(at[2])
+    step = out_ref.shape[1] // 5
+    pair = 2 * step // groups
+    pairs = groups // 2 // CHUNKS
+    for c in range(CHUNKS):
+        own_ref, chip_ref, far_ref = refs[3 * c : 3 * c + 3]
+        for q in range(pairs):
+            place = ((me ^ (2 * (c * pairs + q))) // 2) * pair
+            at = [slice((e * pairs + q) * pair, (e * pairs + q + 1) * pair) for e in range(SHIFTS)]
+            own = [own_ref[:, t] for t in at]
+            chip = [chip_ref[:, t] for t in at]
+            far = [far_ref[:, t] for t in at]
+            lower = [jnp.where(odd, u, v) for u, v in zip(chip, far)]
+            upper = [jnp.where(odd, v, u) for u, v in zip(chip, far)]
+            sums = [lower[0], lower[1] + own[0], lower[2] + own[1] + upper[0], own[2] + upper[1], upper[2]]
+            for e in range(5):
+                out_ref[:, pl.ds(pl.multiple_of(e * step + place, pair), pair)] = sums[e]
 
 
 def body(fine_blocks, source_group, source_row, prolong_blocks, prolong_code):
@@ -156,15 +171,15 @@
     bands = lax.axis_size("band")
     f32 = jnp.float32
     prolong_code = prolong_code.T
-    packed_rows = rows * width + 4 * rows
     packed = pl.pallas_call(
         functools.partial(pack_kernel, width),
-        out_shape=jax.ShapeDtypeStruct((packed_rows, pair), f32),
-        in_specs=[smem(), vmem()],
+        out_shape=jax.ShapeDtypeStruct((rows * width + 4 * rows, pair), f32),
+        in_specs=[pl.BlockSpec(memory_space=pltpu.HBM)] * 2,
         out_specs=vmem(),
+        scratch_shapes=[pltpu.SMEM(prolong_code.shape, jnp.int32), pltpu.SemaphoreType.DMA((2,))],
         compiler_params=PARAMS,
         name="pack",
-    )(prolong_code, prolong_blocks)
+    )(prolong_code, prolong_blocks.reshape(rows * width, pair))
     arrived = [packed] + [
         lax.ppermute(packed, "blk", [(i, i ^ j) for i in range(groups)]) for j in range(1, groups)
     ]
@@ -175,28 +190,38 @@
         out_shape=[jax.ShapeDtypeStruct((groups, height, deep), jnp.bfloat16)] * 2,
         in_specs=[smem(), smem(), vmem(), vmem()],
         out_specs=[vmem()] * 2,
-        cost_estimate=pl.CostEstimate(flops=2 * 3 * groups * height * 128 * deep, bytes_accessed=2000000, transcendentals=0),
+        cost_estimate=pl.CostEstimate(
+            flops=6 * groups * height * pair * deep, bytes_accessed=2000000, transcendentals=0
+        ),
         compiler_params=PARAMS,
         name="left",
     )(source_group, prolong_code, fine_blocks, prolong_blocks)
-    own, chip, far = pl.pallas_call(
-        functools.partial(right_kernel, width, groups),
-        out_shape=[jax.ShapeDtypeStruct((width, SHIFTS * groups * width), f32)] * 3,
-        in_specs=[smem()] * 2 + [vmem()] * (2 + groups),
-        out_specs=[vmem()] * 3,
-        compiler_params=PARAMS,
-        name="right",
-    )(source_group, source_row, hi, lo, *arrived)
-    chip = lax.ppermute(chip, "band", [(i, i ^ 1) for i in range(bands)])
-    far = lax.ppermute(far, "band", [(i, (i + 1 if i % 2 else i - 1) % bands) for i in range(bands)])
+    span = groups // CHUNKS
+    parts = []
+    own = packed
+    for c in range(CHUNKS):
+        own, chip, far = pl.pallas_call(
+            functools.partial(right_kernel, width, c * span),
+            out_shape=[jax.ShapeDtypeStruct((width, SHIFTS * span * width), f32)] * 3,
+            in_specs=[pl.BlockSpec(memory_space=pl.ANY)] + [smem()] * 2 + [vmem()] * (2 + span),
+            out_specs=[vmem()] * 3,
+            cost_estimate=pl.CostEstimate(
+                flops=6 * span * height * height * deep, bytes_accessed=2000000, transcendentals=0
+            ),
+            compiler_params=PARAMS,
+            name=f"right_{c}",
+        )(own, source_group, source_row, hi, lo, *arrived[c * span : (c + 1) * span])
+        far = lax.ppermute(far, "band", [(i, (i + 1 if i % 2 else i - 1) % bands) for i in range(bands)])
+        chip = lax.ppermute(chip, "band", [(i, i ^ 1) for i in range(bands)])
+        parts += [own, chip, far]
     return pl.pallas_call(
-        functools.partial(add_kernel, groups * width),
+        functools.partial(add_kernel, groups),
         out_shape=jax.ShapeDtypeStruct((width, 5 * groups * width), f32),
-        in_specs=[vmem()] * 3,
+        in_specs=[vmem()] * len(parts),
         out_specs=vmem(),
         compiler_params=PARAMS,
         name="add",
-    )(own, chip, far)
+    )(*parts)
 
 
 def solution(mesh):

time: 23.9 us -> 23.2 us (0.971)
  waiting for transfers between devices: 8.85 us -> 5.4 us
  starting transfers between devices: 8.38 us -> 11.2 us
  Pallas kernels: 3.89 us -> 4.85 us
  local copies, waits for them, and re-layouts: 2.55 us -> 1.6 us
    ppermute x1 -> x2, starting transfers between devices: 3.71 us -> 6.51 us  [body(): lax.ppermute(far, 'band', [(i, (i + 1 if i % 2 else i - 1) % bands) for i...]
    ppermute x3, waiting for transfers between devices: 4.09 us -> 1.31 us  [body(): lax.ppermute(packed, 'blk', [(i, i ^ j) for i in range(groups)])]
    unnamed x12 -> x10, local copies, waits for them, and re-layouts: 2.55 us -> 1.6 us
    pallas_call x2 -> x3, Pallas kernels: 2.12 us -> 3.06 us  [the longest x2 2.29 us: body(): pl.pallas_call(functools.partial(right_kernel, width, c * span), out_shap...]
    ppermute x1 -> x2, waiting for transfers between devices: 4.76 us -> 4.08 us  [body(): lax.ppermute(far, 'band', [(i, (i + 1 if i % 2 else i - 1) % bands) for i...]
  transfers between devices with their start and end apart: 5 -> 7, of which waited for: 4 -> 2; matrix products, arithmetic and copies ran while one was open for 0% -> 0% of each run, Pallas kernels for 5% -> 15%
where the time goes in v3:
time: 23.2 us; the launch traced here: 23.1 us
  starting transfers between devices  11.2 us (48%)
  waiting for transfers between devices  5.4 us (23%)
  Pallas kernels  4.85 us (21%)
  local copies, waits for them, and re-layouts  1.6 us (7%)
    ppermute x2, starting transfers between devices, body(): lax.ppermute(far, 'band', [(i, (i + 1 if i % 2 else i - 1) % bands) for i...  6.51 us
    ppermute x3, starting transfers between devices, body(): lax.ppermute(packed, 'blk', [(i, i ^ j) for i in range(groups)])  4.54 us
    ppermute x2, waiting for transfers between devices, body(): lax.ppermute(far, 'band', [(i, (i + 1 if i % 2 else i - 1) % bands) for i...  4.08 us
    pallas_call x2, Pallas kernels, body(): pl.pallas_call(functools.partial(right_kernel, width, c * span), out_shap...  2.29 us
    unnamed x10, local copies, waits for them, and re-layouts  1.6 us
    ppermute x3, waiting for transfers between devices, body(): lax.ppermute(packed, 'blk', [(i, i ^ j) for i in range(groups)])  1.31 us
    pallas_call x1, Pallas kernels, body(): pl.pallas_call(functools.partial(left_kernel, width, groups), out_shape=[...  1.21 us
    pallas_call x1, Pallas kernels, body(): pl.pallas_call(functools.partial(add_kernel, groups), out_shape=jax.Shape...  0.77 us
  transfers between devices with their start and end apart: 7, of which 2 were waited for; matrix products, arithmetic and copies ran while one was open for 0% of the time, Pallas kernels for 15%

profile of v3, /device:TPU:0, one launch (start us, length us, event | category | flops | bytes accessed | tf_op | source)
XLA Modules:
  0.0 23.1 jit_solution(9472781742944657230)
XLA Ops:
  0.0 0.0 copy-start.3
  0.0 0.7 %copy-done.3 = s32[4,2]{0,1:T(2,128)S(1)} copy-done((s32[4,2]{0,1:T(2,128)S(1)}, s32[4,2]{0,1:T(2,128)}, u32[]{:S(2)}) %copy-start.3) | copy-done | bytes 56
  0.7 0.0 copy-start
  0.7 0.9 %copy-done = f32[4,64,128]{2,1,0:T(8,128)S(1)} copy-done((f32[4,64,128]{2,1,0:T(8,128)S(1)}, f32[4,64,128]{2,1,0:T(8,128)}, u32[]{:S(2)}) %copy-start) | copy-done | bytes 131096
  1.6 0.0 copy-start.1
  1.6 0.0 copy-start.4
  1.6 0.6 %pack.1.earlier_ref.refs_0_ = f32[272,128]{1,0:T(8,128)S(1)} custom-call(s32[2,4]{1,0:T(2,128)S(1)} %bitcast.3, f32[256,128]{1,0:T(8,128)S(1)} %bitcast.2), custom_call_target="tpu_custom_call" | custom-call | tf_op jit(solution)/shard_map/pack/pallas_call | solution.py:174
  2.2 3.0 %collective-permute-start = (f32[272,128]{1,0:T(8,128)S(1)}, f32[272,128]{1,0:T(8,128)S(1)}, u32[]{:S(2)}, u32[]{:S(2)}) collective-permute-start(f32[272,128]{1,0:T(8,128)S(1)} %pack.1.earlier_ref.refs_0_), channel_id=1, source_target_pairs={{0,8},{8,0},{16,24},{24,16},{1,9},{9,1},{17,25},{25,17},{2,10},{10... | collective-permute-start | bytes 417800 | tf_op jit(solution)/shard_map/ppermute | solution.py:184
  5.2 1.5 %collective-permute-start.3 = (f32[272,128]{1,0:T(8,128)S(1)}, f32[272,128]{1,0:T(8,128)S(1)}, u32[]{:S(2)}, u32[]{:S(2)}) collective-permute-start(f32[272,128]{1,0:T(8,128)S(1)} %pack.1.earlier_ref.refs_0_), channel_id=1, source_target_pairs={{0,16},{8,24},{16,0},{24,8},{1,17},{9,25},{17,1},{25,9},{2,18},{10... | collective-permute-start | bytes 417800 | tf_op jit(solution)/shard_map/ppermute | solution.py:184
  6.7 0.0 collective-permute-start.4
  6.7 0.0 copy-done.1
  6.7 0.0 copy-done.4
  6.7 1.2 %left.1 = (bf16[4,192,256]{2,1,0:T(8,128)(2,1)S(1)}, bf16[4,192,256]{2,1,0:T(8,128)(2,1)S(1)}) custom-call(s32[4,4]{1,0:T(4,128)S(1)} %copy-done.1, s32[2,4]{1,0:T(2,128)S(1)} %bitcast.4, f32[4,64,256]{2,1,0:T(8,128)S(1)} %copy-done.4, f32[4,64,128]{2,1,0:T(8,128)S(1)} %copy-done), custom_call_target="tpu_custom_call" | custom-call | flops 150994944 | bytes 2000000 | tf_op jit(solution)/shard_map/left/pallas_call | solution.py:188
  7.9 0.0 copy-start.2
  8.0 1.3 %collective-permute-done.refs_1_ = f32[272,128]{1,0:T(8,128)S(1)} collective-permute-done((f32[272,128]{1,0:T(8,128)S(1)}, f32[272,128]{1,0:T(8,128)S(1)}, u32[]{:S(2)}, u32[]{:S(2)}) %collective-permute-start) | collective-permute-done | bytes 139296 | tf_op jit(solution)/shard_map/ppermute | solution.py:184
  9.3 0.0 copy-done.2
  9.3 1.1 %right_0.1 = (f32[64,384]{1,0:T(8,128)S(1)}, f32[64,384]{1,0:T(8,128)S(1)}, f32[64,384]{1,0:T(8,128)S(1)}) custom-call(f32[272,128]{1,0:T(8,128)S(1)} %pack.1.earlier_ref.refs_0_, s32[4,4]{1,0:T(4,128)S(1)} %copy-done.1, s32[4,4]{1,0:T(4,128)S(1)} %copy-done.2, bf16[4,192,256]{2,1,0:T(8,128)(2,1)S(1)} %get-tuple-element.13.hi_ref, ...), custom_call_target="tpu_custom_call" | custom-call | flops 113246208 | bytes 2000000 | tf_op jit(solution)/shard_map/right_0/pallas_call | solution.py:203
  10.4 0.1 collective-permute-start.1
  10.5 4.1 %collective-permute-start.2 = (f32[64,384]{1,0:T(8,128)S(1)}, f32[64,384]{1,0:T(8,128)S(1)}, u32[]{:S(2)}, u32[]{:S(2)}) collective-permute-start(f32[64,384]{1,0:T(8,128)S(1)} %get-tuple-element.17), channel_id=1, source_target_pairs={{0,7},{1,2},{2,1},{3,4},{4,3},{5,6},{6,5},{7,0},{8,15},{9,10},{10,... | collective-permute-start | bytes 294920 | tf_op jit(solution)/shard_map/ppermute | solution.py:214
  14.6 0.0 collective-permute-done.3.refs_0_
  14.6 0.0 collective-permute-done.4.refs_1_
  14.6 1.1 %right_1.1 = (f32[64,384]{1,0:T(8,128)S(1)}, f32[64,384]{1,0:T(8,128)S(1)}, f32[64,384]{1,0:T(8,128)S(1)}) custom-call(f32[64,384]{1,0:T(8,128)S(1)} %get-tuple-element.15.earlier_ref.refs_0_, s32[4,4]{1,0:T(4,128)S(1)} %copy-done.1, s32[4,4]{1,0:T(4,128)S(1)} %copy-done.2, bf16[4,192,256]{2,1,0:T(8,128)(2,1)S(1)} %get-tuple-element.13.hi_ref, ...), custom_call_target="tpu_custom_call" | custom-call | flops 113246208 | bytes 2000000 | tf_op jit(solution)/shard_map/right_1/pallas_call | solution.py:203
  15.8 0.1 collective-permute-start.5
  15.8 2.4 %collective-permute-start.6 = (f32[64,384]{1,0:T(8,128)S(1)}, f32[64,384]{1,0:T(8,128)S(1)}, u32[]{:S(2)}, u32[]{:S(2)}) collective-permute-start(f32[64,384]{1,0:T(8,128)S(1)} %get-tuple-element.20), channel_id=1, source_target_pairs={{0,7},{1,2},{2,1},{3,4},{4,3},{5,6},{6,5},{7,0},{8,15},{9,10},{10,... | collective-permute-start | bytes 294920 | tf_op jit(solution)/shard_map/ppermute | solution.py:214
  18.2 0.0 collective-permute-done.1.refs_1_
  18.2 0.0 collective-permute-done.2.refs_2_
  18.2 0.0 collective-permute-done.5.refs_4_
  18.3 4.1 %collective-permute-done.6.refs_5_ = f32[64,384]{1,0:T(8,128)S(1)} collective-permute-done((f32[64,384]{1,0:T(8,128)S(1)}, f32[64,384]{1,0:T(8,128)S(1)}, u32[]{:S(2)}, u32[]{:S(2)}) %collective-permute-start.6) | collective-permute-done | bytes 98336 | tf_op jit(solution)/shard_map/ppermute | solution.py:214
  22.3 0.8 %add.1 = f32[64,1280]{1,0:T(8,128)} custom-call(f32[64,384]{1,0:T(8,128)S(1)} %get-tuple-element.15.earlier_ref.refs_0_, f32[64,384]{1,0:T(8,128)S(1)} %collective-permute-done.1.refs_1_, f32[64,384]{1,0:T(8,128)S(1)} %collective-permute-done.2.refs_2_, f32[64,384]{1,0:T(8,128)S(1)} %get-tuple-element.18.refs_3_, ...), custom_call_target="tpu_custom_call" | custom-call | tf_op jit(solution)/shard_map/add/pallas_call | solution.py:217
Async XLA Ops:
  0.0 0.7 %copy-start.3 = (s32[4,2]{0,1:T(2,128)S(1)}, s32[4,2]{0,1:T(2,128)}, u32[]{:S(2)}) copy-start(s32[4,2]{0,1:T(2,128)} %param.9) | copy-start | bytes 100
  0.7 0.9 %copy-start = (f32[4,64,128]{2,1,0:T(8,128)S(1)}, f32[4,64,128]{2,1,0:T(8,128)}, u32[]{:S(2)}) copy-start(f32[4,64,128]{2,1,0:T(8,128)} %p_ref.1) | copy-start | bytes 393220
  1.6 5.1 %copy-start.1 = (s32[4,4]{1,0:T(4,128)S(1)}, s32[4,4]{1,0:T(4,128)}, u32[]{:S(2)}) copy-start(s32[4,4]{1,0:T(4,128)} %group_ref.5) | copy-start | bytes 196
  1.6 5.1 %copy-start.4 = (f32[4,64,256]{2,1,0:T(8,128)S(1)}, f32[4,64,256]{2,1,0:T(8,128)}, u32[]{:S(2)}) copy-start(f32[4,64,256]{2,1,0:T(8,128)} %a_ref.1) | copy-start | bytes 786436
  2.2 7.1 %collective-permute-start = (f32[272,128]{1,0:T(8,128)S(1)}, f32[272,128]{1,0:T(8,128)S(1)}, u32[]{:S(2)}, u32[]{:S(2)}) collective-permute-start(f32[272,128]{1,0:T(8,128)S(1)} %pack.1.earlier_ref.refs_0_), channel_id=1, source_target_pairs={{0,8},{8,0},{16,24},{24,16},{1,9},{9,1},{17,25},{25,17},{2,10},{10... | collective-permute-start | bytes 417800 | tf_op jit(solution)/shard_map/ppermute | solution.py:184
  5.2 9.4 %collective-permute-start.3 = (f32[272,128]{1,0:T(8,128)S(1)}, f32[272,128]{1,0:T(8,128)S(1)}, u32[]{:S(2)}, u32[]{:S(2)}) collective-permute-start(f32[272,128]{1,0:T(8,128)S(1)} %pack.1.earlier_ref.refs_0_), channel_id=1, source_target_pairs={{0,16},{8,24},{16,0},{24,8},{1,17},{9,25},{17,1},{25,9},{2,18},{10... | collective-permute-start | bytes 417800 | tf_op jit(solution)/shard_map/ppermute | solution.py:184
  6.7 7.9 %collective-permute-start.4 = (f32[272,128]{1,0:T(8,128)S(1)}, f32[272,128]{1,0:T(8,128)S(1)}, u32[]{:S(2)}, u32[]{:S(2)}) collective-permute-start(f32[272,128]{1,0:T(8,128)S(1)} %pack.1.earlier_ref.refs_0_), channel_id=1, source_target_pairs={{0,24},{8,16},{16,8},{24,0},{1,25},{9,17},{17,9},{25,1},{2,26},{10... | collective-permute-start | bytes 417800 | tf_op jit(solution)/shard_map/ppermute | solution.py:184
  7.9 1.3 %copy-start.2 = (s32[4,4]{1,0:T(4,128)S(1)}, s32[4,4]{1,0:T(4,128)}, u32[]{:S(2)}) copy-start(s32[4,4]{1,0:T(4,128)} %row_ref.3) | copy-start | bytes 196
  10.4 7.8 %collective-permute-start.1 = (f32[64,384]{1,0:T(8,128)S(1)}, f32[64,384]{1,0:T(8,128)S(1)}, u32[]{:S(2)}, u32[]{:S(2)}) collective-permute-start(f32[64,384]{1,0:T(8,128)S(1)} %get-tuple-element.16), channel_id=1, source_target_pairs={{0,1},{1,0},{2,3},{3,2},{4,5},{5,4},{6,7},{7,6},{8,9},{9,8},{10,11... | collective-permute-start | bytes 294920 | tf_op jit(solution)/shard_map/ppermute | solution.py:215
  10.5 7.8 %collective-permute-start.2 = (f32[64,384]{1,0:T(8,128)S(1)}, f32[64,384]{1,0:T(8,128)S(1)}, u32[]{:S(2)}, u32[]{:S(2)}) collective-permute-start(f32[64,384]{1,0:T(8,128)S(1)} %get-tuple-element.17), channel_id=1, source_target_pairs={{0,7},{1,2},{2,1},{3,4},{4,3},{5,6},{6,5},{7,0},{8,15},{9,10},{10,... | collective-permute-start | bytes 294920 | tf_op jit(solution)/shard_map/ppermute | solution.py:214
  15.8 2.5 %collective-permute-start.5 = (f32[64,384]{1,0:T(8,128)S(1)}, f32[64,384]{1,0:T(8,128)S(1)}, u32[]{:S(2)}, u32[]{:S(2)}) collective-permute-start(f32[64,384]{1,0:T(8,128)S(1)} %get-tuple-element.19), channel_id=1, source_target_pairs={{0,1},{1,0},{2,3},{3,2},{4,5},{5,4},{6,7},{7,6},{8,9},{9,8},{10,11... | collective-permute-start | bytes 294920 | tf_op jit(solution)/shard_map/ppermute | solution.py:215
  15.8 6.5 %collective-permute-start.6 = (f32[64,384]{1,0:T(8,128)S(1)}, f32[64,384]{1,0:T(8,128)S(1)}, u32[]{:S(2)}, u32[]{:S(2)}) collective-permute-start(f32[64,384]{1,0:T(8,128)S(1)} %get-tuple-element.20), channel_id=1, source_target_pairs={{0,7},{1,2},{2,1},{3,4},{4,3},{5,6},{6,5},{7,0},{8,15},{9,10},{10,... | collective-permute-start | bytes 294920 | tf_op jit(solution)/shard_map/ppermute | solution.py:214

commit v4 on v3

v4 whole, which is shorter than its diff:
```python
import functools

import jax
import jax.numpy as jnp
from jax import lax
from jax.experimental import pallas as pl
from jax.experimental.pallas import tpu as pltpu
from jax.sharding import PartitionSpec as P

SHIFTS = 3
CHUNKS = 2
PARAMS = pltpu.CompilerParams(vmem_limit_bytes=24 * 1024 * 1024)


def vmem():
    return pl.BlockSpec(memory_space=pltpu.VMEM)


def smem():
    return pl.BlockSpec(memory_space=pltpu.SMEM)


def split(x):
    hi = x.astype(jnp.bfloat16)
    return hi, (x - hi.astype(jnp.float32)).astype(jnp.bfloat16)


def dot(a, b):
    return lax.dot_general(a, b, (((1,), (0,)), ((), ())), preferred_element_type=jnp.float32)


def dot3(a_hi, a_lo, b_hi, b_lo):
    return dot(a_hi, b_hi) + (dot(a_hi, b_lo) + dot(a_lo, b_hi))


def pack_kernel(width, code_hbm, p_hbm, out_hbm, code_ref, out_ref, sems):
    rows = code_ref.shape[1]
    n = 4
    size = rows * width // n
    codes = pltpu.make_async_copy(code_hbm, code_ref, sems.at[2 * n])
    codes.start()
    ins, outs = [], []
    for t in range(n):
        at = pl.ds(t * size, size)
        ins.append(pltpu.make_async_copy(p_hbm.at[at], out_ref.at[at], sems.at[t]))
        outs.append(pltpu.make_async_copy(out_ref.at[at], out_hbm.at[at], sems.at[n + t]))
        ins[t].start()
    codes.wait()
    lane = lax.broadcasted_iota(jnp.int32, (1, 2 * width), 1)
    left = lane < width
    masks = []
    for i in range(rows):
        c0, c1 = code_ref[0, i], code_ref[1, i]
        straight = jnp.where(left, c0, c1)
        crossed = jnp.where(left, c1, c0)
        near = jnp.where(left, 0, 1)
        far = jnp.where(left, 2, -1)
        masks += [straight == near, crossed == near, straight == far, crossed == far]
    out_ref[rows * width :, :] = jnp.concatenate([m.astype(jnp.float32) for m in masks], axis=0)
    tail = pl.ds(rows * width, 4 * rows)
    outs.append(pltpu.make_async_copy(out_ref.at[tail], out_hbm.at[tail], sems.at[2 * n + 1]))
    outs[n].start()
    for t in range(n):
        ins[t].wait()
        outs[t].start()
    for out in outs:
        out.wait()


def left_kernel(width, group_ref, row_ref, code_ref, a_ref, p_ref, hi_ref, lo_ref, b_hi_ref, b_lo_ref):
    rows, per_row = group_ref.shape
    groups = hi_ref.shape[0]
    me = lax.axis_index("blk")
    odd = lax.axis_index("band") % 2
    pair = 2 * width
    wide = rows * width
    b_hi_ref[...] = jnp.zeros_like(b_hi_ref)
    b_lo_ref[...] = jnp.zeros_like(b_lo_ref)
    half = lax.broadcasted_iota(jnp.int32, (width, pair), 1) // width
    for i in range(rows):
        for k in range(per_row):
            x = a_ref[i, :, (k // 2) * pair : (k // 2 + 1) * pair]
            s = row_ref[i, k]
            turned = pltpu.roll(x, width, 1)
            x = jnp.where(half == s % 2, jnp.where(s % 2 == k % 2, x, turned), 0.0)
            x_hi, x_lo = split(x)
            j = group_ref[i, k] ^ me
            at = pl.ds(pl.multiple_of((s // 2) * pair, pair), pair)
            b_hi_ref[j, i * width : (i + 1) * width, at] = x_hi
            b_lo_ref[j, i * width : (i + 1) * width, at] = x_lo
    pt = p_ref[...].reshape(wide, pair).T
    row_of = lax.broadcasted_iota(jnp.int32, (1, wide), 1) // width
    codes = []
    for n in range(2):
        c = jnp.full((1, wide), code_ref[n, 0], jnp.int32)
        for i in range(1, rows):
            c = jnp.where(row_of == i, code_ref[n, i], c)
        codes.append(c)
    blocks = []
    for dest in (1, 2 - 2 * odd, 2 * odd):
        blocks.append(
            jnp.where(codes[0] == dest, pt[:width], 0.0) + jnp.where(codes[1] == dest, pt[width:], 0.0)
        )
    rt_hi, rt_lo = split(jnp.concatenate(blocks, axis=0))
    for j in range(groups):
        hi_ref[j], lo_ref[j] = split(dot3(rt_hi, rt_lo, b_hi_ref[j], b_lo_ref[j]))


def spread(src, rows, width):
    near, far = [], []
    for s in range(rows):
        x = src[s * width : (s + 1) * width, :]
        y = pltpu.roll(x, width, 1)
        at = rows * width + 4 * s
        m = [src[at + t : at + t + 1, :] for t in range(4)]
        near.append(x * m[0] + y * m[1])
        far.append(x * m[2] + y * m[3])
    return jnp.concatenate([jnp.concatenate(near, axis=0), jnp.concatenate(far, axis=0)], axis=1)


def right_kernel(width, first, earlier_ref, hi_ref, lo_ref, *refs):
    sources, (own_ref, chip_ref, far_ref) = refs[:-3], refs[-3:]
    rows = hi_ref.shape[2] // width
    me = lax.axis_index("blk")
    pair = 2 * width
    pairs = len(sources) // 2
    right_half = lax.broadcasted_iota(jnp.int32, (width, pair), 1) >= width
    for q in range(pairs):
        found = []
        for j in (2 * q, 2 * q + 1):
            w_hi, w_lo = split(spread(sources[j], rows, width))
            found.append(dot3(hi_ref[first + j], lo_ref[first + j], w_hi, w_lo))
        swap = me % 2 == 1
        for t, out_ref in enumerate((own_ref, chip_ref, far_ref)):
            a, b = (f[t * width : (t + 1) * width] for f in found)
            before = jnp.where(swap, b, a)
            after = jnp.where(swap, a, b)
            for e in range(SHIFTS):
                tile = slice((e // 2) * pair, (e // 2 + 1) * pair)
                u, v = before[:, tile], after[:, tile]
                if e % 2 == 0:
                    v = pltpu.roll(v, width, 1)
                else:
                    u = pltpu.roll(u, width, 1)
                at = (e * pairs + q) * pair
                out_ref[:, at : at + pair] = jnp.where(right_half, v, u)


def add_kernel(groups, *refs):
    out_ref = refs[-1]
    me = lax.axis_index("blk")
    odd = lax.axis_index("band") % 2 == 1
    step = out_ref.shape[1] // 5
    pair = 2 * step // groups
    pairs = groups // 2 // CHUNKS
    for c in range(CHUNKS):
        own_ref, far_ref, chip_ref = refs[3 * c : 3 * c + 3]
        for q in range(pairs):
            place = ((me ^ (2 * (c * pairs + q))) // 2) * pair
            at = [slice((e * pairs + q) * pair, (e * pairs + q + 1) * pair) for e in range(SHIFTS)]
            own = [own_ref[:, t] for t in at]
            chip = [chip_ref[:, t] for t in at]
            far = [far_ref[:, t] for t in at]
            lower = [jnp.where(odd, u, v) for u, v in zip(chip, far)]
            upper = [jnp.where(odd, v, u) for u, v in zip(chip, far)]
            sums = [lower[0], lower[1] + own[0], lower[2] + own[1] + upper[0], own[2] + upper[1], upper[2]]
            for e in range(5):
                out_ref[:, pl.ds(pl.multiple_of(e * step + place, pair), pair)] = sums[e]


def body(fine_blocks, source_group, source_row, prolong_blocks, prolong_code):
    rows, width, pair = prolong_blocks.shape
    groups = lax.axis_size("blk")
    bands = lax.axis_size("band")
    f32 = jnp.float32
    prolong_code = prolong_code.T
    packed = pl.pallas_call(
        functools.partial(pack_kernel, width),
        out_shape=jax.ShapeDtypeStruct((rows * width + 4 * rows, pair), f32),
        in_specs=[pl.BlockSpec(memory_space=pltpu.HBM)] * 2,
        out_specs=pl.BlockSpec(memory_space=pl.ANY),
        scratch_shapes=[
            pltpu.SMEM(prolong_code.shape, jnp.int32),
            pltpu.VMEM((rows * width + 4 * rows, pair), f32),
            pltpu.SemaphoreType.DMA((2 * 4 + 2,)),
        ],
        compiler_params=pltpu.CompilerParams(vmem_limit_bytes=60 * 1024 * 1024),
        name="pack",
    )(prolong_code, prolong_blocks.reshape(rows * width, pair))
    arrived = [packed] + [
        lax.ppermute(packed, "blk", [(i, i ^ j) for i in range(groups)]) for j in range(1, groups)
    ]
    height = SHIFTS * width
    deep = rows * width
    hi, lo = pl.pallas_call(
        functools.partial(left_kernel, width),
        out_shape=[jax.ShapeDtypeStruct((groups, height, deep), jnp.bfloat16)] * 2,
        in_specs=[smem()] * 3 + [vmem()] * 2,
        out_specs=[vmem()] * 2,
        scratch_shapes=[pltpu.VMEM((groups, deep, deep), jnp.bfloat16)] * 2,
        cost_estimate=pl.CostEstimate(
            flops=6 * groups * height * deep * deep, bytes_accessed=2000000, transcendentals=0
        ),
        compiler_params=PARAMS,
        name="left",
    )(source_group, source_row, prolong_code, fine_blocks, prolong_blocks)
    span = groups // CHUNKS
    parts = []
    own = packed
    for c in range(CHUNKS):
        shape = (width, SHIFTS * span * width)
        own, chip, far = pl.pallas_call(
            functools.partial(right_kernel, width, c * span),
            out_shape=[
                jax.ShapeDtypeStruct(shape, f32),
                jax.ShapeDtypeStruct(shape, f32),
                jax.ShapeDtypeStruct(shape, f32),
            ],
            in_specs=[pl.BlockSpec(memory_space=pl.ANY)] + [vmem()] * (2 + span),
            out_specs=[vmem()] * 3,
            cost_estimate=pl.CostEstimate(
                flops=6 * span * height * height * deep, bytes_accessed=2000000, transcendentals=0
            ),
            compiler_params=PARAMS,
            name=f"right_{c}",
        )(own, hi, lo, *arrived[c * span : (c + 1) * span])
        far = lax.ppermute(far, "band", [(i, (i + 1 if i % 2 else i - 1) % bands) for i in range(bands)])
        chip = lax.ppermute(chip, "band", [(i, i ^ 1) for i in range(bands)])
        parts += [own, far, chip]
    return pl.pallas_call(
        functools.partial(add_kernel, groups),
        out_shape=jax.ShapeDtypeStruct((width, 5 * groups * width), f32),
        in_specs=[vmem()] * len(parts),
        out_specs=vmem(),
        compiler_params=PARAMS,
        name="add",
    )(*parts)


def solution(mesh):
    return jax.shard_map(
        body,
        mesh=mesh,
        in_specs=(
            P(("blk", "band"), None, None),
            P(("blk", "band"), None),
            P(("blk", "band"), None),
            P(("blk", "band"), None, None),
            P(("blk", "band"), None),
        ),
        out_specs=P(("blk", "band"), None),
        check_vma=False,
    )
```

time: 23.2 us -> 21.1 us (0.909)
  starting transfers between devices: 11.2 us -> 8.72 us
  waiting for transfers between devices: 5.4 us -> 6.47 us
  local copies, waits for them, and re-layouts: 1.6 us -> 0.97 us
    ppermute x2, starting transfers between devices: 6.51 us -> 4.16 us  [body(): lax.ppermute(far, 'band', [(i, (i + 1 if i % 2 else i - 1) % bands) for i...]
    pallas_call x2, Pallas kernels: 2.29 us -> 1.09 us  [body(): pl.pallas_call(functools.partial(right_kernel, width, c * span), out_shap...]
    pallas_call x1, Pallas kernels: 0.58 us -> 1.57 us  [body(): pl.pallas_call(functools.partial(pack_kernel, width), out_shape=jax.Shape...]
    unnamed x10 -> x12, local copies, waits for them, and re-layouts: 1.6 us -> 0.97 us
    ppermute x2, waiting for transfers between devices: 4.08 us -> 4.67 us  [body(): lax.ppermute(far, 'band', [(i, (i + 1 if i % 2 else i - 1) % bands) for i...]
    ppermute x3, waiting for transfers between devices: 1.31 us -> 1.79 us  [body(): lax.ppermute(packed, 'blk', [(i, i ^ j) for i in range(groups)])]
  transfers between devices with their start and end apart: 7 -> 7, of which waited for: 2 -> 4; matrix products, arithmetic and copies ran while one was open for 0% -> 0% of each run, Pallas kernels for 15% -> 11%
where the time goes in v4:
time: 21.1 us; the launch traced here: 20.9 us
  starting transfers between devices  8.72 us (41%)
  waiting for transfers between devices  6.47 us (31%)
  Pallas kernels  4.73 us (22%)
  local copies, waits for them, and re-layouts  0.97 us (5%)
    ppermute x2, waiting for transfers between devices, body(): lax.ppermute(far, 'band', [(i, (i + 1 if i % 2 else i - 1) % bands) for i...  4.67 us
    ppermute x3, starting transfers between devices, body(): lax.ppermute(packed, 'blk', [(i, i ^ j) for i in range(groups)])  4.56 us
    ppermute x2, starting transfers between devices, body(): lax.ppermute(far, 'band', [(i, (i + 1 if i % 2 else i - 1) % bands) for i...  4.16 us
    ppermute x3, waiting for transfers between devices, body(): lax.ppermute(packed, 'blk', [(i, i ^ j) for i in range(groups)])  1.79 us
    pallas_call x1, Pallas kernels, body(): pl.pallas_call(functools.partial(pack_kernel, width), out_shape=jax.Shape...  1.57 us
    pallas_call x1, Pallas kernels, body(): pl.pallas_call(functools.partial(left_kernel, width), out_shape=[jax.Shap...  1.3 us
    pallas_call x2, Pallas kernels, body(): pl.pallas_call(functools.partial(right_kernel, width, c * span), out_shap...  1.09 us
    unnamed x12, local copies, waits for them, and re-layouts  0.97 us
  transfers between devices with their start and end apart: 7, of which 4 were waited for; matrix products, arithmetic and copies ran while one was open for 0% of the time, Pallas kernels for 11%

profile of v4, /device:TPU:0, one launch (start us, length us, event | category | flops | bytes accessed | tf_op | source)
XLA Modules:
  0.0 20.9 jit_solution(12941821259150222642)
XLA Ops:
  0.0 0.0 copy-start.1
  0.0 0.0 copy-start.2
  0.0 0.0 copy-start.4
  0.0 0.0 copy-start.5
  0.0 1.6 %pack.1.earlier_ref.refs_0_ = f32[272,128]{1,0:T(8,128)} custom-call(s32[2,4]{1,0:T(2,128)} %bitcast.3, f32[256,128]{1,0:T(8,128)} %bitcast.2), custom_call_target="tpu_custom_call" | custom-call | tf_op jit(solution)/shard_map/pack/pallas_call | solution.py:177
  1.6 0.0 copy-start
  1.6 3.0 %collective-permute-start = (f32[272,128]{1,0:T(8,128)}, f32[272,128]{1,0:T(8,128)S(1)}, u32[]{:S(2)}, u32[]{:S(2)}) collective-permute-start(f32[272,128]{1,0:T(8,128)} %pack.1.earlier_ref.refs_0_), channel_id=1, source_target_pairs={{0,8},{8,0},{16,24},{24,16},{1,9},{9,1},{17,25},{25,17},{2,10},{10... | collective-permute-start | bytes 417800 | tf_op jit(solution)/shard_map/ppermute | solution.py:191
  4.6 1.5 %collective-permute-start.3 = (f32[272,128]{1,0:T(8,128)}, f32[272,128]{1,0:T(8,128)S(1)}, u32[]{:S(2)}, u32[]{:S(2)}) collective-permute-start(f32[272,128]{1,0:T(8,128)} %pack.1.earlier_ref.refs_0_), channel_id=1, source_target_pairs={{0,16},{8,24},{16,0},{24,8},{1,17},{9,25},{17,1},{25,9},{2,18},{10... | collective-permute-start | bytes 417800 | tf_op jit(solution)/shard_map/ppermute | solution.py:191
  6.1 0.0 collective-permute-start.4
  6.2 0.0 copy-done.1
  6.2 0.0 copy-done.2
  6.2 0.0 copy-done.4
  6.2 0.0 copy-done.5
  6.2 0.0 copy-start.3
  6.2 0.9 %copy-done.3 = f32[4,64,256]{2,1,0:T(8,128)S(1)} copy-done((f32[4,64,256]{2,1,0:T(8,128)S(1)}, f32[4,64,256]{2,1,0:T(8,128)}, u32[]{:S(2)}) %copy-start.3) | copy-done | bytes 262168
  7.1 1.3 %left.1 = (bf16[4,192,256]{2,1,0:T(8,128)(2,1)S(1)}, bf16[4,192,256]{2,1,0:T(8,128)(2,1)S(1)}) custom-call(s32[4,4]{1,0:T(4,128)S(1)} %copy-done.4, s32[4,4]{1,0:T(4,128)S(1)} %copy-done.5, s32[2,4]{1,0:T(2,128)S(1)} %bitcast.4, f32[4,64,256]{2,1,0:T(8,128)S(1)} %copy-done.3, f32[4,64,128]{2,1,0:T(8,128)S(1)} %copy-done.1), custom_call_target="tpu_custom_call" | custom-call | flops 301989888 | bytes 2000000 | tf_op jit(solution)/shard_map/left/pallas_call | solution.py:195
  8.4 0.6 %collective-permute-done.refs_1_ = f32[272,128]{1,0:T(8,128)S(1)} collective-permute-done((f32[272,128]{1,0:T(8,128)}, f32[272,128]{1,0:T(8,128)S(1)}, u32[]{:S(2)}, u32[]{:S(2)}) %collective-permute-start) | collective-permute-done | bytes 139296 | tf_op jit(solution)/shard_map/ppermute | solution.py:191
  9.0 0.0 copy-done
  9.0 0.5 %right_0.1 = (f32[64,384]{1,0:T(8,128)S(1)}, f32[64,384]{1,0:T(8,128)S(1)}, f32[64,384]{1,0:T(8,128)S(1)}) custom-call(f32[272,128]{1,0:T(8,128)S(1)} %copy-done, bf16[4,192,256]{2,1,0:T(8,128)(2,1)S(1)} %get-tuple-element.13.hi_ref, bf16[4,192,256]{2,1,0:T(8,128)(2,1)S(1)} %get-tuple-element.14.lo_ref, f32[272,128]{1,0:T(8,128)S(1)} %copy-done, ...), custom_call_target="tpu_custom_call" | custom-call | flops 113246208 | bytes 2000000 | tf_op jit(solution)/shard_map/right_0/pallas_call | solution.py:212
  9.6 2.2 %collective-permute-start.1 = (f32[64,384]{1,0:T(8,128)S(1)}, f32[64,384]{1,0:T(8,128)S(1)}, u32[]{:S(2)}, u32[]{:S(2)}) collective-permute-start(f32[64,384]{1,0:T(8,128)S(1)} %get-tuple-element.16), channel_id=1, source_target_pairs={{0,7},{1,2},{2,1},{3,4},{4,3},{5,6},{6,5},{7,0},{8,15},{9,10},{10,... | collective-permute-start | bytes 294920 | tf_op jit(solution)/shard_map/ppermute | solution.py:227
  11.7 0.0 collective-permute-start.2
  11.7 1.2 %collective-permute-done.3.refs_0_ = f32[272,128]{1,0:T(8,128)S(1)} collective-permute-done((f32[272,128]{1,0:T(8,128)}, f32[272,128]{1,0:T(8,128)S(1)}, u32[]{:S(2)}, u32[]{:S(2)}) %collective-permute-start.3) | collective-permute-done | bytes 139296 | tf_op jit(solution)/shard_map/ppermute | solution.py:191
  12.9 0.0 collective-permute-done.4.refs_1_
  12.9 0.5 %right_1.1 = (f32[64,384]{1,0:T(8,128)S(1)}, f32[64,384]{1,0:T(8,128)S(1)}, f32[64,384]{1,0:T(8,128)S(1)}) custom-call(f32[64,384]{1,0:T(8,128)S(1)} %get-tuple-element.15.earlier_ref.refs_0_, bf16[4,192,256]{2,1,0:T(8,128)(2,1)S(1)} %get-tuple-element.13.hi_ref, bf16[4,192,256]{2,1,0:T(8,128)(2,1)S(1)} %get-tuple-element.14.lo_ref, ...), custom_call_target="tpu_custom_call" | custom-call | flops 113246208 | bytes 2000000 | tf_op jit(solution)/shard_map/right_1/pallas_call | solution.py:212
  13.5 2.0 %collective-permute-start.5 = (f32[64,384]{1,0:T(8,128)S(1)}, f32[64,384]{1,0:T(8,128)S(1)}, u32[]{:S(2)}, u32[]{:S(2)}) collective-permute-start(f32[64,384]{1,0:T(8,128)S(1)} %get-tuple-element.19), channel_id=1, source_target_pairs={{0,7},{1,2},{2,1},{3,4},{4,3},{5,6},{6,5},{7,0},{8,15},{9,10},{10,... | collective-permute-start | bytes 294920 | tf_op jit(solution)/shard_map/ppermute | solution.py:227
  15.5 0.0 collective-permute-start.6
  15.5 0.4 %collective-permute-done.1.refs_1_ = f32[64,384]{1,0:T(8,128)S(1)} collective-permute-done((f32[64,384]{1,0:T(8,128)S(1)}, f32[64,384]{1,0:T(8,128)S(1)}, u32[]{:S(2)}, u32[]{:S(2)}) %collective-permute-start.1) | collective-permute-done | bytes 98336 | tf_op jit(solution)/shard_map/ppermute | solution.py:227
  15.9 0.0 collective-permute-done.2.refs_2_
  15.9 4.2 %collective-permute-done.5.refs_4_ = f32[64,384]{1,0:T(8,128)S(1)} collective-permute-done((f32[64,384]{1,0:T(8,128)S(1)}, f32[64,384]{1,0:T(8,128)S(1)}, u32[]{:S(2)}, u32[]{:S(2)}) %collective-permute-start.5) | collective-permute-done | bytes 98336 | tf_op jit(solution)/shard_map/ppermute | solution.py:227
  20.2 0.0 collective-permute-done.6.refs_5_
  20.2 0.8 %add.1 = f32[64,1280]{1,0:T(8,128)} custom-call(f32[64,384]{1,0:T(8,128)S(1)} %get-tuple-element.15.earlier_ref.refs_0_, f32[64,384]{1,0:T(8,128)S(1)} %collective-permute-done.1.refs_1_, f32[64,384]{1,0:T(8,128)S(1)} %collective-permute-done.2.refs_2_, f32[64,384]{1,0:T(8,128)S(1)} %get-tuple-element.18.refs_3_, ...), custom_call_target="tpu_custom_call" | custom-call | tf_op jit(solution)/shard_map/add/pallas_call | solution.py:230
Async XLA Ops:
  0.0 6.2 %copy-start.1 = (f32[4,64,128]{2,1,0:T(8,128)S(1)}, f32[4,64,128]{2,1,0:T(8,128)}, u32[]{:S(2)}) copy-start(f32[4,64,128]{2,1,0:T(8,128)} %p_ref.1) | copy-start | bytes 393220
  0.0 6.2 %copy-start.2 = (s32[4,2]{0,1:T(2,128)S(1)}, s32[4,2]{0,1:T(2,128)}, u32[]{:S(2)}) copy-start(s32[4,2]{0,1:T(2,128)} %param.9) | copy-start | bytes 100
  0.0 6.2 %copy-start.4 = (s32[4,4]{1,0:T(4,128)S(1)}, s32[4,4]{1,0:T(4,128)}, u32[]{:S(2)}) copy-start(s32[4,4]{1,0:T(4,128)} %group_ref.1) | copy-start | bytes 196
  0.0 6.2 %copy-start.5 = (s32[4,4]{1,0:T(4,128)S(1)}, s32[4,4]{1,0:T(4,128)}, u32[]{:S(2)}) copy-start(s32[4,4]{1,0:T(4,128)} %row_ref.1) | copy-start | bytes 196
  1.6 7.4 %copy-start = (f32[272,128]{1,0:T(8,128)S(1)}, f32[272,128]{1,0:T(8,128)}, u32[]{:S(2)}) copy-start(f32[272,128]{1,0:T(8,128)} %pack.1.earlier_ref.refs_0_) | copy-start | bytes 417796
  1.6 7.4 %collective-permute-start = (f32[272,128]{1,0:T(8,128)}, f32[272,128]{1,0:T(8,128)S(1)}, u32[]{:S(2)}, u32[]{:S(2)}) collective-permute-start(f32[272,128]{1,0:T(8,128)} %pack.1.earlier_ref.refs_0_), channel_id=1, source_target_pairs={{0,8},{8,0},{16,24},{24,16},{1,9},{9,1},{17,25},{25,17},{2,10},{10... | collective-permute-start | bytes 417800 | tf_op jit(solution)/shard_map/ppermute | solution.py:191
  4.6 8.3 %collective-permute-start.3 = (f32[272,128]{1,0:T(8,128)}, f32[272,128]{1,0:T(8,128)S(1)}, u32[]{:S(2)}, u32[]{:S(2)}) collective-permute-start(f32[272,128]{1,0:T(8,128)} %pack.1.earlier_ref.refs_0_), channel_id=1, source_target_pairs={{0,16},{8,24},{16,0},{24,8},{1,17},{9,25},{17,1},{25,9},{2,18},{10... | collective-permute-start | bytes 417800 | tf_op jit(solution)/shard_map/ppermute | solution.py:191
  6.1 6.8 %collective-permute-start.4 = (f32[272,128]{1,0:T(8,128)}, f32[272,128]{1,0:T(8,128)S(1)}, u32[]{:S(2)}, u32[]{:S(2)}) collective-permute-start(f32[272,128]{1,0:T(8,128)} %pack.1.earlier_ref.refs_0_), channel_id=1, source_target_pairs={{0,24},{8,16},{16,8},{24,0},{1,25},{9,17},{17,9},{25,1},{2,26},{10... | collective-permute-start | bytes 417800 | tf_op jit(solution)/shard_map/ppermute | solution.py:191
  6.2 1.0 %copy-start.3 = (f32[4,64,256]{2,1,0:T(8,128)S(1)}, f32[4,64,256]{2,1,0:T(8,128)}, u32[]{:S(2)}) copy-start(f32[4,64,256]{2,1,0:T(8,128)} %a_ref.1) | copy-start | bytes 786436
  9.6 6.4 %collective-permute-start.1 = (f32[64,384]{1,0:T(8,128)S(1)}, f32[64,384]{1,0:T(8,128)S(1)}, u32[]{:S(2)}, u32[]{:S(2)}) collective-permute-start(f32[64,384]{1,0:T(8,128)S(1)} %get-tuple-element.16), channel_id=1, source_target_pairs={{0,7},{1,2},{2,1},{3,4},{4,3},{5,6},{6,5},{7,0},{8,15},{9,10},{10,... | collective-permute-start | bytes 294920 | tf_op jit(solution)/shard_map/ppermute | solution.py:227
  11.7 4.2 %collective-permute-start.2 = (f32[64,384]{1,0:T(8,128)S(1)}, f32[64,384]{1,0:T(8,128)S(1)}, u32[]{:S(2)}, u32[]{:S(2)}) collective-permute-start(f32[64,384]{1,0:T(8,128)S(1)} %get-tuple-element.17), channel_id=1, source_target_pairs={{0,1},{1,0},{2,3},{3,2},{4,5},{5,4},{6,7},{7,6},{8,9},{9,8},{10,11... | collective-permute-start | bytes 294920 | tf_op jit(solution)/shard_map/ppermute | solution.py:228
  13.5 6.7 %collective-permute-start.5 = (f32[64,384]{1,0:T(8,128)S(1)}, f32[64,384]{1,0:T(8,128)S(1)}, u32[]{:S(2)}, u32[]{:S(2)}) collective-permute-start(f32[64,384]{1,0:T(8,128)S(1)} %get-tuple-element.19), channel_id=1, source_target_pairs={{0,7},{1,2},{2,1},{3,4},{4,3},{5,6},{6,5},{7,0},{8,15},{9,10},{10,... | collective-permute-start | bytes 294920 | tf_op jit(solution)/shard_map/ppermute | solution.py:227
  15.5 4.7 %collective-permute-start.6 = (f32[64,384]{1,0:T(8,128)S(1)}, f32[64,384]{1,0:T(8,128)S(1)}, u32[]{:S(2)}, u32[]{:S(2)}) collective-permute-start(f32[64,384]{1,0:T(8,128)S(1)} %get-tuple-element.20), channel_id=1, source_target_pairs={{0,1},{1,0},{2,3},{3,2},{4,5},{5,4},{6,7},{7,6},{8,9},{9,8},{10,11... | collective-permute-start | bytes 294920 | tf_op jit(solution)/shard_map/ppermute | solution.py:228

commit v5 on v4

--- a/solution.py
+++ b/solution.py
@@ -33,38 +33,19 @@
     return dot(a_hi, b_hi) + (dot(a_hi, b_lo) + dot(a_lo, b_hi))
 
 
-def pack_kernel(width, code_hbm, p_hbm, out_hbm, code_ref, out_ref, sems):
-    rows = code_ref.shape[1]
-    n = 4
-    size = rows * width // n
-    codes = pltpu.make_async_copy(code_hbm, code_ref, sems.at[2 * n])
-    codes.start()
-    ins, outs = [], []
-    for t in range(n):
-        at = pl.ds(t * size, size)
-        ins.append(pltpu.make_async_copy(p_hbm.at[at], out_ref.at[at], sems.at[t]))
-        outs.append(pltpu.make_async_copy(out_ref.at[at], out_hbm.at[at], sems.at[n + t]))
-        ins[t].start()
-    codes.wait()
-    lane = lax.broadcasted_iota(jnp.int32, (1, 2 * width), 1)
-    left = lane < width
-    masks = []
-    for i in range(rows):
-        c0, c1 = code_ref[0, i], code_ref[1, i]
-        straight = jnp.where(left, c0, c1)
-        crossed = jnp.where(left, c1, c0)
-        near = jnp.where(left, 0, 1)
-        far = jnp.where(left, 2, -1)
-        masks += [straight == near, crossed == near, straight == far, crossed == far]
-    out_ref[rows * width :, :] = jnp.concatenate([m.astype(jnp.float32) for m in masks], axis=0)
-    tail = pl.ds(rows * width, 4 * rows)
-    outs.append(pltpu.make_async_copy(out_ref.at[tail], out_hbm.at[tail], sems.at[2 * n + 1]))
-    outs[n].start()
-    for t in range(n):
-        ins[t].wait()
-        outs[t].start()
-    for out in outs:
-        out.wait()
+def lanes_kernel(out_ref):
+    pair = out_ref.shape[1]
+    out_ref[...] = lax.broadcasted_iota(jnp.int32, out_ref.shape, 1) // (pair // 2)
+
+
+def pack_kernel(width, lanes_ref, code_ref, p_ref, out_ref):
+    deep = p_ref.shape[0]
+    rows = deep // width
+    out_ref[:deep, :] = p_ref[...]
+    left = lanes_ref[...] == 0
+    straight = [jnp.where(left, code_ref[0:1, i : i + 1], code_ref[1:2, i : i + 1]) for i in range(rows)]
+    crossed = [jnp.where(left, code_ref[1:2, i : i + 1], code_ref[0:1, i : i + 1]) for i in range(rows)]
+    out_ref[deep:, :] = jnp.concatenate(straight + crossed, axis=0).astype(jnp.float32)
 
 
 def left_kernel(width, group_ref, row_ref, code_ref, a_ref, p_ref, hi_ref, lo_ref, b_hi_ref, b_lo_ref):
@@ -107,14 +88,18 @@
 
 
 def spread(src, rows, width):
+    lane = lax.broadcasted_iota(jnp.int32, (1, 2 * width), 1)
+    low = jnp.where(lane < width, 0.0, 1.0)
+    high = jnp.where(lane < width, 2.0, -1.0)
+    deep = rows * width
     near, far = [], []
     for s in range(rows):
         x = src[s * width : (s + 1) * width, :]
         y = pltpu.roll(x, width, 1)
-        at = rows * width + 4 * s
-        m = [src[at + t : at + t + 1, :] for t in range(4)]
-        near.append(x * m[0] + y * m[1])
-        far.append(x * m[2] + y * m[3])
+        straight = src[deep + s : deep + s + 1, :]
+        crossed = src[deep + rows + s : deep + rows + s + 1, :]
+        near.append(jnp.where(straight == low, x, 0.0) + jnp.where(crossed == low, y, 0.0))
+        far.append(jnp.where(straight == high, x, 0.0) + jnp.where(crossed == high, y, 0.0))
     return jnp.concatenate([jnp.concatenate(near, axis=0), jnp.concatenate(far, axis=0)], axis=1)
 
 
@@ -174,19 +159,22 @@
     bands = lax.axis_size("band")
     f32 = jnp.float32
     prolong_code = prolong_code.T
+    lanes = pl.pallas_call(
+        lanes_kernel,
+        out_shape=jax.ShapeDtypeStruct((1, pair), jnp.int32),
+        out_specs=vmem(),
+        cost_estimate=pl.CostEstimate(flops=4000000000, bytes_accessed=10000000, transcendentals=0),
+        compiler_params=PARAMS,
+        name="lanes",
+    )()
     packed = pl.pallas_call(
         functools.partial(pack_kernel, width),
-        out_shape=jax.ShapeDtypeStruct((rows * width + 4 * rows, pair), f32),
-        in_specs=[pl.BlockSpec(memory_space=pltpu.HBM)] * 2,
-        out_specs=pl.BlockSpec(memory_space=pl.ANY),
-        scratch_shapes=[
-            pltpu.SMEM(prolong_code.shape, jnp.int32),
-            pltpu.VMEM((rows * width + 4 * rows, pair), f32),
-            pltpu.SemaphoreType.DMA((2 * 4 + 2,)),
-        ],
-        compiler_params=pltpu.CompilerParams(vmem_limit_bytes=60 * 1024 * 1024),
+        out_shape=jax.ShapeDtypeStruct((rows * width + 2 * rows, pair), f32),
+        in_specs=[vmem()] * 3,
+        out_specs=vmem(),
+        compiler_params=PARAMS,
         name="pack",
-    )(prolong_code, prolong_blocks.reshape(rows * width, pair))
+    )(lanes, prolong_code, prolong_blocks.reshape(rows * width, pair))
     arrived = [packed] + [
         lax.ppermute(packed, "blk", [(i, i ^ j) for i in range(groups)]) for j in range(1, groups)
     ]

time: 21.1 us -> 20.1 us (0.953)
  Pallas kernels: 4.73 us -> 3.25 us
  waiting for transfers between devices: 6.47 us -> 7.22 us
    pallas_call x1, Pallas kernels: 1.57 us -> 0.08 us  [body(): pl.pallas_call(functools.partial(pack_kernel, width), out_shape=jax.Shape...]
    ppermute x3, waiting for transfers between devices: 1.79 us -> 2.45 us  [body(): lax.ppermute(packed, 'blk', [(i, i ^ j) for i in range(groups)])]
    unnamed x12 -> x10, local copies, waits for them, and re-layouts: 0.97 us -> 0.9 us
  transfers between devices with their start and end apart: 7 -> 7, of which waited for: 4 -> 4; matrix products, arithmetic and copies ran while one was open for 0% -> 0% of each run, Pallas kernels for 11% -> 12%
where the time goes in v5:
time: 20.1 us; the launch traced here: 20 us
  starting transfers between devices  8.54 us (42%)
  waiting for transfers between devices  7.22 us (36%)
  Pallas kernels  3.25 us (16%)
  local copies, waits for them, and re-layouts  0.9 us (4%)
    ppermute x2, waiting for transfers between devices, body(): lax.ppermute(far, 'band', [(i, (i + 1 if i % 2 else i - 1) % bands) for i...  4.77 us
    ppermute x3, starting transfers between devices, body(): lax.ppermute(packed, 'blk', [(i, i ^ j) for i in range(groups)])  4.54 us
    ppermute x2, starting transfers between devices, body(): lax.ppermute(far, 'band', [(i, (i + 1 if i % 2 else i - 1) % bands) for i...  3.99 us
    ppermute x3, waiting for transfers between devices, body(): lax.ppermute(packed, 'blk', [(i, i ^ j) for i in range(groups)])  2.45 us
    pallas_call x1, Pallas kernels, body(): pl.pallas_call(functools.partial(left_kernel, width), out_shape=[jax.Shap...  1.31 us
    pallas_call x2, Pallas kernels, body(): pl.pallas_call(functools.partial(right_kernel, width, c * span), out_shap...  1.08 us
    unnamed x10, local copies, waits for them, and re-layouts  0.9 us
    pallas_call x1, Pallas kernels, body(): pl.pallas_call(functools.partial(add_kernel, groups), out_shape=jax.Shape...  0.77 us
  transfers between devices with their start and end apart: 7, of which 4 were waited for; matrix products, arithmetic and copies ran while one was open for 0% of the time, Pallas kernels for 12%

profile of v5, /device:TPU:0, one launch (start us, length us, event | category | flops | bytes accessed | tf_op | source)
XLA Modules:
  0.0 20.0 jit_solution(14579273865839611705)
XLA Ops:
  0.0 0.0 copy-start
  0.0 0.0 copy-start.1
  0.0 0.0 copy-start.2
  0.0 0.9 %copy-done = f32[4,64,128]{2,1,0:T(8,128)S(1)} copy-done((f32[4,64,128]{2,1,0:T(8,128)S(1)}, f32[4,64,128]{2,1,0:T(8,128)}, u32[]{:S(2)}) %copy-start) | copy-done | bytes 131096
  0.9 0.0 copy-done.1
  0.9 0.0 copy-start.3
  0.9 0.0 copy-start.4
  0.9 0.1 pack.1.earlier_ref.refs_0_
  1.0 3.0 %collective-permute-start = (f32[264,128]{1,0:T(8,128)S(1)}, f32[264,128]{1,0:T(8,128)S(1)}, u32[]{:S(2)}, u32[]{:S(2)}) collective-permute-start(f32[264,128]{1,0:T(8,128)S(1)} %pack.1.earlier_ref.refs_0_), channel_id=1, source_target_pairs={{0,8},{8,0},{16,24},{24,16},{1,9},{9,1},{17,25},{25,17},{2,10},{10... | collective-permute-start | bytes 405512 | tf_op jit(solution)/shard_map/ppermute | solution.py:179
  4.0 1.5 %collective-permute-start.3 = (f32[264,128]{1,0:T(8,128)S(1)}, f32[264,128]{1,0:T(8,128)S(1)}, u32[]{:S(2)}, u32[]{:S(2)}) collective-permute-start(f32[264,128]{1,0:T(8,128)S(1)} %pack.1.earlier_ref.refs_0_), channel_id=1, source_target_pairs={{0,16},{8,24},{16,0},{24,8},{1,17},{9,25},{17,1},{25,9},{2,18},{10... | collective-permute-start | bytes 405512 | tf_op jit(solution)/shard_map/ppermute | solution.py:179
  5.5 0.0 collective-permute-start.4
  5.5 0.0 copy-done.2
  5.5 0.0 copy-done.3
  5.5 0.0 copy-done.4
  5.5 1.3 %left.1 = (bf16[4,192,256]{2,1,0:T(8,128)(2,1)S(1)}, bf16[4,192,256]{2,1,0:T(8,128)(2,1)S(1)}) custom-call(s32[4,4]{1,0:T(4,128)S(1)} %copy-done.3, s32[4,4]{1,0:T(4,128)S(1)} %copy-done.4, s32[2,4]{1,0:T(2,128)S(1)} %bitcast.4, f32[4,64,256]{2,1,0:T(8,128)S(1)} %copy-done.2, f32[4,64,128]{2,1,0:T(8,128)S(1)} %copy-done), custom_call_target="tpu_custom_call" | custom-call | flops 301989888 | bytes 2000000 | tf_op jit(solution)/shard_map/left/pallas_call | solution.py:183
  6.9 1.1 %collective-permute-done.refs_1_ = f32[264,128]{1,0:T(8,128)S(1)} collective-permute-done((f32[264,128]{1,0:T(8,128)S(1)}, f32[264,128]{1,0:T(8,128)S(1)}, u32[]{:S(2)}, u32[]{:S(2)}) %collective-permute-start) | collective-permute-done | bytes 135200 | tf_op jit(solution)/shard_map/ppermute | solution.py:179
  8.0 0.5 %right_0.1 = (f32[64,384]{1,0:T(8,128)S(1)}, f32[64,384]{1,0:T(8,128)S(1)}, f32[64,384]{1,0:T(8,128)S(1)}) custom-call(f32[264,128]{1,0:T(8,128)S(1)} %pack.1.earlier_ref.refs_0_, bf16[4,192,256]{2,1,0:T(8,128)(2,1)S(1)} %get-tuple-element.13.hi_ref, bf16[4,192,256]{2,1,0:T(8,128)(2,1)S(1)} %get-tuple-element.14.lo_ref, ...), custom_call_target="tpu_custom_call" | custom-call | flops 113246208 | bytes 2000000 | tf_op jit(solution)/shard_map/right_0/pallas_call | solution.py:200
  8.5 2.1 %collective-permute-start.1 = (f32[64,384]{1,0:T(8,128)S(1)}, f32[64,384]{1,0:T(8,128)S(1)}, u32[]{:S(2)}, u32[]{:S(2)}) collective-permute-start(f32[64,384]{1,0:T(8,128)S(1)} %get-tuple-element.16), channel_id=1, source_target_pairs={{0,7},{1,2},{2,1},{3,4},{4,3},{5,6},{6,5},{7,0},{8,15},{9,10},{10,... | collective-permute-start | bytes 294920 | tf_op jit(solution)/shard_map/ppermute | solution.py:215
  10.6 0.0 collective-permute-start.2
  10.6 1.3 %collective-permute-done.3.refs_0_ = f32[264,128]{1,0:T(8,128)S(1)} collective-permute-done((f32[264,128]{1,0:T(8,128)S(1)}, f32[264,128]{1,0:T(8,128)S(1)}, u32[]{:S(2)}, u32[]{:S(2)}) %collective-permute-start.3) | collective-permute-done | bytes 135200 | tf_op jit(solution)/shard_map/ppermute | solution.py:179
  11.9 0.0 collective-permute-done.4.refs_1_
  11.9 0.5 %right_1.1 = (f32[64,384]{1,0:T(8,128)S(1)}, f32[64,384]{1,0:T(8,128)S(1)}, f32[64,384]{1,0:T(8,128)S(1)}) custom-call(f32[64,384]{1,0:T(8,128)S(1)} %get-tuple-element.15.earlier_ref.refs_0_, bf16[4,192,256]{2,1,0:T(8,128)(2,1)S(1)} %get-tuple-element.13.hi_ref, bf16[4,192,256]{2,1,0:T(8,128)(2,1)S(1)} %get-tuple-element.14.lo_ref, ...), custom_call_target="tpu_custom_call" | custom-call | flops 113246208 | bytes 2000000 | tf_op jit(solution)/shard_map/right_1/pallas_call | solution.py:200
  12.5 1.9 %collective-permute-start.5 = (f32[64,384]{1,0:T(8,128)S(1)}, f32[64,384]{1,0:T(8,128)S(1)}, u32[]{:S(2)}, u32[]{:S(2)}) collective-permute-start(f32[64,384]{1,0:T(8,128)S(1)} %get-tuple-element.19), channel_id=1, source_target_pairs={{0,7},{1,2},{2,1},{3,4},{4,3},{5,6},{6,5},{7,0},{8,15},{9,10},{10,... | collective-permute-start | bytes 294920 | tf_op jit(solution)/shard_map/ppermute | solution.py:215
  14.4 0.0 collective-permute-start.6
  14.4 0.5 %collective-permute-done.1.refs_1_ = f32[64,384]{1,0:T(8,128)S(1)} collective-permute-done((f32[64,384]{1,0:T(8,128)S(1)}, f32[64,384]{1,0:T(8,128)S(1)}, u32[]{:S(2)}, u32[]{:S(2)}) %collective-permute-start.1) | collective-permute-done | bytes 98336 | tf_op jit(solution)/shard_map/ppermute | solution.py:215
  14.9 0.0 collective-permute-done.2.refs_2_
  14.9 4.3 %collective-permute-done.5.refs_4_ = f32[64,384]{1,0:T(8,128)S(1)} collective-permute-done((f32[64,384]{1,0:T(8,128)S(1)}, f32[64,384]{1,0:T(8,128)S(1)}, u32[]{:S(2)}, u32[]{:S(2)}) %collective-permute-start.5) | collective-permute-done | bytes 98336 | tf_op jit(solution)/shard_map/ppermute | solution.py:215
  19.2 0.0 collective-permute-done.6.refs_5_
  19.2 0.8 %add.1 = f32[64,1280]{1,0:T(8,128)} custom-call(f32[64,384]{1,0:T(8,128)S(1)} %get-tuple-element.15.earlier_ref.refs_0_, f32[64,384]{1,0:T(8,128)S(1)} %collective-permute-done.1.refs_1_, f32[64,384]{1,0:T(8,128)S(1)} %collective-permute-done.2.refs_2_, f32[64,384]{1,0:T(8,128)S(1)} %get-tuple-element.18.refs_3_, ...), custom_call_target="tpu_custom_call" | custom-call | tf_op jit(solution)/shard_map/add/pallas_call | solution.py:218
  (1 shorter events, 0.0 us)
Async XLA Ops:
  0.0 0.9 %copy-start = (f32[4,64,128]{2,1,0:T(8,128)S(1)}, f32[4,64,128]{2,1,0:T(8,128)}, u32[]{:S(2)}) copy-start(f32[4,64,128]{2,1,0:T(8,128)} %p_ref.1) | copy-start | bytes 393220
  0.0 0.9 %copy-start.1 = (s32[4,2]{0,1:T(2,128)S(1)}, s32[4,2]{0,1:T(2,128)}, u32[]{:S(2)}) copy-start(s32[4,2]{0,1:T(2,128)} %param.9) | copy-start | bytes 100
  0.0 5.5 %copy-start.2 = (f32[4,64,256]{2,1,0:T(8,128)S(1)}, f32[4,64,256]{2,1,0:T(8,128)}, u32[]{:S(2)}) copy-start(f32[4,64,256]{2,1,0:T(8,128)} %a_ref.1) | copy-start | bytes 786436
  0.9 4.6 %copy-start.3 = (s32[4,4]{1,0:T(4,128)S(1)}, s32[4,4]{1,0:T(4,128)}, u32[]{:S(2)}) copy-start(s32[4,4]{1,0:T(4,128)} %group_ref.1) | copy-start | bytes 196
  0.9 4.6 %copy-start.4 = (s32[4,4]{1,0:T(4,128)S(1)}, s32[4,4]{1,0:T(4,128)}, u32[]{:S(2)}) copy-start(s32[4,4]{1,0:T(4,128)} %row_ref.1) | copy-start | bytes 196
  1.0 7.0 %collective-permute-start = (f32[264,128]{1,0:T(8,128)S(1)}, f32[264,128]{1,0:T(8,128)S(1)}, u32[]{:S(2)}, u32[]{:S(2)}) collective-permute-start(f32[264,128]{1,0:T(8,128)S(1)} %pack.1.earlier_ref.refs_0_), channel_id=1, source_target_pairs={{0,8},{8,0},{16,24},{24,16},{1,9},{9,1},{17,25},{25,17},{2,10},{10... | collective-permute-start | bytes 405512 | tf_op jit(solution)/shard_map/ppermute | solution.py:179
  4.0 7.9 %collective-permute-start.3 = (f32[264,128]{1,0:T(8,128)S(1)}, f32[264,128]{1,0:T(8,128)S(1)}, u32[]{:S(2)}, u32[]{:S(2)}) collective-permute-start(f32[264,128]{1,0:T(8,128)S(1)} %pack.1.earlier_ref.refs_0_), channel_id=1, source_target_pairs={{0,16},{8,24},{16,0},{24,8},{1,17},{9,25},{17,1},{25,9},{2,18},{10... | collective-permute-start | bytes 405512 | tf_op jit(solution)/shard_map/ppermute | solution.py:179
  5.5 6.4 %collective-permute-start.4 = (f32[264,128]{1,0:T(8,128)S(1)}, f32[264,128]{1,0:T(8,128)S(1)}, u32[]{:S(2)}, u32[]{:S(2)}) collective-permute-start(f32[264,128]{1,0:T(8,128)S(1)} %pack.1.earlier_ref.refs_0_), channel_id=1, source_target_pairs={{0,24},{8,16},{16,8},{24,0},{1,25},{9,17},{17,9},{25,1},{2,26},{10... | collective-permute-start | bytes 405512 | tf_op jit(solution)/shard_map/ppermute | solution.py:179
  8.5 6.3 %collective-permute-start.1 = (f32[64,384]{1,0:T(8,128)S(1)}, f32[64,384]{1,0:T(8,128)S(1)}, u32[]{:S(2)}, u32[]{:S(2)}) collective-permute-start(f32[64,384]{1,0:T(8,128)S(1)} %get-tuple-element.16), channel_id=1, source_target_pairs={{0,7},{1,2},{2,1},{3,4},{4,3},{5,6},{6,5},{7,0},{8,15},{9,10},{10,... | collective-permute-start | bytes 294920 | tf_op jit(solution)/shard_map/ppermute | solution.py:215
  10.6 4.3 %collective-permute-start.2 = (f32[64,384]{1,0:T(8,128)S(1)}, f32[64,384]{1,0:T(8,128)S(1)}, u32[]{:S(2)}, u32[]{:S(2)}) collective-permute-start(f32[64,384]{1,0:T(8,128)S(1)} %get-tuple-element.17), channel_id=1, source_target_pairs={{0,1},{1,0},{2,3},{3,2},{4,5},{5,4},{6,7},{7,6},{8,9},{9,8},{10,11... | collective-permute-start | bytes 294920 | tf_op jit(solution)/shard_map/ppermute | solution.py:216
  12.5 6.7 %collective-permute-start.5 = (f32[64,384]{1,0:T(8,128)S(1)}, f32[64,384]{1,0:T(8,128)S(1)}, u32[]{:S(2)}, u32[]{:S(2)}) collective-permute-start(f32[64,384]{1,0:T(8,128)S(1)} %get-tuple-element.19), channel_id=1, source_target_pairs={{0,7},{1,2},{2,1},{3,4},{4,3},{5,6},{6,5},{7,0},{8,15},{9,10},{10,... | collective-permute-start | bytes 294920 | tf_op jit(solution)/shard_map/ppermute | solution.py:215
  14.4 4.8 %collective-permute-start.6 = (f32[64,384]{1,0:T(8,128)S(1)}, f32[64,384]{1,0:T(8,128)S(1)}, u32[]{:S(2)}, u32[]{:S(2)}) collective-permute-start(f32[64,384]{1,0:T(8,128)S(1)} %get-tuple-element.20), channel_id=1, source_target_pairs={{0,1},{1,0},{2,3},{3,2},{4,5},{5,4},{6,7},{7,6},{8,9},{9,8},{10,11... | collective-permute-start | bytes 294920 | tf_op jit(solution)/shard_map/ppermute | solution.py:216

commit v6 on v5

--- a/solution.py
+++ b/solution.py
@@ -8,7 +8,7 @@
 from jax.sharding import PartitionSpec as P
 
 SHIFTS = 3
-CHUNKS = 2
+LAG = 1
 PARAMS = pltpu.CompilerParams(vmem_limit_bytes=24 * 1024 * 1024)
 
 
@@ -48,7 +48,7 @@
     out_ref[deep:, :] = jnp.concatenate(straight + crossed, axis=0).astype(jnp.float32)
 
 
-def left_kernel(width, group_ref, row_ref, code_ref, a_ref, p_ref, hi_ref, lo_ref, b_hi_ref, b_lo_ref):
+def left_kernel(width, group_ref, row_ref, code_ref, a_ref, packed_ref, hi_ref, lo_ref, b_hi_ref, b_lo_ref):
     rows, per_row = group_ref.shape
     groups = hi_ref.shape[0]
     me = lax.axis_index("blk")
@@ -69,7 +69,7 @@
             at = pl.ds(pl.multiple_of((s // 2) * pair, pair), pair)
             b_hi_ref[j, i * width : (i + 1) * width, at] = x_hi
             b_lo_ref[j, i * width : (i + 1) * width, at] = x_lo
-    pt = p_ref[...].reshape(wide, pair).T
+    pt = packed_ref[:wide, :].T
     row_of = lax.broadcasted_iota(jnp.int32, (1, wide), 1) // width
     codes = []
     for n in range(2):
@@ -91,33 +91,31 @@
     lane = lax.broadcasted_iota(jnp.int32, (1, 2 * width), 1)
     low = jnp.where(lane < width, 0.0, 1.0)
     high = jnp.where(lane < width, 2.0, -1.0)
-    deep = rows * width
+    base = rows * width
     near, far = [], []
     for s in range(rows):
         x = src[s * width : (s + 1) * width, :]
         y = pltpu.roll(x, width, 1)
-        straight = src[deep + s : deep + s + 1, :]
-        crossed = src[deep + rows + s : deep + rows + s + 1, :]
+        straight = src[base + s : base + s + 1, :]
+        crossed = src[base + rows + s : base + rows + s + 1, :]
         near.append(jnp.where(straight == low, x, 0.0) + jnp.where(crossed == low, y, 0.0))
         far.append(jnp.where(straight == high, x, 0.0) + jnp.where(crossed == high, y, 0.0))
     return jnp.concatenate([jnp.concatenate(near, axis=0), jnp.concatenate(far, axis=0)], axis=1)
 
 
-def right_kernel(width, first, earlier_ref, hi_ref, lo_ref, *refs):
-    sources, (own_ref, chip_ref, far_ref) = refs[:-3], refs[-3:]
+def multiply(hi_ref, lo_ref, slot, src, width):
     rows = hi_ref.shape[2] // width
-    me = lax.axis_index("blk")
+    return dot3(hi_ref[slot], lo_ref[slot], *split(spread(src, rows, width)))
+
+
+def lay_out(found, outs, width):
+    swap = lax.axis_index("blk") % 2 == 1
     pair = 2 * width
-    pairs = len(sources) // 2
+    pairs = len(found) // 2
     right_half = lax.broadcasted_iota(jnp.int32, (width, pair), 1) >= width
     for q in range(pairs):
-        found = []
-        for j in (2 * q, 2 * q + 1):
-            w_hi, w_lo = split(spread(sources[j], rows, width))
-            found.append(dot3(hi_ref[first + j], lo_ref[first + j], w_hi, w_lo))
-        swap = me % 2 == 1
-        for t, out_ref in enumerate((own_ref, chip_ref, far_ref)):
-            a, b = (f[t * width : (t + 1) * width] for f in found)
+        for t, out_ref in enumerate(outs):
+            a, b = (f[t * width : (t + 1) * width] for f in found[2 * q : 2 * q + 2])
             before = jnp.where(swap, b, a)
             after = jnp.where(swap, a, b)
             for e in range(SHIFTS):
@@ -131,26 +129,67 @@
                 out_ref[:, at : at + pair] = jnp.where(right_half, v, u)
 
 
-def add_kernel(groups, *refs):
-    out_ref = refs[-1]
+def near_kernel(width, hi_ref, lo_ref, *refs):
+    lay_out([multiply(hi_ref, lo_ref, j, src, width) for j, src in enumerate(refs[:-3])], refs[-3:], width)
+
+
+def product_kernel(width, first, turn, earlier_ref, hi_ref, lo_ref, *refs):
+    sources, out_ref = refs[:-1], refs[-1]
+
+    @pl.when(lax.axis_index("band") % 2 == turn)
+    def _():
+        for j, src in enumerate(sources):
+            out_ref[j] = multiply(hi_ref, lo_ref, first + j, src, width)
+
+
+def join_kernel(width, turn, hi_ref, lo_ref, found_ref, last_ref, *refs):
+    handed, outs = refs[:-3], refs[-3:]
+    mine = lax.axis_index("band") % 2 == turn
+
+    @pl.when(mine)
+    def _():
+        found = [found_ref[j] for j in range(found_ref.shape[0])]
+        found.append(multiply(hi_ref, lo_ref, hi_ref.shape[0] - 1, last_ref, width))
+        lay_out(found, outs, width)
+
+    @pl.when(jnp.logical_not(mine))
+    def _():
+        for out_ref in outs[: 3 - len(handed)]:
+            out_ref[...] = jnp.zeros_like(out_ref)
+        for out_ref, given_ref in zip(outs[3 - len(handed) :], handed):
+            out_ref[...] = given_ref[...]
+
+
+def place(sum_ref, part_ref, groups, first, shift):
     me = lax.axis_index("blk")
-    odd = lax.axis_index("band") % 2 == 1
-    step = out_ref.shape[1] // 5
-    pair = 2 * step // groups
-    pairs = groups // 2 // CHUNKS
-    for c in range(CHUNKS):
-        own_ref, far_ref, chip_ref = refs[3 * c : 3 * c + 3]
-        for q in range(pairs):
-            place = ((me ^ (2 * (c * pairs + q))) // 2) * pair
-            at = [slice((e * pairs + q) * pair, (e * pairs + q + 1) * pair) for e in range(SHIFTS)]
-            own = [own_ref[:, t] for t in at]
-            chip = [chip_ref[:, t] for t in at]
-            far = [far_ref[:, t] for t in at]
-            lower = [jnp.where(odd, u, v) for u, v in zip(chip, far)]
-            upper = [jnp.where(odd, v, u) for u, v in zip(chip, far)]
-            sums = [lower[0], lower[1] + own[0], lower[2] + own[1] + upper[0], own[2] + upper[1], upper[2]]
-            for e in range(5):
-                out_ref[:, pl.ds(pl.multiple_of(e * step + place, pair), pair)] = sums[e]
+    pair = 2 * part_ref.shape[0]
+    pairs = part_ref.shape[1] // (SHIFTS * pair)
+    for q in range(pairs):
+        tile = (me ^ (first + 2 * q)) // 2
+        for e in range(SHIFTS):
+            at = pl.ds(pl.multiple_of(((e + shift) * (groups // 2) + tile) * pair, pair), pair)
+            sum_ref[:, at] += part_ref[:, (e * pairs + q) * pair : (e * pairs + q + 1) * pair]
+
+
+def first_kernel(groups, near_ref, far_ref, out_ref):
+    out_ref[...] = jnp.zeros_like(out_ref)
+    place(out_ref, near_ref, groups, 0, 1)
+    place(out_ref, far_ref, groups, 0, 2 * (lax.axis_index("band") % 2))
+
+
+def early_kernel(groups, first_ref, rest_ref, up_ref, out_ref):
+    span = groups // 2
+    out_ref[...] = first_ref[...]
+    place(out_ref, rest_ref, groups, span, 1)
+    place(out_ref, up_ref, groups, span * (1 - lax.axis_index("band") % 2), 0)
+
+
+def late_kernel(groups, early_ref, down_ref, chip_ref, out_ref):
+    odd = lax.axis_index("band") % 2
+    span = groups // 2
+    out_ref[...] = early_ref[...]
+    place(out_ref, chip_ref, groups, span, 2 - 2 * odd)
+    place(out_ref, down_ref, groups, span * odd, 2)
 
 
 def body(fine_blocks, source_group, source_row, prolong_blocks, prolong_code):
@@ -175,11 +214,36 @@
         compiler_params=PARAMS,
         name="pack",
     )(lanes, prolong_code, prolong_blocks.reshape(rows * width, pair))
-    arrived = [packed] + [
-        lax.ppermute(packed, "blk", [(i, i ^ j) for i in range(groups)]) for j in range(1, groups)
-    ]
     height = SHIFTS * width
     deep = rows * width
+
+    def call(kernel, name, shapes, dtype=f32, inputs=0, **more):
+        more.setdefault("in_specs", [vmem()] * inputs)
+        single = not isinstance(shapes, list)
+        out = [jax.ShapeDtypeStruct(x, dtype) for x in ([shapes] if single else shapes)]
+        return pl.pallas_call(
+            kernel,
+            out_shape=out[0] if single else out,
+            out_specs=vmem() if single else [vmem()] * len(out),
+            compiler_params=PARAMS,
+            name=name,
+            **more,
+        )
+
+    def gather(offsets):
+        to = []
+        for b in range(groups):
+            for r in range(bands):
+                offset = offsets[r % 2]
+                other = (b, r ^ 2) if offset is None else (b ^ offset, r)
+                to.append((b * bands + r, other[0] * bands + other[1]))
+        return lax.ppermute(packed, ("blk", "band"), to)
+
+    span = groups // 2
+    sources = [packed] + [gather((j, j)) for j in range(1, span)]
+    odd_steps = [*range(span, groups)] + [None] * LAG
+    even_steps = [None] * LAG + [*range(span, groups)]
+    rest = [gather(offsets) for offsets in zip(even_steps, odd_steps)]
     hi, lo = pl.pallas_call(
         functools.partial(left_kernel, width),
         out_shape=[jax.ShapeDtypeStruct((groups, height, deep), jnp.bfloat16)] * 2,
@@ -191,38 +255,38 @@
         ),
         compiler_params=PARAMS,
         name="left",
-    )(source_group, source_row, prolong_code, fine_blocks, prolong_blocks)
-    span = groups // CHUNKS
-    parts = []
-    own = packed
-    for c in range(CHUNKS):
-        shape = (width, SHIFTS * span * width)
-        own, chip, far = pl.pallas_call(
-            functools.partial(right_kernel, width, c * span),
-            out_shape=[
-                jax.ShapeDtypeStruct(shape, f32),
-                jax.ShapeDtypeStruct(shape, f32),
-                jax.ShapeDtypeStruct(shape, f32),
-            ],
-            in_specs=[pl.BlockSpec(memory_space=pl.ANY)] + [vmem()] * (2 + span),
-            out_specs=[vmem()] * 3,
-            cost_estimate=pl.CostEstimate(
-                flops=6 * span * height * height * deep, bytes_accessed=2000000, transcendentals=0
-            ),
-            compiler_params=PARAMS,
-            name=f"right_{c}",
-        )(own, hi, lo, *arrived[c * span : (c + 1) * span])
-        far = lax.ppermute(far, "band", [(i, (i + 1 if i % 2 else i - 1) % bands) for i in range(bands)])
-        chip = lax.ppermute(chip, "band", [(i, i ^ 1) for i in range(bands)])
-        parts += [own, far, chip]
-    return pl.pallas_call(
-        functools.partial(add_kernel, groups),
-        out_shape=jax.ShapeDtypeStruct((width, 5 * groups * width), f32),
-        in_specs=[vmem()] * len(parts),
-        out_specs=vmem(),
-        compiler_params=PARAMS,
-        name="add",
-    )(*parts)
+    )(source_group, source_row, prolong_code, fine_blocks, packed)
+
+    def products(name, turn, sources, earlier):
+        kernel = functools.partial(product_kernel, width, span, turn)
+        specs = [pl.BlockSpec(memory_space=pl.ANY)] + [vmem()] * (2 + len(sources))
+        shape = (len(sources), height, 2 * pair)
+        return call(kernel, name, shape, in_specs=specs)(earlier, hi, lo, *sources)
+
+    parts = [(width, SHIFTS * span * width)] * 3
+
+    def join(name, turn, found, last, *handed):
+        kernel = functools.partial(join_kernel, width, turn)
+        return call(kernel, name, parts, inputs=4 + len(handed))(hi, lo, found, last, *handed)
+
+    own_near, chip_near, far = call(
+        functools.partial(near_kernel, width), "near", parts, inputs=2 + span
+    )(hi, lo, *sources)
+    far = lax.ppermute(far, "band", [(i, (i + 1 if i % 2 else i - 1) % bands) for i in range(bands)])
+    found = products("rest_odd", 1, rest[: span - 1], own_near)
+    own, chip, up = join("join_odd", 1, found, rest[span - 1], chip_near)
+    up = lax.ppermute(up, "band", [(i, (i + 1) % bands) for i in range(bands)])
+    found = products("rest_even", 0, rest[LAG : LAG + span - 1], own)
+    own, chip, down = join("join_even", 0, found, rest[-1], own, chip, chip_near)
+    down = lax.ppermute(down, "band", [((i + 1) % bands, i) for i in range(bands)])
+    chip = lax.ppermute(chip, "band", [(i, i ^ 1) for i in range(bands)])
+    whole = (width, 5 * groups * width)
+    slow = pl.CostEstimate(flops=4000000000, bytes_accessed=2000000, transcendentals=0)
+    first = call(functools.partial(first_kernel, groups), "first", whole, inputs=2)(own_near, far)
+    early = call(functools.partial(early_kernel, groups), "early", whole, inputs=3, cost_estimate=slow)(
+        first, own, up
+    )
+    return call(functools.partial(late_kernel, groups), "late", whole, inputs=3)(early, down, chip)
 
 
 def solution(mesh):

time: 20.1 us -> 18.9 us (0.940)
  the two profiles are of different devices: /device:TPU:0 before, /device:TPU:1 now
where the time goes in v6:
time: 18.9 us; the launch traced here: 18.8 us
  starting transfers between devices  11.6 us (61%)
  Pallas kernels  3.64 us (19%)
  waiting for transfers between devices  2.47 us (13%)
  local copies, waits for them, and re-layouts  0.89 us (5%)
    ppermute x4, starting transfers between devices, gather(): return lax.ppermute(packed, ('blk', 'band'), to)  4.84 us
    ppermute x1, starting transfers between devices, body(): up = lax.ppermute(up, 'band', [(i, (i + 1) % bands) for i in range(bands)])  2.68 us
    ppermute x1, waiting for transfers between devices, body(): lax.ppermute(down, 'band', [((i + 1) % bands, i) for i in range(bands)])  2.45 us
    ppermute x1, starting transfers between devices, body(): lax.ppermute(far, 'band', [(i, (i + 1 if i % 2 else i - 1) % bands) for i...  2.44 us
    ppermute x1, starting transfers between devices, body(): chip = lax.ppermute(chip, 'band', [(i, i ^ 1) for i in range(bands)])  1.63 us
    pallas_call x1, Pallas kernels, body(): pl.pallas_call(functools.partial(left_kernel, width), out_shape=[jax.Shap...  1.3 us
    unnamed x10, local copies, waits for them, and re-layouts  0.89 us
    pallas_call x1, Pallas kernels, body(): call(functools.partial(late_kernel, groups), 'late', whole, inputs=3)  0.78 us
  transfers between devices with their start and end apart: 8, of which 1 were waited for; matrix products, arithmetic and copies ran while one was open for 0% of the time, Pallas kernels for 15%

profile of v6, /device:TPU:1, one launch (start us, length us, event | category | flops | bytes accessed | tf_op | source)
XLA Modules:
  0.0 18.8 jit_solution(5335288058107113636)
XLA Ops:
  0.0 0.0 copy-start
  0.0 0.0 copy-start.1
  0.0 0.0 copy-start.2
  0.0 0.9 %copy-done = f32[4,64,128]{2,1,0:T(8,128)S(1)} copy-done((f32[4,64,128]{2,1,0:T(8,128)S(1)}, f32[4,64,128]{2,1,0:T(8,128)}, u32[]{:S(2)}) %copy-start) | copy-done | bytes 131096
  0.9 0.0 copy-done.1
  0.9 0.0 copy-start.3
  0.9 0.1 pack.1.packed_ref.refs_0_
  1.0 2.1 %collective-permute-start = (f32[264,128]{1,0:T(8,128)S(1)}, f32[264,128]{1,0:T(8,128)S(1)}, u32[]{:S(2)}, u32[]{:S(2)}) collective-permute-start(f32[264,128]{1,0:T(8,128)S(1)} %pack.1.packed_ref.refs_0_), channel_id=1, source_target_pairs={{0,8},{1,9},{2,10},{3,11},{4,12},{5,13},{6,14},{7,15},{8,0},{9,1},... | collective-permute-start | bytes 405512 | tf_op jit(solution)/shard_map/ppermute | solution.py:240
  3.1 1.2 %collective-permute-start.2 = (f32[264,128]{1,0:T(8,128)S(1)}, f32[264,128]{1,0:T(8,128)S(1)}, u32[]{:S(2)}, u32[]{:S(2)}) collective-permute-start(f32[264,128]{1,0:T(8,128)S(1)} %pack.1.packed_ref.refs_0_), channel_id=1, source_target_pairs={{0,2},{1,17},{2,0},{3,19},{4,6},{5,21},{6,4},{7,23},{8,10},{9,25},... | collective-permute-start | bytes 405512 | tf_op jit(solution)/shard_map/ppermute | solution.py:240
  4.3 0.0 collective-permute-start.3
  4.4 1.5 %collective-permute-start.4 = (f32[264,128]{1,0:T(8,128)S(1)}, f32[264,128]{1,0:T(8,128)S(1)}, u32[]{:S(2)}, u32[]{:S(2)}) collective-permute-start(f32[264,128]{1,0:T(8,128)S(1)} %pack.1.packed_ref.refs_0_), channel_id=1, source_target_pairs={{0,24},{1,3},{2,26},{3,1},{4,28},{5,7},{6,30},{7,5},{8,16},{9,11},... | collective-permute-start | bytes 405512 | tf_op jit(solution)/shard_map/ppermute | solution.py:240
  5.8 0.0 copy-done.2
  5.8 0.0 copy-done.3
  5.8 0.0 copy-done.4
  5.8 1.3 %left.1 = (bf16[4,192,256]{2,1,0:T(8,128)(2,1)S(1)}, bf16[4,192,256]{2,1,0:T(8,128)(2,1)S(1)}) custom-call(s32[4,4]{1,0:T(4,128)S(1)} %copy-done.3, s32[4,4]{1,0:T(4,128)S(1)} %copy-done.4, s32[2,4]{1,0:T(2,128)S(1)} %bitcast.4, f32[4,64,256]{2,1,0:T(8,128)S(1)} %copy-done.2, f32[264,128]{1,0:T(8,128)S(1)} %pack.1.packed_ref.refs_0_), custom_call_target="tpu_custom_call" | custom-call | flops 301989888 | bytes 2000000 | tf_op jit(solution)/shard_map/left/pallas_call | solution.py:247
  7.2 0.0 collective-permute-done.refs_1_
  7.2 0.5 %near.1 = (f32[64,384]{1,0:T(8,128)S(1)}, f32[64,384]{1,0:T(8,128)S(1)}, f32[64,384]{1,0:T(8,128)S(1)}) custom-call(bf16[4,192,256]{2,1,0:T(8,128)(2,1)S(1)} %get-tuple-element.16.hi_ref, bf16[4,192,256]{2,1,0:T(8,128)(2,1)S(1)} %get-tuple-element.17.lo_ref, f32[264,128]{1,0:T(8,128)S(1)} %pack.1.packed_ref.refs_0_, f32[264,128]{1,0:T(8,128)S(1)} %collective-permute-done.refs_1_), custom_call_target="tpu_custom_call" | custom-call | tf_op jit(solution)/shard_map/near/pallas_call | solution.py:272
  7.7 2.4 %collective-permute-start.1 = (f32[64,384]{1,0:T(8,128)S(1)}, f32[64,384]{1,0:T(8,128)S(1)}, u32[]{:S(2)}, u32[]{:S(2)}) collective-permute-start(f32[64,384]{1,0:T(8,128)S(1)} %get-tuple-element.19), channel_id=1, source_target_pairs={{0,7},{1,2},{2,1},{3,4},{4,3},{5,6},{6,5},{7,0},{8,15},{9,10},{10,... | collective-permute-start | bytes 294920 | tf_op jit(solution)/shard_map/ppermute | solution.py:275
  10.2 0.0 collective-permute-done.2.refs_0_
  10.2 0.3 %rest_odd.1.found_ref = f32[1,192,256]{2,1,0:T(8,128)S(1)} custom-call(f32[64,384]{1,0:T(8,128)S(1)} %get-tuple-element.18.near_ref.earlier_ref, bf16[4,192,256]{2,1,0:T(8,128)(2,1)S(1)} %get-tuple-element.16.hi_ref, bf16[4,192,256]{2,1,0:T(8,128)(2,1)S(1)} %get-tuple-element.17.lo_ref, f32[264,128]{1,0:T(8,128)S(1)} %collective-permute-done.2.refs_0_), custom_call_target="tpu_custom_call" | custom-call | tf_op jit(solution)/shard_map/rest_odd/pallas_call | solution.py:264
  10.5 0.0 collective-permute-done.3.last_ref.refs_0_
  10.5 0.5 %join_odd.1 = (f32[64,384]{1,0:T(8,128)S(1)}, f32[64,384]{1,0:T(8,128)S(1)}, f32[64,384]{1,0:T(8,128)S(1)}) custom-call(bf16[4,192,256]{2,1,0:T(8,128)(2,1)S(1)} %get-tuple-element.16.hi_ref, bf16[4,192,256]{2,1,0:T(8,128)(2,1)S(1)} %get-tuple-element.17.lo_ref, f32[1,192,256]{2,1,0:T(8,128)S(1)} %rest_odd.1.found_ref, ...), custom_call_target="tpu_custom_call" | custom-call | tf_op jit(solution)/shard_map/join_odd/pallas_call | solution.py:270
  11.0 2.7 %collective-permute-start.5 = (f32[64,384]{1,0:T(8,128)S(1)}, f32[64,384]{1,0:T(8,128)S(1)}, u32[]{:S(2)}, u32[]{:S(2)}) collective-permute-start(f32[64,384]{1,0:T(8,128)S(1)} %get-tuple-element.24), channel_id=1, source_target_pairs={{0,1},{1,2},{2,3},{3,4},{4,5},{5,6},{6,7},{7,0},{8,9},{9,10},{10,1... | collective-permute-start | bytes 294920 | tf_op jit(solution)/shard_map/ppermute | solution.py:278
  13.7 0.0 collective-permute-done.4.last_ref
  13.7 0.1 collective-permute-start.6
  13.8 1.6 %collective-permute-start.7 = (f32[64,384]{1,0:T(8,128)S(1)}, f32[64,384]{1,0:T(8,128)S(1)}, u32[]{:S(2)}, u32[]{:S(2)}) collective-permute-start(f32[64,384]{1,0:T(8,128)S(1)} %get-tuple-element.26), channel_id=1, source_target_pairs={{0,1},{1,0},{2,3},{3,2},{4,5},{5,4},{6,7},{7,6},{8,9},{9,8},{10,11... | collective-permute-start | bytes 294920 | tf_op jit(solution)/shard_map/ppermute | solution.py:282
  15.4 0.0 collective-permute-done.1.far_ref
  15.5 0.0 collective-permute-done.5.up_ref
  15.5 0.1 early.1.early_ref
  15.5 2.4 %collective-permute-done.6.down_ref = f32[64,384]{1,0:T(8,128)S(1)} collective-permute-done((f32[64,384]{1,0:T(8,128)S(1)}, f32[64,384]{1,0:T(8,128)S(1)}, u32[]{:S(2)}, u32[]{:S(2)}) %collective-permute-start.6) | collective-permute-done | bytes 98336 | tf_op jit(solution)/shard_map/ppermute | solution.py:281
  18.0 0.0 collective-permute-done.7.chip_ref
  18.0 0.8 %late.1 = f32[64,1280]{1,0:T(8,128)} custom-call(f32[64,1280]{1,0:T(8,128)S(1)} %early.1.early_ref, f32[64,384]{1,0:T(8,128)S(1)} %collective-permute-done.6.down_ref, f32[64,384]{1,0:T(8,128)S(1)} %collective-permute-done.7.chip_ref), custom_call_target="tpu_custom_call" | custom-call | tf_op jit(solution)/shard_map/late/pallas_call | solution.py:289
  (5 shorter events, 0.1 us)
Async XLA Ops:
  0.0 0.9 %copy-start = (f32[4,64,128]{2,1,0:T(8,128)S(1)}, f32[4,64,128]{2,1,0:T(8,128)}, u32[]{:S(2)}) copy-start(f32[4,64,128]{2,1,0:T(8,128)} %param.8) | copy-start | bytes 393220
  0.0 0.9 %copy-start.1 = (s32[4,2]{0,1:T(2,128)S(1)}, s32[4,2]{0,1:T(2,128)}, u32[]{:S(2)}) copy-start(s32[4,2]{0,1:T(2,128)} %param.9) | copy-start | bytes 100
  0.0 5.8 %copy-start.2 = (f32[4,64,256]{2,1,0:T(8,128)S(1)}, f32[4,64,256]{2,1,0:T(8,128)}, u32[]{:S(2)}) copy-start(f32[4,64,256]{2,1,0:T(8,128)} %a_ref.1) | copy-start | bytes 786436
  0.9 4.9 %copy-start.3 = (s32[4,4]{1,0:T(4,128)S(1)}, s32[4,4]{1,0:T(4,128)}, u32[]{:S(2)}) copy-start(s32[4,4]{1,0:T(4,128)} %group_ref.1) | copy-start | bytes 196
  0.9 4.9 %copy-start.4 = (s32[4,4]{1,0:T(4,128)S(1)}, s32[4,4]{1,0:T(4,128)}, u32[]{:S(2)}) copy-start(s32[4,4]{1,0:T(4,128)} %row_ref.1) | copy-start | bytes 196
  1.0 6.2 %collective-permute-start = (f32[264,128]{1,0:T(8,128)S(1)}, f32[264,128]{1,0:T(8,128)S(1)}, u32[]{:S(2)}, u32[]{:S(2)}) collective-permute-start(f32[264,128]{1,0:T(8,128)S(1)} %pack.1.packed_ref.refs_0_), channel_id=1, source_target_pairs={{0,8},{1,9},{2,10},{3,11},{4,12},{5,13},{6,14},{7,15},{8,0},{9,1},... | collective-permute-start | bytes 405512 | tf_op jit(solution)/shard_map/ppermute | solution.py:240
  3.1 7.1 %collective-permute-start.2 = (f32[264,128]{1,0:T(8,128)S(1)}, f32[264,128]{1,0:T(8,128)S(1)}, u32[]{:S(2)}, u32[]{:S(2)}) collective-permute-start(f32[264,128]{1,0:T(8,128)S(1)} %pack.1.packed_ref.refs_0_), channel_id=1, source_target_pairs={{0,2},{1,17},{2,0},{3,19},{4,6},{5,21},{6,4},{7,23},{8,10},{9,25},... | collective-permute-start | bytes 405512 | tf_op jit(solution)/shard_map/ppermute | solution.py:240
  4.3 6.2 %collective-permute-start.3 = (f32[264,128]{1,0:T(8,128)S(1)}, f32[264,128]{1,0:T(8,128)S(1)}, u32[]{:S(2)}, u32[]{:S(2)}) collective-permute-start(f32[264,128]{1,0:T(8,128)S(1)} %pack.1.packed_ref.refs_0_), channel_id=1, source_target_pairs={{0,16},{1,25},{2,18},{3,27},{4,20},{5,29},{6,22},{7,31},{8,24},{9,... | collective-permute-start | bytes 405512 | tf_op jit(solution)/shard_map/ppermute | solution.py:240
  4.4 9.3 %collective-permute-start.4 = (f32[264,128]{1,0:T(8,128)S(1)}, f32[264,128]{1,0:T(8,128)S(1)}, u32[]{:S(2)}, u32[]{:S(2)}) collective-permute-start(f32[264,128]{1,0:T(8,128)S(1)} %pack.1.packed_ref.refs_0_), channel_id=1, source_target_pairs={{0,24},{1,3},{2,26},{3,1},{4,28},{5,7},{6,30},{7,5},{8,16},{9,11},... | collective-permute-start | bytes 405512 | tf_op jit(solution)/shard_map/ppermute | solution.py:240
  7.7 7.7 %collective-permute-start.1 = (f32[64,384]{1,0:T(8,128)S(1)}, f32[64,384]{1,0:T(8,128)S(1)}, u32[]{:S(2)}, u32[]{:S(2)}) collective-permute-start(f32[64,384]{1,0:T(8,128)S(1)} %get-tuple-element.19), channel_id=1, source_target_pairs={{0,7},{1,2},{2,1},{3,4},{4,3},{5,6},{6,5},{7,0},{8,15},{9,10},{10,... | collective-permute-start | bytes 294920 | tf_op jit(solution)/shard_map/ppermute | solution.py:275
  11.0 4.5 %collective-permute-start.5 = (f32[64,384]{1,0:T(8,128)S(1)}, f32[64,384]{1,0:T(8,128)S(1)}, u32[]{:S(2)}, u32[]{:S(2)}) collective-permute-start(f32[64,384]{1,0:T(8,128)S(1)} %get-tuple-element.24), channel_id=1, source_target_pairs={{0,1},{1,2},{2,3},{3,4},{4,5},{5,6},{6,7},{7,0},{8,9},{9,10},{10,1... | collective-permute-start | bytes 294920 | tf_op jit(solution)/shard_map/ppermute | solution.py:278
  13.7 4.3 %collective-permute-start.6 = (f32[64,384]{1,0:T(8,128)S(1)}, f32[64,384]{1,0:T(8,128)S(1)}, u32[]{:S(2)}, u32[]{:S(2)}) collective-permute-start(f32[64,384]{1,0:T(8,128)S(1)} %get-tuple-element.25), channel_id=1, source_target_pairs={{1,0},{2,1},{3,2},{4,3},{5,4},{6,5},{7,6},{0,7},{9,8},{10,9},{11,1... | collective-permute-start | bytes 294920 | tf_op jit(solution)/shard_map/ppermute | solution.py:281
  13.8 4.2 %collective-permute-start.7 = (f32[64,384]{1,0:T(8,128)S(1)}, f32[64,384]{1,0:T(8,128)S(1)}, u32[]{:S(2)}, u32[]{:S(2)}) collective-permute-start(f32[64,384]{1,0:T(8,128)S(1)} %get-tuple-element.26), channel_id=1, source_target_pairs={{0,1},{1,0},{2,3},{3,2},{4,5},{5,4},{6,7},{7,6},{8,9},{9,8},{10,11... | collective-permute-start | bytes 294920 | tf_op jit(solution)/shard_map/ppermute | solution.py:282

commit v7 on v6

--- a/solution.py
+++ b/solution.py
@@ -14,10 +14,6 @@
 
 def vmem():
     return pl.BlockSpec(memory_space=pltpu.VMEM)
-
-
-def smem():
-    return pl.BlockSpec(memory_space=pltpu.SMEM)
 
 
 def split(x):
@@ -48,34 +44,21 @@
     out_ref[deep:, :] = jnp.concatenate(straight + crossed, axis=0).astype(jnp.float32)
 
 
-def left_kernel(width, group_ref, row_ref, code_ref, a_ref, packed_ref, hi_ref, lo_ref, b_hi_ref, b_lo_ref):
+def left_kernel(width, group_ref, row_ref, code_ref, a_ref, packed_ref, hi_ref, lo_ref):
     rows, per_row = group_ref.shape
     groups = hi_ref.shape[0]
     me = lax.axis_index("blk")
     odd = lax.axis_index("band") % 2
     pair = 2 * width
     wide = rows * width
-    b_hi_ref[...] = jnp.zeros_like(b_hi_ref)
-    b_lo_ref[...] = jnp.zeros_like(b_lo_ref)
-    half = lax.broadcasted_iota(jnp.int32, (width, pair), 1) // width
-    for i in range(rows):
-        for k in range(per_row):
-            x = a_ref[i, :, (k // 2) * pair : (k // 2 + 1) * pair]
-            s = row_ref[i, k]
-            turned = pltpu.roll(x, width, 1)
-            x = jnp.where(half == s % 2, jnp.where(s % 2 == k % 2, x, turned), 0.0)
-            x_hi, x_lo = split(x)
-            j = group_ref[i, k] ^ me
-            at = pl.ds(pl.multiple_of((s // 2) * pair, pair), pair)
-            b_hi_ref[j, i * width : (i + 1) * width, at] = x_hi
-            b_lo_ref[j, i * width : (i + 1) * width, at] = x_lo
+    lane_block = lax.broadcasted_iota(jnp.int32, (rows, wide), 1) // width
     pt = packed_ref[:wide, :].T
-    row_of = lax.broadcasted_iota(jnp.int32, (1, wide), 1) // width
+    row_of = lane_block[:1]
     codes = []
     for n in range(2):
-        c = jnp.full((1, wide), code_ref[n, 0], jnp.int32)
+        c = jnp.broadcast_to(code_ref[n : n + 1, :1], (1, wide))
         for i in range(1, rows):
-            c = jnp.where(row_of == i, code_ref[n, i], c)
+            c = jnp.where(row_of == i, code_ref[n : n + 1, i : i + 1], c)
         codes.append(c)
     blocks = []
     for dest in (1, 2 - 2 * odd, 2 * odd):
@@ -83,8 +66,26 @@
             jnp.where(codes[0] == dest, pt[:width], 0.0) + jnp.where(codes[1] == dest, pt[width:], 0.0)
         )
     rt_hi, rt_lo = split(jnp.concatenate(blocks, axis=0))
+    left_half = lax.broadcasted_iota(jnp.int32, (width, pair), 1) < width
+    twice = []
+    for i in range(rows):
+        for k in range(0, per_row, 2):
+            x = a_ref[i, :, (k // 2) * pair : (k // 2 + 1) * pair]
+            y = pltpu.roll(x, width, 1)
+            twice += [jnp.where(left_half, x, y), jnp.where(left_half, y, x)]
+    slots = [group_ref[:, k : k + 1] ^ me for k in range(per_row)]
+    here = [row_ref[:, k : k + 1] == lane_block for k in range(per_row)]
     for j in range(groups):
-        hi_ref[j], lo_ref[j] = split(dot3(rt_hi, rt_lo, b_hi_ref[j], b_lo_ref[j]))
+        chosen = [jnp.where(here[k] & (slots[k] == j), 1, 0) for k in range(per_row)]
+        placed = []
+        for i in range(rows):
+            x = jnp.zeros((width, wide), jnp.float32)
+            for k in range(per_row):
+                block = twice[i * per_row + k]
+                x = jnp.where(chosen[k][i : i + 1] == 1, jnp.concatenate([block] * (rows // 2), axis=1), x)
+            placed.append(x)
+        b_hi, b_lo = split(jnp.concatenate(placed, axis=0))
+        hi_ref[j], lo_ref[j] = split(dot3(rt_hi, rt_lo, b_hi, b_lo))
 
 
 def spread(src, rows, width):
@@ -242,14 +243,13 @@
     span = groups // 2
     sources = [packed] + [gather((j, j)) for j in range(1, span)]
     odd_steps = [*range(span, groups)] + [None] * LAG
-    even_steps = [None] * LAG + [*range(span, groups)]
+    even_steps = [*range(span, groups - 1)] + [None] * LAG + [groups - 1]
     rest = [gather(offsets) for offsets in zip(even_steps, odd_steps)]
     hi, lo = pl.pallas_call(
         functools.partial(left_kernel, width),
         out_shape=[jax.ShapeDtypeStruct((groups, height, deep), jnp.bfloat16)] * 2,
-        in_specs=[smem()] * 3 + [vmem()] * 2,
+        in_specs=[vmem()] * 5,
         out_specs=[vmem()] * 2,
-        scratch_shapes=[pltpu.VMEM((groups, deep, deep), jnp.bfloat16)] * 2,
         cost_estimate=pl.CostEstimate(
             flops=6 * groups * height * deep * deep, bytes_accessed=2000000, transcendentals=0
         ),
@@ -276,7 +276,7 @@
     found = products("rest_odd", 1, rest[: span - 1], own_near)
     own, chip, up = join("join_odd", 1, found, rest[span - 1], chip_near)
     up = lax.ppermute(up, "band", [(i, (i + 1) % bands) for i in range(bands)])
-    found = products("rest_even", 0, rest[LAG : LAG + span - 1], own)
+    found = products("rest_even", 0, rest[: span - 1], own)
     own, chip, down = join("join_even", 0, found, rest[-1], own, chip, chip_near)
     down = lax.ppermute(down, "band", [((i + 1) % bands, i) for i in range(bands)])
     chip = lax.ppermute(chip, "band", [(i, i ^ 1) for i in range(bands)])

time: 18.9 us -> 18.3 us (0.968)
  Pallas kernels: 3.64 us -> 3.14 us
  starting transfers between devices: 11.6 us -> 11.1 us
  waiting for transfers between devices: 2.47 us -> 2.9 us
    ppermute x1, starting transfers between devices: 1.63 us -> 0.81 us  [body(): chip = lax.ppermute(chip, 'band', [(i, i ^ 1) for i in range(bands)])]
    ppermute x1, starting transfers between devices: 2.44 us -> 2.93 us  [body(): lax.ppermute(far, 'band', [(i, (i + 1 if i % 2 else i - 1) % bands) for i...]
    pallas_call x1, Pallas kernels: 1.3 us -> 0.81 us  [body(): pl.pallas_call(functools.partial(left_kernel, width), out_shape=[jax.Shap...]
    ppermute x1, waiting for transfers between devices: 0.01 us -> 0.46 us  [body(): up = lax.ppermute(up, 'band', [(i, (i + 1) % bands) for i in range(bands)])]
    ppermute x1, starting transfers between devices: 2.68 us -> 2.27 us  [body(): up = lax.ppermute(up, 'band', [(i, (i + 1) % bands) for i in range(bands)])]
    ppermute x1, starting transfers between devices: 0.06 us -> 0.29 us  [body(): lax.ppermute(down, 'band', [((i + 1) % bands, i) for i in range(bands)])]
  transfers between devices with their start and end apart: 8 -> 8, of which waited for: 1 -> 2; matrix products, arithmetic and copies ran while one was open for 0% -> 0% of each run, Pallas kernels for 15% -> 12%
where the time goes in v7:
time: 18.3 us; the launch traced here: 18.2 us
  starting transfers between devices  11.1 us (61%)
  Pallas kernels  3.14 us (17%)
  waiting for transfers between devices  2.9 us (16%)
  local copies, waits for them, and re-layouts  0.89 us (5%)
    ppermute x4, starting transfers between devices, gather(): return lax.ppermute(packed, ('blk', 'band'), to)  4.84 us
    ppermute x1, starting transfers between devices, body(): lax.ppermute(far, 'band', [(i, (i + 1 if i % 2 else i - 1) % bands) for i...  2.93 us
    ppermute x1, waiting for transfers between devices, body(): lax.ppermute(down, 'band', [((i + 1) % bands, i) for i in range(bands)])  2.43 us
    ppermute x1, starting transfers between devices, body(): up = lax.ppermute(up, 'band', [(i, (i + 1) % bands) for i in range(bands)])  2.27 us
    unnamed x10, local copies, waits for them, and re-layouts  0.89 us
    pallas_call x1, Pallas kernels, body(): pl.pallas_call(functools.partial(left_kernel, width), out_shape=[jax.Shap...  0.81 us
    ppermute x1, starting transfers between devices, body(): chip = lax.ppermute(chip, 'band', [(i, i ^ 1) for i in range(bands)])  0.81 us
    pallas_call x1, Pallas kernels, body(): call(functools.partial(late_kernel, groups), 'late', whole, inputs=3)  0.78 us
  transfers between devices with their start and end apart: 8, of which 2 were waited for; matrix products, arithmetic and copies ran while one was open for 0% of the time, Pallas kernels for 12%

profile of v7, /device:TPU:1, one launch (start us, length us, event | category | flops | bytes accessed | tf_op | source)
XLA Modules:
  0.0 18.2 jit_solution(8353681655687688780)
XLA Ops:
  0.0 0.0 copy-start
  0.0 0.0 copy-start.1
  0.0 0.0 copy-start.2
  0.0 0.9 %copy-done = f32[4,64,128]{2,1,0:T(8,128)S(1)} copy-done((f32[4,64,128]{2,1,0:T(8,128)S(1)}, f32[4,64,128]{2,1,0:T(8,128)}, u32[]{:S(2)}) %copy-start) | copy-done | bytes 131096
  0.9 0.0 copy-done.1
  0.9 0.0 copy-start.3
  0.9 0.0 copy-start.4
  0.9 0.1 pack.1.packed_ref.refs_0_
  1.0 2.1 %collective-permute-start = (f32[264,128]{1,0:T(8,128)S(1)}, f32[264,128]{1,0:T(8,128)S(1)}, u32[]{:S(2)}, u32[]{:S(2)}) collective-permute-start(f32[264,128]{1,0:T(8,128)S(1)} %pack.1.packed_ref.refs_0_), channel_id=1, source_target_pairs={{0,8},{1,9},{2,10},{3,11},{4,12},{5,13},{6,14},{7,15},{8,0},{9,1},... | collective-permute-start | bytes 405512 | tf_op jit(solution)/shard_map/ppermute | solution.py:241
  3.1 1.2 %collective-permute-start.2 = (f32[264,128]{1,0:T(8,128)S(1)}, f32[264,128]{1,0:T(8,128)S(1)}, u32[]{:S(2)}, u32[]{:S(2)}) collective-permute-start(f32[264,128]{1,0:T(8,128)S(1)} %pack.1.packed_ref.refs_0_), channel_id=1, source_target_pairs={{0,16},{1,17},{2,18},{3,19},{4,20},{5,21},{6,22},{7,23},{8,24},{9,... | collective-permute-start | bytes 405512 | tf_op jit(solution)/shard_map/ppermute | solution.py:241
  4.3 0.0 collective-permute-start.3
  4.4 1.5 %collective-permute-start.4 = (f32[264,128]{1,0:T(8,128)S(1)}, f32[264,128]{1,0:T(8,128)S(1)}, u32[]{:S(2)}, u32[]{:S(2)}) collective-permute-start(f32[264,128]{1,0:T(8,128)S(1)} %pack.1.packed_ref.refs_0_), channel_id=1, source_target_pairs={{0,24},{1,3},{2,26},{3,1},{4,28},{5,7},{6,30},{7,5},{8,16},{9,11},... | collective-permute-start | bytes 405512 | tf_op jit(solution)/shard_map/ppermute | solution.py:241
  5.8 0.0 copy-done.2
  5.8 0.0 copy-done.3
  5.8 0.0 copy-done.4
  5.8 0.8 %left.1 = (bf16[4,192,256]{2,1,0:T(8,128)(2,1)S(1)}, bf16[4,192,256]{2,1,0:T(8,128)(2,1)S(1)}) custom-call(s32[4,4]{1,0:T(4,128)S(1)} %copy-done.3, s32[4,4]{1,0:T(4,128)S(1)} %copy-done.4, s32[2,4]{1,0:T(2,128)S(1)} %bitcast.4, f32[4,64,256]{2,1,0:T(8,128)S(1)} %copy-done.2, f32[264,128]{1,0:T(8,128)S(1)} %pack.1.packed_ref.refs_0_), custom_call_target="tpu_custom_call" | custom-call | flops 301989888 | bytes 2000000 | tf_op jit(solution)/shard_map/left/pallas_call | solution.py:248
  6.7 0.0 collective-permute-done.refs_1_
  6.7 0.5 %near.1 = (f32[64,384]{1,0:T(8,128)S(1)}, f32[64,384]{1,0:T(8,128)S(1)}, f32[64,384]{1,0:T(8,128)S(1)}) custom-call(bf16[4,192,256]{2,1,0:T(8,128)(2,1)S(1)} %get-tuple-element.16.hi_ref, bf16[4,192,256]{2,1,0:T(8,128)(2,1)S(1)} %get-tuple-element.17.lo_ref, f32[264,128]{1,0:T(8,128)S(1)} %pack.1.packed_ref.refs_0_, f32[264,128]{1,0:T(8,128)S(1)} %collective-permute-done.refs_1_), custom_call_target="tpu_custom_call" | custom-call | tf_op jit(solution)/shard_map/near/pallas_call | solution.py:272
  7.2 2.9 %collective-permute-start.1 = (f32[64,384]{1,0:T(8,128)S(1)}, f32[64,384]{1,0:T(8,128)S(1)}, u32[]{:S(2)}, u32[]{:S(2)}) collective-permute-start(f32[64,384]{1,0:T(8,128)S(1)} %get-tuple-element.19), channel_id=1, source_target_pairs={{0,7},{1,2},{2,1},{3,4},{4,3},{5,6},{6,5},{7,0},{8,15},{9,10},{10,... | collective-permute-start | bytes 294920 | tf_op jit(solution)/shard_map/ppermute | solution.py:275
  10.2 0.0 collective-permute-done.2.refs_0_
  10.2 0.3 %rest_odd.1.found_ref = f32[1,192,256]{2,1,0:T(8,128)S(1)} custom-call(f32[64,384]{1,0:T(8,128)S(1)} %get-tuple-element.18.near_ref.earlier_ref, bf16[4,192,256]{2,1,0:T(8,128)(2,1)S(1)} %get-tuple-element.16.hi_ref, bf16[4,192,256]{2,1,0:T(8,128)(2,1)S(1)} %get-tuple-element.17.lo_ref, f32[264,128]{1,0:T(8,128)S(1)} %collective-permute-done.2.refs_0_), custom_call_target="tpu_custom_call" | custom-call | tf_op jit(solution)/shard_map/rest_odd/pallas_call | solution.py:264
  10.5 0.0 collective-permute-done.3.last_ref
  10.5 0.5 %join_odd.1 = (f32[64,384]{1,0:T(8,128)S(1)}, f32[64,384]{1,0:T(8,128)S(1)}, f32[64,384]{1,0:T(8,128)S(1)}) custom-call(bf16[4,192,256]{2,1,0:T(8,128)(2,1)S(1)} %get-tuple-element.16.hi_ref, bf16[4,192,256]{2,1,0:T(8,128)(2,1)S(1)} %get-tuple-element.17.lo_ref, f32[1,192,256]{2,1,0:T(8,128)S(1)} %rest_odd.1.found_ref, ...), custom_call_target="tpu_custom_call" | custom-call | tf_op jit(solution)/shard_map/join_odd/pallas_call | solution.py:270
  11.0 2.3 %collective-permute-start.5 = (f32[64,384]{1,0:T(8,128)S(1)}, f32[64,384]{1,0:T(8,128)S(1)}, u32[]{:S(2)}, u32[]{:S(2)}) collective-permute-start(f32[64,384]{1,0:T(8,128)S(1)} %get-tuple-element.24), channel_id=1, source_target_pairs={{0,1},{1,2},{2,3},{3,4},{4,5},{5,6},{6,7},{7,0},{8,9},{9,10},{10,1... | collective-permute-start | bytes 294920 | tf_op jit(solution)/shard_map/ppermute | solution.py:278
  13.3 0.0 collective-permute-done.4.last_ref
  13.3 0.3 %collective-permute-start.6 = (f32[64,384]{1,0:T(8,128)S(1)}, f32[64,384]{1,0:T(8,128)S(1)}, u32[]{:S(2)}, u32[]{:S(2)}) collective-permute-start(f32[64,384]{1,0:T(8,128)S(1)} %get-tuple-element.25), channel_id=1, source_target_pairs={{1,0},{2,1},{3,2},{4,3},{5,4},{6,5},{7,6},{0,7},{9,8},{10,9},{11,1... | collective-permute-start | bytes 294920 | tf_op jit(solution)/shard_map/ppermute | solution.py:281
  13.6 0.8 %collective-permute-start.7 = (f32[64,384]{1,0:T(8,128)S(1)}, f32[64,384]{1,0:T(8,128)S(1)}, u32[]{:S(2)}, u32[]{:S(2)}) collective-permute-start(f32[64,384]{1,0:T(8,128)S(1)} %get-tuple-element.26), channel_id=1, source_target_pairs={{0,1},{1,0},{2,3},{3,2},{4,5},{5,4},{6,7},{7,6},{8,9},{9,8},{10,11... | collective-permute-start | bytes 294920 | tf_op jit(solution)/shard_map/ppermute | solution.py:282
  14.4 0.0 collective-permute-done.1.far_ref
  14.4 0.5 %collective-permute-done.5.up_ref = f32[64,384]{1,0:T(8,128)S(1)} collective-permute-done((f32[64,384]{1,0:T(8,128)S(1)}, f32[64,384]{1,0:T(8,128)S(1)}, u32[]{:S(2)}, u32[]{:S(2)}) %collective-permute-start.5) | collective-permute-done | bytes 98336 | tf_op jit(solution)/shard_map/ppermute | solution.py:278
  15.0 2.4 %collective-permute-done.6.down_ref = f32[64,384]{1,0:T(8,128)S(1)} collective-permute-done((f32[64,384]{1,0:T(8,128)S(1)}, f32[64,384]{1,0:T(8,128)S(1)}, u32[]{:S(2)}, u32[]{:S(2)}) %collective-permute-start.6) | collective-permute-done | bytes 98336 | tf_op jit(solution)/shard_map/ppermute | solution.py:281
  17.4 0.0 collective-permute-done.7.chip_ref
  17.4 0.8 %late.1 = f32[64,1280]{1,0:T(8,128)} custom-call(f32[64,1280]{1,0:T(8,128)S(1)} %early.1.early_ref, f32[64,384]{1,0:T(8,128)S(1)} %collective-permute-done.6.down_ref, f32[64,384]{1,0:T(8,128)S(1)} %collective-permute-done.7.chip_ref), custom_call_target="tpu_custom_call" | custom-call | tf_op jit(solution)/shard_map/late/pallas_call | solution.py:289
  (5 shorter events, 0.1 us)
Async XLA Ops:
  0.0 0.9 %copy-start = (f32[4,64,128]{2,1,0:T(8,128)S(1)}, f32[4,64,128]{2,1,0:T(8,128)}, u32[]{:S(2)}) copy-start(f32[4,64,128]{2,1,0:T(8,128)} %param.8) | copy-start | bytes 393220
  0.0 0.9 %copy-start.1 = (s32[4,2]{0,1:T(2,128)S(1)}, s32[4,2]{0,1:T(2,128)}, u32[]{:S(2)}) copy-start(s32[4,2]{0,1:T(2,128)} %param.9) | copy-start | bytes 100
  0.0 5.8 %copy-start.2 = (f32[4,64,256]{2,1,0:T(8,128)S(1)}, f32[4,64,256]{2,1,0:T(8,128)}, u32[]{:S(2)}) copy-start(f32[4,64,256]{2,1,0:T(8,128)} %a_ref.1) | copy-start | bytes 786436
  0.9 4.9 %copy-start.3 = (s32[4,4]{1,0:T(4,128)S(1)}, s32[4,4]{1,0:T(4,128)}, u32[]{:S(2)}) copy-start(s32[4,4]{1,0:T(4,128)} %group_ref.1) | copy-start | bytes 196
  0.9 4.9 %copy-start.4 = (s32[4,4]{1,0:T(4,128)S(1)}, s32[4,4]{1,0:T(4,128)}, u32[]{:S(2)}) copy-start(s32[4,4]{1,0:T(4,128)} %row_ref.1) | copy-start | bytes 196
  1.0 5.7 %collective-permute-start = (f32[264,128]{1,0:T(8,128)S(1)}, f32[264,128]{1,0:T(8,128)S(1)}, u32[]{:S(2)}, u32[]{:S(2)}) collective-permute-start(f32[264,128]{1,0:T(8,128)S(1)} %pack.1.packed_ref.refs_0_), channel_id=1, source_target_pairs={{0,8},{1,9},{2,10},{3,11},{4,12},{5,13},{6,14},{7,15},{8,0},{9,1},... | collective-permute-start | bytes 405512 | tf_op jit(solution)/shard_map/ppermute | solution.py:241
  3.1 7.1 %collective-permute-start.2 = (f32[264,128]{1,0:T(8,128)S(1)}, f32[264,128]{1,0:T(8,128)S(1)}, u32[]{:S(2)}, u32[]{:S(2)}) collective-permute-start(f32[264,128]{1,0:T(8,128)S(1)} %pack.1.packed_ref.refs_0_), channel_id=1, source_target_pairs={{0,16},{1,17},{2,18},{3,19},{4,20},{5,21},{6,22},{7,23},{8,24},{9,... | collective-permute-start | bytes 405512 | tf_op jit(solution)/shard_map/ppermute | solution.py:241
  4.3 6.2 %collective-permute-start.3 = (f32[264,128]{1,0:T(8,128)S(1)}, f32[264,128]{1,0:T(8,128)S(1)}, u32[]{:S(2)}, u32[]{:S(2)}) collective-permute-start(f32[264,128]{1,0:T(8,128)S(1)} %pack.1.packed_ref.refs_0_), channel_id=1, source_target_pairs={{0,2},{1,25},{2,0},{3,27},{4,6},{5,29},{6,4},{7,31},{8,10},{9,17},... | collective-permute-start | bytes 405512 | tf_op jit(solution)/shard_map/ppermute | solution.py:241
  4.4 8.9 %collective-permute-start.4 = (f32[264,128]{1,0:T(8,128)S(1)}, f32[264,128]{1,0:T(8,128)S(1)}, u32[]{:S(2)}, u32[]{:S(2)}) collective-permute-start(f32[264,128]{1,0:T(8,128)S(1)} %pack.1.packed_ref.refs_0_), channel_id=1, source_target_pairs={{0,24},{1,3},{2,26},{3,1},{4,28},{5,7},{6,30},{7,5},{8,16},{9,11},... | collective-permute-start | bytes 405512 | tf_op jit(solution)/shard_map/ppermute | solution.py:241
  7.2 7.2 %collective-permute-start.1 = (f32[64,384]{1,0:T(8,128)S(1)}, f32[64,384]{1,0:T(8,128)S(1)}, u32[]{:S(2)}, u32[]{:S(2)}) collective-permute-start(f32[64,384]{1,0:T(8,128)S(1)} %get-tuple-element.19), channel_id=1, source_target_pairs={{0,7},{1,2},{2,1},{3,4},{4,3},{5,6},{6,5},{7,0},{8,15},{9,10},{10,... | collective-permute-start | bytes 294920 | tf_op jit(solution)/shard_map/ppermute | solution.py:275
  11.0 3.9 %collective-permute-start.5 = (f32[64,384]{1,0:T(8,128)S(1)}, f32[64,384]{1,0:T(8,128)S(1)}, u32[]{:S(2)}, u32[]{:S(2)}) collective-permute-start(f32[64,384]{1,0:T(8,128)S(1)} %get-tuple-element.24), channel_id=1, source_target_pairs={{0,1},{1,2},{2,3},{3,4},{4,5},{5,6},{6,7},{7,0},{8,9},{9,10},{10,1... | collective-permute-start | bytes 294920 | tf_op jit(solution)/shard_map/ppermute | solution.py:278
  13.3 4.1 %collective-permute-start.6 = (f32[64,384]{1,0:T(8,128)S(1)}, f32[64,384]{1,0:T(8,128)S(1)}, u32[]{:S(2)}, u32[]{:S(2)}) collective-permute-start(f32[64,384]{1,0:T(8,128)S(1)} %get-tuple-element.25), channel_id=1, source_target_pairs={{1,0},{2,1},{3,2},{4,3},{5,4},{6,5},{7,6},{0,7},{9,8},{10,9},{11,1... | collective-permute-start | bytes 294920 | tf_op jit(solution)/shard_map/ppermute | solution.py:281
  13.6 3.8 %collective-permute-start.7 = (f32[64,384]{1,0:T(8,128)S(1)}, f32[64,384]{1,0:T(8,128)S(1)}, u32[]{:S(2)}, u32[]{:S(2)}) collective-permute-start(f32[64,384]{1,0:T(8,128)S(1)} %get-tuple-element.26), channel_id=1, source_target_pairs={{0,1},{1,0},{2,3},{3,2},{4,5},{5,4},{6,7},{7,6},{8,9},{9,8},{10,11... | collective-permute-start | bytes 294920 | tf_op jit(solution)/shard_map/ppermute | solution.py:282

commit v8 on v7

--- a/solution.py
+++ b/solution.py
@@ -231,12 +231,19 @@
             **more,
         )
 
+    def idle(b, r):
+        if r % 2:
+            return b, r ^ 2
+        if r == 0:
+            return b ^ 1, r
+        return b, r + 2 if r + 2 < bands else 2
+
     def gather(offsets):
         to = []
         for b in range(groups):
             for r in range(bands):
                 offset = offsets[r % 2]
-                other = (b, r ^ 2) if offset is None else (b ^ offset, r)
+                other = idle(b, r) if offset is None else (b ^ offset, r)
                 to.append((b * bands + r, other[0] * bands + other[1]))
         return lax.ppermute(packed, ("blk", "band"), to)
 

time: 18.3 us -> 18.2 us (level)
    ppermute x1, starting transfers between devices: 0.29 us -> 0.87 us  [body(): lax.ppermute(down, 'band', [((i + 1) % bands, i) for i in range(bands)])]
    ppermute x1, starting transfers between devices: 2.27 us -> 1.72 us  [body(): up = lax.ppermute(up, 'band', [(i, (i + 1) % bands) for i in range(bands)])]
    ppermute x1, waiting for transfers between devices: 0.46 us -> 0.01 us  [body(): up = lax.ppermute(up, 'band', [(i, (i + 1) % bands) for i in range(bands)])]
    ppermute x1, waiting for transfers between devices: 2.43 us -> 2.78 us  [body(): lax.ppermute(down, 'band', [((i + 1) % bands, i) for i in range(bands)])]
  transfers between devices with their start and end apart: 8 -> 8, of which waited for: 2 -> 1; matrix products, arithmetic and copies ran while one was open for 0% -> 0% of each run, Pallas kernels for 12% -> 13%
where the time goes in v8:
time: 18.2 us; the launch traced here: 18.1 us
  starting transfers between devices  11.1 us (61%)
  Pallas kernels  3.14 us (17%)
  waiting for transfers between devices  2.8 us (15%)
  local copies, waits for them, and re-layouts  0.89 us (5%)
    ppermute x4, starting transfers between devices, gather(): return lax.ppermute(packed, ('blk', 'band'), to)  4.84 us
    ppermute x1, starting transfers between devices, body(): lax.ppermute(far, 'band', [(i, (i + 1 if i % 2 else i - 1) % bands) for i...  3.03 us
    ppermute x1, waiting for transfers between devices, body(): lax.ppermute(down, 'band', [((i + 1) % bands, i) for i in range(bands)])  2.78 us
    ppermute x1, starting transfers between devices, body(): up = lax.ppermute(up, 'band', [(i, (i + 1) % bands) for i in range(bands)])  1.72 us
    unnamed x10, local copies, waits for them, and re-layouts  0.89 us
    ppermute x1, starting transfers between devices, body(): lax.ppermute(down, 'band', [((i + 1) % bands, i) for i in range(bands)])  0.87 us
    pallas_call x1, Pallas kernels, body(): pl.pallas_call(functools.partial(left_kernel, width), out_shape=[jax.Shap...  0.81 us
    pallas_call x1, Pallas kernels, body(): call(functools.partial(late_kernel, groups), 'late', whole, inputs=3)  0.78 us
  transfers between devices with their start and end apart: 8, of which 1 were waited for; matrix products, arithmetic and copies ran while one was open for 0% of the time, Pallas kernels for 13%

profile of v8, /device:TPU:1, one launch (start us, length us, event | category | flops | bytes accessed | tf_op | source)
XLA Modules:
  0.0 18.1 jit_solution(2624696853956761098)
XLA Ops:
  0.0 0.0 copy-start
  0.0 0.0 copy-start.1
  0.0 0.0 copy-start.2
  0.0 0.9 %copy-done = f32[4,64,128]{2,1,0:T(8,128)S(1)} copy-done((f32[4,64,128]{2,1,0:T(8,128)S(1)}, f32[4,64,128]{2,1,0:T(8,128)}, u32[]{:S(2)}) %copy-start) | copy-done | bytes 131096
  0.9 0.0 copy-done.1
  0.9 0.0 copy-start.3
  0.9 0.1 pack.1.packed_ref.refs_0_
  1.0 2.1 %collective-permute-start = (f32[264,128]{1,0:T(8,128)S(1)}, f32[264,128]{1,0:T(8,128)S(1)}, u32[]{:S(2)}, u32[]{:S(2)}) collective-permute-start(f32[264,128]{1,0:T(8,128)S(1)} %pack.1.packed_ref.refs_0_), channel_id=1, source_target_pairs={{0,8},{1,9},{2,10},{3,11},{4,12},{5,13},{6,14},{7,15},{8,0},{9,1},... | collective-permute-start | bytes 405512 | tf_op jit(solution)/shard_map/ppermute | solution.py:248
  3.1 1.2 %collective-permute-start.2 = (f32[264,128]{1,0:T(8,128)S(1)}, f32[264,128]{1,0:T(8,128)S(1)}, u32[]{:S(2)}, u32[]{:S(2)}) collective-permute-start(f32[264,128]{1,0:T(8,128)S(1)} %pack.1.packed_ref.refs_0_), channel_id=1, source_target_pairs={{0,16},{1,17},{2,18},{3,19},{4,20},{5,21},{6,22},{7,23},{8,24},{9,... | collective-permute-start | bytes 405512 | tf_op jit(solution)/shard_map/ppermute | solution.py:248
  4.3 0.0 collective-permute-start.3
  4.4 1.5 %collective-permute-start.4 = (f32[264,128]{1,0:T(8,128)S(1)}, f32[264,128]{1,0:T(8,128)S(1)}, u32[]{:S(2)}, u32[]{:S(2)}) collective-permute-start(f32[264,128]{1,0:T(8,128)S(1)} %pack.1.packed_ref.refs_0_), channel_id=1, source_target_pairs={{0,24},{1,3},{2,26},{3,1},{4,28},{5,7},{6,30},{7,5},{8,16},{9,11},... | collective-permute-start | bytes 405512 | tf_op jit(solution)/shard_map/ppermute | solution.py:248
  5.8 0.0 copy-done.2
  5.8 0.0 copy-done.3
  5.8 0.0 copy-done.4
  5.8 0.8 %left.1 = (bf16[4,192,256]{2,1,0:T(8,128)(2,1)S(1)}, bf16[4,192,256]{2,1,0:T(8,128)(2,1)S(1)}) custom-call(s32[4,4]{1,0:T(4,128)S(1)} %copy-done.3, s32[4,4]{1,0:T(4,128)S(1)} %copy-done.4, s32[2,4]{1,0:T(2,128)S(1)} %bitcast.4, f32[4,64,256]{2,1,0:T(8,128)S(1)} %copy-done.2, f32[264,128]{1,0:T(8,128)S(1)} %pack.1.packed_ref.refs_0_), custom_call_target="tpu_custom_call" | custom-call | flops 301989888 | bytes 2000000 | tf_op jit(solution)/shard_map/left/pallas_call | solution.py:255
  6.7 0.0 collective-permute-done.refs_1_
  6.7 0.5 %near.1 = (f32[64,384]{1,0:T(8,128)S(1)}, f32[64,384]{1,0:T(8,128)S(1)}, f32[64,384]{1,0:T(8,128)S(1)}) custom-call(bf16[4,192,256]{2,1,0:T(8,128)(2,1)S(1)} %get-tuple-element.16.hi_ref, bf16[4,192,256]{2,1,0:T(8,128)(2,1)S(1)} %get-tuple-element.17.lo_ref, f32[264,128]{1,0:T(8,128)S(1)} %pack.1.packed_ref.refs_0_, f32[264,128]{1,0:T(8,128)S(1)} %collective-permute-done.refs_1_), custom_call_target="tpu_custom_call" | custom-call | tf_op jit(solution)/shard_map/near/pallas_call | solution.py:279
  7.2 3.0 %collective-permute-start.1 = (f32[64,384]{1,0:T(8,128)S(1)}, f32[64,384]{1,0:T(8,128)S(1)}, u32[]{:S(2)}, u32[]{:S(2)}) collective-permute-start(f32[64,384]{1,0:T(8,128)S(1)} %get-tuple-element.19), channel_id=1, source_target_pairs={{0,7},{1,2},{2,1},{3,4},{4,3},{5,6},{6,5},{7,0},{8,15},{9,10},{10,... | collective-permute-start | bytes 294920 | tf_op jit(solution)/shard_map/ppermute | solution.py:282
  10.3 0.0 collective-permute-done.2.refs_0_
  10.3 0.3 %rest_odd.1.found_ref = f32[1,192,256]{2,1,0:T(8,128)S(1)} custom-call(f32[64,384]{1,0:T(8,128)S(1)} %get-tuple-element.18.near_ref.earlier_ref, bf16[4,192,256]{2,1,0:T(8,128)(2,1)S(1)} %get-tuple-element.16.hi_ref, bf16[4,192,256]{2,1,0:T(8,128)(2,1)S(1)} %get-tuple-element.17.lo_ref, f32[264,128]{1,0:T(8,128)S(1)} %collective-permute-done.2.refs_0_), custom_call_target="tpu_custom_call" | custom-call | tf_op jit(solution)/shard_map/rest_odd/pallas_call | solution.py:271
  10.6 0.0 collective-permute-done.3.last_ref
  10.6 0.5 %join_odd.1 = (f32[64,384]{1,0:T(8,128)S(1)}, f32[64,384]{1,0:T(8,128)S(1)}, f32[64,384]{1,0:T(8,128)S(1)}) custom-call(bf16[4,192,256]{2,1,0:T(8,128)(2,1)S(1)} %get-tuple-element.16.hi_ref, bf16[4,192,256]{2,1,0:T(8,128)(2,1)S(1)} %get-tuple-element.17.lo_ref, f32[1,192,256]{2,1,0:T(8,128)S(1)} %rest_odd.1.found_ref, ...), custom_call_target="tpu_custom_call" | custom-call | tf_op jit(solution)/shard_map/join_odd/pallas_call | solution.py:277
  11.1 1.7 %collective-permute-start.5 = (f32[64,384]{1,0:T(8,128)S(1)}, f32[64,384]{1,0:T(8,128)S(1)}, u32[]{:S(2)}, u32[]{:S(2)}) collective-permute-start(f32[64,384]{1,0:T(8,128)S(1)} %get-tuple-element.24), channel_id=1, source_target_pairs={{0,1},{1,2},{2,3},{3,4},{4,5},{5,6},{6,7},{7,0},{8,9},{9,10},{10,1... | collective-permute-start | bytes 294920 | tf_op jit(solution)/shard_map/ppermute | solution.py:285
  12.8 0.0 collective-permute-done.4.last_ref
  12.8 0.9 %collective-permute-start.6 = (f32[64,384]{1,0:T(8,128)S(1)}, f32[64,384]{1,0:T(8,128)S(1)}, u32[]{:S(2)}, u32[]{:S(2)}) collective-permute-start(f32[64,384]{1,0:T(8,128)S(1)} %get-tuple-element.25), channel_id=1, source_target_pairs={{1,0},{2,1},{3,2},{4,3},{5,4},{6,5},{7,6},{0,7},{9,8},{10,9},{11,1... | collective-permute-start | bytes 294920 | tf_op jit(solution)/shard_map/ppermute | solution.py:288
  13.7 0.7 %collective-permute-start.7 = (f32[64,384]{1,0:T(8,128)S(1)}, f32[64,384]{1,0:T(8,128)S(1)}, u32[]{:S(2)}, u32[]{:S(2)}) collective-permute-start(f32[64,384]{1,0:T(8,128)S(1)} %get-tuple-element.26), channel_id=1, source_target_pairs={{0,1},{1,0},{2,3},{3,2},{4,5},{5,4},{6,7},{7,6},{8,9},{9,8},{10,11... | collective-permute-start | bytes 294920 | tf_op jit(solution)/shard_map/ppermute | solution.py:289
  14.4 0.0 collective-permute-done.1.far_ref
  14.4 0.0 collective-permute-done.5.up_ref
  14.5 0.1 early.1.early_ref
  14.5 2.8 %collective-permute-done.6.down_ref = f32[64,384]{1,0:T(8,128)S(1)} collective-permute-done((f32[64,384]{1,0:T(8,128)S(1)}, f32[64,384]{1,0:T(8,128)S(1)}, u32[]{:S(2)}, u32[]{:S(2)}) %collective-permute-start.6) | collective-permute-done | bytes 98336 | tf_op jit(solution)/shard_map/ppermute | solution.py:288
  17.3 0.0 collective-permute-done.7.chip_ref
  17.3 0.8 %late.1 = f32[64,1280]{1,0:T(8,128)} custom-call(f32[64,1280]{1,0:T(8,128)S(1)} %early.1.early_ref, f32[64,384]{1,0:T(8,128)S(1)} %collective-permute-done.6.down_ref, f32[64,384]{1,0:T(8,128)S(1)} %collective-permute-done.7.chip_ref), custom_call_target="tpu_custom_call" | custom-call | tf_op jit(solution)/shard_map/late/pallas_call | solution.py:296
  (5 shorter events, 0.1 us)
Async XLA Ops:
  0.0 0.9 %copy-start = (f32[4,64,128]{2,1,0:T(8,128)S(1)}, f32[4,64,128]{2,1,0:T(8,128)}, u32[]{:S(2)}) copy-start(f32[4,64,128]{2,1,0:T(8,128)} %param.8) | copy-start | bytes 393220
  0.0 0.9 %copy-start.1 = (s32[4,2]{0,1:T(2,128)S(1)}, s32[4,2]{0,1:T(2,128)}, u32[]{:S(2)}) copy-start(s32[4,2]{0,1:T(2,128)} %param.9) | copy-start | bytes 100
  0.0 5.8 %copy-start.2 = (f32[4,64,256]{2,1,0:T(8,128)S(1)}, f32[4,64,256]{2,1,0:T(8,128)}, u32[]{:S(2)}) copy-start(f32[4,64,256]{2,1,0:T(8,128)} %a_ref.1) | copy-start | bytes 786436
  0.9 4.9 %copy-start.3 = (s32[4,4]{1,0:T(4,128)S(1)}, s32[4,4]{1,0:T(4,128)}, u32[]{:S(2)}) copy-start(s32[4,4]{1,0:T(4,128)} %group_ref.1) | copy-start | bytes 196
  0.9 4.9 %copy-start.4 = (s32[4,4]{1,0:T(4,128)S(1)}, s32[4,4]{1,0:T(4,128)}, u32[]{:S(2)}) copy-start(s32[4,4]{1,0:T(4,128)} %row_ref.1) | copy-start | bytes 196
  1.0 5.7 %collective-permute-start = (f32[264,128]{1,0:T(8,128)S(1)}, f32[264,128]{1,0:T(8,128)S(1)}, u32[]{:S(2)}, u32[]{:S(2)}) collective-permute-start(f32[264,128]{1,0:T(8,128)S(1)} %pack.1.packed_ref.refs_0_), channel_id=1, source_target_pairs={{0,8},{1,9},{2,10},{3,11},{4,12},{5,13},{6,14},{7,15},{8,0},{9,1},... | collective-permute-start | bytes 405512 | tf_op jit(solution)/shard_map/ppermute | solution.py:248
  3.1 7.2 %collective-permute-start.2 = (f32[264,128]{1,0:T(8,128)S(1)}, f32[264,128]{1,0:T(8,128)S(1)}, u32[]{:S(2)}, u32[]{:S(2)}) collective-permute-start(f32[264,128]{1,0:T(8,128)S(1)} %pack.1.packed_ref.refs_0_), channel_id=1, source_target_pairs={{0,16},{1,17},{2,18},{3,19},{4,20},{5,21},{6,22},{7,23},{8,24},{9,... | collective-permute-start | bytes 405512 | tf_op jit(solution)/shard_map/ppermute | solution.py:248
  4.3 6.3 %collective-permute-start.3 = (f32[264,128]{1,0:T(8,128)S(1)}, f32[264,128]{1,0:T(8,128)S(1)}, u32[]{:S(2)}, u32[]{:S(2)}) collective-permute-start(f32[264,128]{1,0:T(8,128)S(1)} %pack.1.packed_ref.refs_0_), channel_id=1, source_target_pairs={{0,8},{1,25},{2,4},{3,27},{4,6},{5,29},{6,2},{7,31},{8,0},{9,17},{... | collective-permute-start | bytes 405512 | tf_op jit(solution)/shard_map/ppermute | solution.py:248
  4.4 8.5 %collective-permute-start.4 = (f32[264,128]{1,0:T(8,128)S(1)}, f32[264,128]{1,0:T(8,128)S(1)}, u32[]{:S(2)}, u32[]{:S(2)}) collective-permute-start(f32[264,128]{1,0:T(8,128)S(1)} %pack.1.packed_ref.refs_0_), channel_id=1, source_target_pairs={{0,24},{1,3},{2,26},{3,1},{4,28},{5,7},{6,30},{7,5},{8,16},{9,11},... | collective-permute-start | bytes 405512 | tf_op jit(solution)/shard_map/ppermute | solution.py:248
  7.2 7.2 %collective-permute-start.1 = (f32[64,384]{1,0:T(8,128)S(1)}, f32[64,384]{1,0:T(8,128)S(1)}, u32[]{:S(2)}, u32[]{:S(2)}) collective-permute-start(f32[64,384]{1,0:T(8,128)S(1)} %get-tuple-element.19), channel_id=1, source_target_pairs={{0,7},{1,2},{2,1},{3,4},{4,3},{5,6},{6,5},{7,0},{8,15},{9,10},{10,... | collective-permute-start | bytes 294920 | tf_op jit(solution)/shard_map/ppermute | solution.py:282
  11.1 3.4 %collective-permute-start.5 = (f32[64,384]{1,0:T(8,128)S(1)}, f32[64,384]{1,0:T(8,128)S(1)}, u32[]{:S(2)}, u32[]{:S(2)}) collective-permute-start(f32[64,384]{1,0:T(8,128)S(1)} %get-tuple-element.24), channel_id=1, source_target_pairs={{0,1},{1,2},{2,3},{3,4},{4,5},{5,6},{6,7},{7,0},{8,9},{9,10},{10,1... | collective-permute-start | bytes 294920 | tf_op jit(solution)/shard_map/ppermute | solution.py:285
  12.8 4.5 %collective-permute-start.6 = (f32[64,384]{1,0:T(8,128)S(1)}, f32[64,384]{1,0:T(8,128)S(1)}, u32[]{:S(2)}, u32[]{:S(2)}) collective-permute-start(f32[64,384]{1,0:T(8,128)S(1)} %get-tuple-element.25), channel_id=1, source_target_pairs={{1,0},{2,1},{3,2},{4,3},{5,4},{6,5},{7,6},{0,7},{9,8},{10,9},{11,1... | collective-permute-start | bytes 294920 | tf_op jit(solution)/shard_map/ppermute | solution.py:288
  13.7 3.6 %collective-permute-start.7 = (f32[64,384]{1,0:T(8,128)S(1)}, f32[64,384]{1,0:T(8,128)S(1)}, u32[]{:S(2)}, u32[]{:S(2)}) collective-permute-start(f32[64,384]{1,0:T(8,128)S(1)} %get-tuple-element.26), channel_id=1, source_target_pairs={{0,1},{1,0},{2,3},{3,2},{4,5},{5,4},{6,7},{7,6},{8,9},{9,8},{10,11... | collective-permute-start | bytes 294920 | tf_op jit(solution)/shard_map/ppermute | solution.py:289

commit v9 on v8

--- a/solution.py
+++ b/solution.py
@@ -104,9 +104,9 @@
     return jnp.concatenate([jnp.concatenate(near, axis=0), jnp.concatenate(far, axis=0)], axis=1)
 
 
-def multiply(hi_ref, lo_ref, slot, src, width):
+def multiply(hi_ref, lo_ref, slot, src, width, at=slice(None)):
     rows = hi_ref.shape[2] // width
-    return dot3(hi_ref[slot], lo_ref[slot], *split(spread(src, rows, width)))
+    return dot3(hi_ref[slot, at, :], lo_ref[slot, at, :], *split(spread(src, rows, width)))
 
 
 def lay_out(found, outs, width):
@@ -143,22 +143,30 @@
             out_ref[j] = multiply(hi_ref, lo_ref, first + j, src, width)
 
 
-def join_kernel(width, turn, hi_ref, lo_ref, found_ref, last_ref, *refs):
-    handed, outs = refs[:-3], refs[-3:]
+def finish(width, at, hi_ref, lo_ref, found_ref, last_ref, outs):
+    found = [found_ref[j, at, :] for j in range(found_ref.shape[0])]
+    found.append(multiply(hi_ref, lo_ref, hi_ref.shape[0] - 1, last_ref, width, at))
+    lay_out(found, outs, width)
+
+
+def far_kernel(width, turn, hi_ref, lo_ref, found_ref, last_ref, given_ref, out_ref):
     mine = lax.axis_index("band") % 2 == turn
 
     @pl.when(mine)
     def _():
-        found = [found_ref[j] for j in range(found_ref.shape[0])]
-        found.append(multiply(hi_ref, lo_ref, hi_ref.shape[0] - 1, last_ref, width))
-        lay_out(found, outs, width)
+        finish(width, slice(2 * width, 3 * width), hi_ref, lo_ref, found_ref, last_ref, [out_ref])
 
     @pl.when(jnp.logical_not(mine))
     def _():
-        for out_ref in outs[: 3 - len(handed)]:
-            out_ref[...] = jnp.zeros_like(out_ref)
-        for out_ref, given_ref in zip(outs[3 - len(handed) :], handed):
-            out_ref[...] = given_ref[...]
+        out_ref[...] = given_ref[...]
+
+
+def join_kernel(width, earlier_ref, hi_ref, lo_ref, *refs):
+    outs = refs[-2:]
+    odd = lax.axis_index("band") % 2 == 1
+    at = slice(0, 2 * width)
+    pl.when(odd)(lambda: finish(width, at, hi_ref, lo_ref, refs[0], refs[1], outs))
+    pl.when(jnp.logical_not(odd))(lambda: finish(width, at, hi_ref, lo_ref, refs[2], refs[3], outs))
 
 
 def place(sum_ref, part_ref, groups, first, shift):
@@ -233,7 +241,7 @@
 
     def idle(b, r):
         if r % 2:
-            return b, r ^ 2
+            return b, (r + 2) % bands
         if r == 0:
             return b ^ 1, r
         return b, r + 2 if r + 2 < bands else 2
@@ -272,20 +280,26 @@
 
     parts = [(width, SHIFTS * span * width)] * 3
 
-    def join(name, turn, found, last, *handed):
-        kernel = functools.partial(join_kernel, width, turn)
-        return call(kernel, name, parts, inputs=4 + len(handed))(hi, lo, found, last, *handed)
+    def far_part(name, turn, found, last):
+        kernel = functools.partial(far_kernel, width, turn)
+        return call(kernel, name, parts[0], inputs=5)(hi, lo, found, last, chip_near)
 
     own_near, chip_near, far = call(
         functools.partial(near_kernel, width), "near", parts, inputs=2 + span
     )(hi, lo, *sources)
     far = lax.ppermute(far, "band", [(i, (i + 1 if i % 2 else i - 1) % bands) for i in range(bands)])
-    found = products("rest_odd", 1, rest[: span - 1], own_near)
-    own, chip, up = join("join_odd", 1, found, rest[span - 1], chip_near)
-    up = lax.ppermute(up, "band", [(i, (i + 1) % bands) for i in range(bands)])
-    found = products("rest_even", 0, rest[: span - 1], own)
-    own, chip, down = join("join_even", 0, found, rest[-1], own, chip, chip_near)
-    down = lax.ppermute(down, "band", [((i + 1) % bands, i) for i in range(bands)])
+    odd_found = products("rest_odd", 1, rest[: span - 1], own_near)
+    far_up = far_part("far_odd", 1, odd_found, rest[span - 1])
+    up = lax.ppermute(far_up, "band", [(i, (i + 1) % bands) for i in range(bands)])
+    even_found = products("rest_even", 0, rest[: span - 1], far_up)
+    far_down = far_part("far_even", 0, even_found, rest[-1])
+    down = lax.ppermute(far_down, "band", [((i + 1) % bands, i) for i in range(bands)])
+    own, chip = call(
+        functools.partial(join_kernel, width),
+        "join",
+        parts[:2],
+        in_specs=[pl.BlockSpec(memory_space=pl.ANY)] + [vmem()] * 6,
+    )(far_down, hi, lo, odd_found, rest[span - 1], even_found, rest[-1])
     chip = lax.ppermute(chip, "band", [(i, i ^ 1) for i in range(bands)])
     whole = (width, 5 * groups * width)
     slow = pl.CostEstimate(flops=4000000000, bytes_accessed=2000000, transcendentals=0)

time: 18.2 us -> 18.2 us (level)
  waiting for transfers between devices: 2.8 us -> 2.36 us
  Pallas kernels: 3.14 us -> 3.47 us
  starting transfers between devices: 11.1 us -> 11.3 us
    ppermute x2, waiting for transfers between devices: 2.79 us -> 1.53 us  [the longest x1 1.52 us: body(): lax.ppermute(far_down, 'band', [((i + 1) % bands, i) for i in range(bands)])]
    ppermute x1, waiting for transfers between devices: 0.01 us -> 0.82 us  [body(): chip = lax.ppermute(chip, 'band', [(i, i ^ 1) for i in range(bands)])]
    pallas_call x2 -> x3, Pallas kernels: 0.49 us -> 0.81 us  [the longest x1 0.41 us: body(): call(functools.partial(join_kernel, width), 'join', parts[:2], in_specs=[...]
  transfers between devices with their start and end apart: 8 -> 8, of which waited for: 1 -> 2; matrix products, arithmetic and copies ran while one was open for 0% -> 0% of each run, Pallas kernels for 13% -> 14%
where the time goes in v9:
time: 18.2 us; the launch traced here: 18.1 us
  starting transfers between devices  11.3 us (62%)
  Pallas kernels  3.47 us (19%)
  waiting for transfers between devices  2.36 us (13%)
  local copies, waits for them, and re-layouts  0.89 us (5%)
    ppermute x4, starting transfers between devices, gather(): return lax.ppermute(packed, ('blk', 'band'), to)  4.84 us
    ppermute x1, starting transfers between devices, body(): lax.ppermute(far, 'band', [(i, (i + 1 if i % 2 else i - 1) % bands) for i...  3.04 us
    ppermute x1, starting transfers between devices, body(): lax.ppermute(far_up, 'band', [(i, (i + 1) % bands) for i in range(bands)])  1.71 us
    ppermute x1, waiting for transfers between devices, body(): lax.ppermute(far_down, 'band', [((i + 1) % bands, i) for i in range(bands)])  1.52 us
    unnamed x10, local copies, waits for them, and re-layouts  0.89 us
    ppermute x1, starting transfers between devices, body(): lax.ppermute(far_down, 'band', [((i + 1) % bands, i) for i in range(bands)])  0.88 us
    ppermute x1, waiting for transfers between devices, body(): chip = lax.ppermute(chip, 'band', [(i, i ^ 1) for i in range(bands)])  0.82 us
    pallas_call x1, Pallas kernels, body(): pl.pallas_call(functools.partial(left_kernel, width), out_shape=[jax.Shap...  0.81 us
  transfers between devices with their start and end apart: 8, of which 2 were waited for; matrix products, arithmetic and copies ran while one was open for 0% of the time, Pallas kernels for 14%

profile of v9, /device:TPU:1, one launch (start us, length us, event | category | flops | bytes accessed | tf_op | source)
XLA Modules:
  0.0 18.1 jit_solution(1044211822442703353)
XLA Ops:
  0.0 0.0 copy-start
  0.0 0.0 copy-start.1
  0.0 0.0 copy-start.2
  0.0 0.9 %copy-done = f32[4,64,128]{2,1,0:T(8,128)S(1)} copy-done((f32[4,64,128]{2,1,0:T(8,128)S(1)}, f32[4,64,128]{2,1,0:T(8,128)}, u32[]{:S(2)}) %copy-start) | copy-done | bytes 131096
  0.9 0.0 copy-done.1
  0.9 0.1 pack.1.packed_ref.refs_0_
  1.0 2.1 %collective-permute-start = (f32[264,128]{1,0:T(8,128)S(1)}, f32[264,128]{1,0:T(8,128)S(1)}, u32[]{:S(2)}, u32[]{:S(2)}) collective-permute-start(f32[264,128]{1,0:T(8,128)S(1)} %pack.1.packed_ref.refs_0_), channel_id=1, source_target_pairs={{0,8},{1,9},{2,10},{3,11},{4,12},{5,13},{6,14},{7,15},{8,0},{9,1},... | collective-permute-start | bytes 405512 | tf_op jit(solution)/shard_map/ppermute | solution.py:256
  3.1 1.2 %collective-permute-start.2 = (f32[264,128]{1,0:T(8,128)S(1)}, f32[264,128]{1,0:T(8,128)S(1)}, u32[]{:S(2)}, u32[]{:S(2)}) collective-permute-start(f32[264,128]{1,0:T(8,128)S(1)} %pack.1.packed_ref.refs_0_), channel_id=1, source_target_pairs={{0,16},{1,17},{2,18},{3,19},{4,20},{5,21},{6,22},{7,23},{8,24},{9,... | collective-permute-start | bytes 405512 | tf_op jit(solution)/shard_map/ppermute | solution.py:256
  4.3 0.0 collective-permute-start.3
  4.4 1.5 %collective-permute-start.4 = (f32[264,128]{1,0:T(8,128)S(1)}, f32[264,128]{1,0:T(8,128)S(1)}, u32[]{:S(2)}, u32[]{:S(2)}) collective-permute-start(f32[264,128]{1,0:T(8,128)S(1)} %pack.1.packed_ref.refs_0_), channel_id=1, source_target_pairs={{0,24},{1,3},{2,26},{3,5},{4,28},{5,7},{6,30},{7,1},{8,16},{9,11},... | collective-permute-start | bytes 405512 | tf_op jit(solution)/shard_map/ppermute | solution.py:256
  5.8 0.0 copy-done.2
  5.8 0.0 copy-done.3
  5.8 0.0 copy-done.4
  5.8 0.8 %left.1 = (bf16[4,192,256]{2,1,0:T(8,128)(2,1)S(1)}, bf16[4,192,256]{2,1,0:T(8,128)(2,1)S(1)}) custom-call(s32[4,4]{1,0:T(4,128)S(1)} %copy-done.3, s32[4,4]{1,0:T(4,128)S(1)} %copy-done.4, s32[2,4]{1,0:T(2,128)S(1)} %bitcast.4, f32[4,64,256]{2,1,0:T(8,128)S(1)} %copy-done.2, f32[264,128]{1,0:T(8,128)S(1)} %pack.1.packed_ref.refs_0_), custom_call_target="tpu_custom_call" | custom-call | flops 301989888 | bytes 2000000 | tf_op jit(solution)/shard_map/left/pallas_call | solution.py:263
  6.7 0.0 collective-permute-done.refs_1_
  6.7 0.5 %near.1 = (f32[64,384]{1,0:T(8,128)S(1)}, f32[64,384]{1,0:T(8,128)S(1)}, f32[64,384]{1,0:T(8,128)S(1)}) custom-call(bf16[4,192,256]{2,1,0:T(8,128)(2,1)S(1)} %get-tuple-element.12.hi_ref, bf16[4,192,256]{2,1,0:T(8,128)(2,1)S(1)} %get-tuple-element.13.lo_ref, f32[264,128]{1,0:T(8,128)S(1)} %pack.1.packed_ref.refs_0_, f32[264,128]{1,0:T(8,128)S(1)} %collective-permute-done.refs_1_), custom_call_target="tpu_custom_call" | custom-call | tf_op jit(solution)/shard_map/near/pallas_call | solution.py:287
  7.2 3.0 %collective-permute-start.1 = (f32[64,384]{1,0:T(8,128)S(1)}, f32[64,384]{1,0:T(8,128)S(1)}, u32[]{:S(2)}, u32[]{:S(2)}) collective-permute-start(f32[64,384]{1,0:T(8,128)S(1)} %get-tuple-element.15), channel_id=1, source_target_pairs={{0,7},{1,2},{2,1},{3,4},{4,3},{5,6},{6,5},{7,0},{8,15},{9,10},{10,... | collective-permute-start | bytes 294920 | tf_op jit(solution)/shard_map/ppermute | solution.py:290
  10.3 0.0 collective-permute-done.2.refs_0_
  10.3 0.3 %rest_odd.1.found_ref.refs_0_ = f32[1,192,256]{2,1,0:T(8,128)S(1)} custom-call(f32[64,384]{1,0:T(8,128)S(1)} %get-tuple-element.14.near_ref.earlier_ref, bf16[4,192,256]{2,1,0:T(8,128)(2,1)S(1)} %get-tuple-element.12.hi_ref, bf16[4,192,256]{2,1,0:T(8,128)(2,1)S(1)} %get-tuple-element.13.lo_ref, f32[264,128]{1,0:T(8,128)S(1)} %collective-permute-done.2.refs_0_), custom_call_target="tpu_custom_call" | custom-call | tf_op jit(solution)/shard_map/rest_odd/pallas_call | solution.py:279
  10.6 0.0 collective-permute-done.3.last_ref.refs_1_
  10.6 0.4 %far_odd.1.earlier_ref = f32[64,384]{1,0:T(8,128)S(1)} custom-call(bf16[4,192,256]{2,1,0:T(8,128)(2,1)S(1)} %get-tuple-element.12.hi_ref, bf16[4,192,256]{2,1,0:T(8,128)(2,1)S(1)} %get-tuple-element.13.lo_ref, f32[1,192,256]{2,1,0:T(8,128)S(1)} %rest_odd.1.found_ref.refs_0_, f32[264,128]{1,0:T(8,128)S(1)} %collective-permute-done.3.last_ref.refs_1_, ...), custom_call_target="tpu_custom_call" | custom-call | tf_op jit(solution)/shard_map/far_odd/pallas_call | solution.py:285
  11.0 1.7 %collective-permute-start.5 = (f32[64,384]{1,0:T(8,128)S(1)}, f32[64,384]{1,0:T(8,128)S(1)}, u32[]{:S(2)}, u32[]{:S(2)}) collective-permute-start(f32[64,384]{1,0:T(8,128)S(1)} %far_odd.1.earlier_ref), channel_id=1, source_target_pairs={{0,1},{1,2},{2,3},{3,4},{4,5},{5,6},{6,7},{7,0},{8,9},{9,10},{10,1... | collective-permute-start | bytes 294920 | tf_op jit(solution)/shard_map/ppermute | solution.py:293
  12.7 0.0 collective-permute-done.4.last_ref.refs_3_
  12.7 0.9 %collective-permute-start.6 = (f32[64,384]{1,0:T(8,128)S(1)}, f32[64,384]{1,0:T(8,128)S(1)}, u32[]{:S(2)}, u32[]{:S(2)}) collective-permute-start(f32[64,384]{1,0:T(8,128)S(1)} %far_even.1.earlier_ref), channel_id=1, source_target_pairs={{1,0},{2,1},{3,2},{4,3},{5,4},{6,5},{7,6},{0,7},{9,8},{10,9},{11,1... | collective-permute-start | bytes 294920 | tf_op jit(solution)/shard_map/ppermute | solution.py:296
  13.6 0.4 %join.1 = (f32[64,384]{1,0:T(8,128)S(1)}, f32[64,384]{1,0:T(8,128)S(1)}) custom-call(f32[64,384]{1,0:T(8,128)S(1)} %far_even.1.earlier_ref, bf16[4,192,256]{2,1,0:T(8,128)(2,1)S(1)} %get-tuple-element.12.hi_ref, bf16[4,192,256]{2,1,0:T(8,128)(2,1)S(1)} %get-tuple-element.13.lo_ref, f32[1,192,256]{2,1,0:T(8,128)S(1)} %rest_odd.1.found_ref.refs_0_, ...), custom_call_target="tpu_custom_call" | custom-call | tf_op jit(solution)/shard_map/join/pallas_call | solution.py:297
  14.0 0.8 %collective-permute-start.7 = (f32[64,384]{1,0:T(8,128)S(1)}, f32[64,384]{1,0:T(8,128)S(1)}, u32[]{:S(2)}, u32[]{:S(2)}) collective-permute-start(f32[64,384]{1,0:T(8,128)S(1)} %get-tuple-element.18), channel_id=1, source_target_pairs={{0,1},{1,0},{2,3},{3,2},{4,5},{5,4},{6,7},{7,6},{8,9},{9,8},{10,11... | collective-permute-start | bytes 294920 | tf_op jit(solution)/shard_map/ppermute | solution.py:303
  14.8 0.0 collective-permute-done.1.far_ref
  14.9 0.0 collective-permute-done.5.up_ref
  14.9 0.1 early.1.early_ref
  15.0 0.8 %collective-permute-done.7.chip_ref = f32[64,384]{1,0:T(8,128)S(1)} collective-permute-done((f32[64,384]{1,0:T(8,128)S(1)}, f32[64,384]{1,0:T(8,128)S(1)}, u32[]{:S(2)}, u32[]{:S(2)}) %collective-permute-start.7) | collective-permute-done | bytes 98336 | tf_op jit(solution)/shard_map/ppermute | solution.py:303
  15.8 1.5 %collective-permute-done.6.down_ref = f32[64,384]{1,0:T(8,128)S(1)} collective-permute-done((f32[64,384]{1,0:T(8,128)S(1)}, f32[64,384]{1,0:T(8,128)S(1)}, u32[]{:S(2)}, u32[]{:S(2)}) %collective-permute-start.6) | collective-permute-done | bytes 98336 | tf_op jit(solution)/shard_map/ppermute | solution.py:296
  17.3 0.8 %late.1 = f32[64,1280]{1,0:T(8,128)} custom-call(f32[64,1280]{1,0:T(8,128)S(1)} %early.1.early_ref, f32[64,384]{1,0:T(8,128)S(1)} %collective-permute-done.6.down_ref, f32[64,384]{1,0:T(8,128)S(1)} %collective-permute-done.7.chip_ref), custom_call_target="tpu_custom_call" | custom-call | tf_op jit(solution)/shard_map/late/pallas_call | solution.py:310
  (6 shorter events, 0.1 us)
Async XLA Ops:
  0.0 0.9 %copy-start = (f32[4,64,128]{2,1,0:T(8,128)S(1)}, f32[4,64,128]{2,1,0:T(8,128)}, u32[]{:S(2)}) copy-start(f32[4,64,128]{2,1,0:T(8,128)} %param.8) | copy-start | bytes 393220
  0.0 0.9 %copy-start.1 = (s32[4,2]{0,1:T(2,128)S(1)}, s32[4,2]{0,1:T(2,128)}, u32[]{:S(2)}) copy-start(s32[4,2]{0,1:T(2,128)} %param.9) | copy-start | bytes 100
  0.0 5.8 %copy-start.2 = (f32[4,64,256]{2,1,0:T(8,128)S(1)}, f32[4,64,256]{2,1,0:T(8,128)}, u32[]{:S(2)}) copy-start(f32[4,64,256]{2,1,0:T(8,128)} %a_ref.1) | copy-start | bytes 786436
  0.9 4.9 %copy-start.3 = (s32[4,4]{1,0:T(4,128)S(1)}, s32[4,4]{1,0:T(4,128)}, u32[]{:S(2)}) copy-start(s32[4,4]{1,0:T(4,128)} %group_ref.1) | copy-start | bytes 196
  0.9 4.9 %copy-start.4 = (s32[4,4]{1,0:T(4,128)S(1)}, s32[4,4]{1,0:T(4,128)}, u32[]{:S(2)}) copy-start(s32[4,4]{1,0:T(4,128)} %row_ref.1) | copy-start | bytes 196
  1.0 5.7 %collective-permute-start = (f32[264,128]{1,0:T(8,128)S(1)}, f32[264,128]{1,0:T(8,128)S(1)}, u32[]{:S(2)}, u32[]{:S(2)}) collective-permute-start(f32[264,128]{1,0:T(8,128)S(1)} %pack.1.packed_ref.refs_0_), channel_id=1, source_target_pairs={{0,8},{1,9},{2,10},{3,11},{4,12},{5,13},{6,14},{7,15},{8,0},{9,1},... | collective-permute-start | bytes 405512 | tf_op jit(solution)/shard_map/ppermute | solution.py:256
  3.1 7.2 %collective-permute-start.2 = (f32[264,128]{1,0:T(8,128)S(1)}, f32[264,128]{1,0:T(8,128)S(1)}, u32[]{:S(2)}, u32[]{:S(2)}) collective-permute-start(f32[264,128]{1,0:T(8,128)S(1)} %pack.1.packed_ref.refs_0_), channel_id=1, source_target_pairs={{0,16},{1,17},{2,18},{3,19},{4,20},{5,21},{6,22},{7,23},{8,24},{9,... | collective-permute-start | bytes 405512 | tf_op jit(solution)/shard_map/ppermute | solution.py:256
  4.3 6.3 %collective-permute-start.3 = (f32[264,128]{1,0:T(8,128)S(1)}, f32[264,128]{1,0:T(8,128)S(1)}, u32[]{:S(2)}, u32[]{:S(2)}) collective-permute-start(f32[264,128]{1,0:T(8,128)S(1)} %pack.1.packed_ref.refs_0_), channel_id=1, source_target_pairs={{0,8},{1,25},{2,4},{3,27},{4,6},{5,29},{6,2},{7,31},{8,0},{9,17},{... | collective-permute-start | bytes 405512 | tf_op jit(solution)/shard_map/ppermute | solution.py:256
  4.4 8.4 %collective-permute-start.4 = (f32[264,128]{1,0:T(8,128)S(1)}, f32[264,128]{1,0:T(8,128)S(1)}, u32[]{:S(2)}, u32[]{:S(2)}) collective-permute-start(f32[264,128]{1,0:T(8,128)S(1)} %pack.1.packed_ref.refs_0_), channel_id=1, source_target_pairs={{0,24},{1,3},{2,26},{3,5},{4,28},{5,7},{6,30},{7,1},{8,16},{9,11},... | collective-permute-start | bytes 405512 | tf_op jit(solution)/shard_map/ppermute | solution.py:256
  7.2 7.6 %collective-permute-start.1 = (f32[64,384]{1,0:T(8,128)S(1)}, f32[64,384]{1,0:T(8,128)S(1)}, u32[]{:S(2)}, u32[]{:S(2)}) collective-permute-start(f32[64,384]{1,0:T(8,128)S(1)} %get-tuple-element.15), channel_id=1, source_target_pairs={{0,7},{1,2},{2,1},{3,4},{4,3},{5,6},{6,5},{7,0},{8,15},{9,10},{10,... | collective-permute-start | bytes 294920 | tf_op jit(solution)/shard_map/ppermute | solution.py:290
  11.0 3.9 %collective-permute-start.5 = (f32[64,384]{1,0:T(8,128)S(1)}, f32[64,384]{1,0:T(8,128)S(1)}, u32[]{:S(2)}, u32[]{:S(2)}) collective-permute-start(f32[64,384]{1,0:T(8,128)S(1)} %far_odd.1.earlier_ref), channel_id=1, source_target_pairs={{0,1},{1,2},{2,3},{3,4},{4,5},{5,6},{6,7},{7,0},{8,9},{9,10},{10,1... | collective-permute-start | bytes 294920 | tf_op jit(solution)/shard_map/ppermute | solution.py:293
  12.7 4.6 %collective-permute-start.6 = (f32[64,384]{1,0:T(8,128)S(1)}, f32[64,384]{1,0:T(8,128)S(1)}, u32[]{:S(2)}, u32[]{:S(2)}) collective-permute-start(f32[64,384]{1,0:T(8,128)S(1)} %far_even.1.earlier_ref), channel_id=1, source_target_pairs={{1,0},{2,1},{3,2},{4,3},{5,4},{6,5},{7,6},{0,7},{9,8},{10,9},{11,1... | collective-permute-start | bytes 294920 | tf_op jit(solution)/shard_map/ppermute | solution.py:296
  14.0 1.7 %collective-permute-start.7 = (f32[64,384]{1,0:T(8,128)S(1)}, f32[64,384]{1,0:T(8,128)S(1)}, u32[]{:S(2)}, u32[]{:S(2)}) collective-permute-start(f32[64,384]{1,0:T(8,128)S(1)} %get-tuple-element.18), channel_id=1, source_target_pairs={{0,1},{1,0},{2,3},{3,2},{4,5},{5,4},{6,7},{7,6},{8,9},{9,8},{10,11... | collective-permute-start | bytes 294920 | tf_op jit(solution)/shard_map/ppermute | solution.py:303

commit v10 on v9

--- a/solution.py
+++ b/solution.py
@@ -44,7 +44,7 @@
     out_ref[deep:, :] = jnp.concatenate(straight + crossed, axis=0).astype(jnp.float32)
 
 
-def left_kernel(width, group_ref, row_ref, code_ref, a_ref, packed_ref, hi_ref, lo_ref):
+def left_kernel(width, group_ref, row_ref, code_ref, a_ref, packed_ref, hi_ref, lo_ref, far_ref):
     rows, per_row = group_ref.shape
     groups = hi_ref.shape[0]
     me = lax.axis_index("blk")
@@ -86,6 +86,7 @@
             placed.append(x)
         b_hi, b_lo = split(jnp.concatenate(placed, axis=0))
         hi_ref[j], lo_ref[j] = split(dot3(rt_hi, rt_lo, b_hi, b_lo))
+    far_ref[...] = multiply(hi_ref, lo_ref, 0, packed_ref, width, slice(2 * width, 3 * width))
 
 
 def spread(src, rows, width):
@@ -130,8 +131,10 @@
                 out_ref[:, at : at + pair] = jnp.where(right_half, v, u)
 
 
-def near_kernel(width, hi_ref, lo_ref, *refs):
-    lay_out([multiply(hi_ref, lo_ref, j, src, width) for j, src in enumerate(refs[:-3])], refs[-3:], width)
+def near_kernel(width, hi_ref, lo_ref, own_ref, *refs):
+    at = slice(2 * width, 3 * width)
+    found = [multiply(hi_ref, lo_ref, 1 + j, src, width, at) for j, src in enumerate(refs[:-1])]
+    lay_out([own_ref[...]] + found, refs[-1:], width)
 
 
 def product_kernel(width, first, turn, earlier_ref, hi_ref, lo_ref, *refs):
@@ -149,7 +152,7 @@
     lay_out(found, outs, width)
 
 
-def far_kernel(width, turn, hi_ref, lo_ref, found_ref, last_ref, given_ref, out_ref):
+def far_kernel(width, turn, hi_ref, lo_ref, found_ref, last_ref, out_ref):
     mine = lax.axis_index("band") % 2 == turn
 
     @pl.when(mine)
@@ -158,13 +161,16 @@
 
     @pl.when(jnp.logical_not(mine))
     def _():
-        out_ref[...] = given_ref[...]
+        out_ref[...] = jnp.zeros_like(out_ref)
 
 
 def join_kernel(width, earlier_ref, hi_ref, lo_ref, *refs):
-    outs = refs[-2:]
+    sources, (near_ref, rest_ref, chip_ref) = refs[4:-3], refs[-3:]
     odd = lax.axis_index("band") % 2 == 1
     at = slice(0, 2 * width)
+    found = [multiply(hi_ref, lo_ref, j, src, width, at) for j, src in enumerate(sources)]
+    lay_out(found, [near_ref, chip_ref.at[:width]], width)
+    outs = [rest_ref, chip_ref.at[width:]]
     pl.when(odd)(lambda: finish(width, at, hi_ref, lo_ref, refs[0], refs[1], outs))
     pl.when(jnp.logical_not(odd))(lambda: finish(width, at, hi_ref, lo_ref, refs[2], refs[3], outs))
 
@@ -190,15 +196,17 @@
     span = groups // 2
     out_ref[...] = first_ref[...]
     place(out_ref, rest_ref, groups, span, 1)
-    place(out_ref, up_ref, groups, span * (1 - lax.axis_index("band") % 2), 0)
+    place(out_ref, up_ref, groups, span, 0)
 
 
 def late_kernel(groups, early_ref, down_ref, chip_ref, out_ref):
     odd = lax.axis_index("band") % 2
     span = groups // 2
+    height = early_ref.shape[0]
     out_ref[...] = early_ref[...]
-    place(out_ref, chip_ref, groups, span, 2 - 2 * odd)
-    place(out_ref, down_ref, groups, span * odd, 2)
+    place(out_ref, chip_ref.at[:height], groups, 0, 2 - 2 * odd)
+    place(out_ref, chip_ref.at[height:], groups, span, 2 - 2 * odd)
+    place(out_ref, down_ref, groups, span, 2)
 
 
 def body(fine_blocks, source_group, source_row, prolong_blocks, prolong_code):
@@ -260,11 +268,12 @@
     odd_steps = [*range(span, groups)] + [None] * LAG
     even_steps = [*range(span, groups - 1)] + [None] * LAG + [groups - 1]
     rest = [gather(offsets) for offsets in zip(even_steps, odd_steps)]
-    hi, lo = pl.pallas_call(
+    hi, lo, own_far = pl.pallas_call(
         functools.partial(left_kernel, width),
-        out_shape=[jax.ShapeDtypeStruct((groups, height, deep), jnp.bfloat16)] * 2,
+        out_shape=[jax.ShapeDtypeStruct((groups, height, deep), jnp.bfloat16)] * 2
+        + [jax.ShapeDtypeStruct((width, 2 * pair), f32)],
         in_specs=[vmem()] * 5,
-        out_specs=[vmem()] * 2,
+        out_specs=[vmem()] * 3,
         cost_estimate=pl.CostEstimate(
             flops=6 * groups * height * deep * deep, bytes_accessed=2000000, transcendentals=0
         ),
@@ -282,24 +291,24 @@
 
     def far_part(name, turn, found, last):
         kernel = functools.partial(far_kernel, width, turn)
-        return call(kernel, name, parts[0], inputs=5)(hi, lo, found, last, chip_near)
-
-    own_near, chip_near, far = call(
-        functools.partial(near_kernel, width), "near", parts, inputs=2 + span
-    )(hi, lo, *sources)
-    far = lax.ppermute(far, "band", [(i, (i + 1 if i % 2 else i - 1) % bands) for i in range(bands)])
-    odd_found = products("rest_odd", 1, rest[: span - 1], own_near)
+        return call(kernel, name, parts[0], inputs=4)(hi, lo, found, last)
+
+    far_near = call(functools.partial(near_kernel, width), "near", parts[0], inputs=2 + span)(
+        hi, lo, own_far, *sources[1:]
+    )
+    far = lax.ppermute(far_near, "band", [(i, (i + 1 if i % 2 else i - 1) % bands) for i in range(bands)])
+    odd_found = products("rest_odd", 1, rest[: span - 1], far_near)
     far_up = far_part("far_odd", 1, odd_found, rest[span - 1])
     up = lax.ppermute(far_up, "band", [(i, (i + 1) % bands) for i in range(bands)])
     even_found = products("rest_even", 0, rest[: span - 1], far_up)
     far_down = far_part("far_even", 0, even_found, rest[-1])
     down = lax.ppermute(far_down, "band", [((i + 1) % bands, i) for i in range(bands)])
-    own, chip = call(
+    own_near, own, chip = call(
         functools.partial(join_kernel, width),
         "join",
-        parts[:2],
-        in_specs=[pl.BlockSpec(memory_space=pl.ANY)] + [vmem()] * 6,
-    )(far_down, hi, lo, odd_found, rest[span - 1], even_found, rest[-1])
+        [parts[0], parts[0], (2 * width, parts[0][1])],
+        in_specs=[pl.BlockSpec(memory_space=pl.ANY)] + [vmem()] * (6 + span),
+    )(far_down, hi, lo, odd_found, rest[span - 1], even_found, rest[-1], *sources)
     chip = lax.ppermute(chip, "band", [(i, i ^ 1) for i in range(bands)])
     whole = (width, 5 * groups * width)
     slow = pl.CostEstimate(flops=4000000000, bytes_accessed=2000000, transcendentals=0)

time: 18.2 us -> 18.1 us (level)
  waiting for transfers between devices: 2.36 us -> 1.93 us
  Pallas kernels: 3.47 us -> 3.85 us
    ppermute x1, waiting for transfers between devices: 0.82 us -> 0.01 us  [body(): chip = lax.ppermute(chip, 'band', [(i, i ^ 1) for i in range(bands)])]
    ppermute x1, waiting for transfers between devices: 1.52 us -> 1.85 us  [body(): lax.ppermute(far_down, 'band', [((i + 1) % bands, i) for i in range(bands)])]
    pallas_call x4, Pallas kernels: 1.35 us -> 1.66 us  [the longest x1 0.9 us: body(): call(functools.partial(join_kernel, width), 'join', [parts[0], parts[0],...]
  transfers between devices with their start and end apart: 8 -> 8, of which waited for: 2 -> 2; matrix products, arithmetic and copies ran while one was open for 0% -> 0% of each run, Pallas kernels for 14% -> 16%
where the time goes in v10:
time: 18.1 us; the launch traced here: 18 us
  starting transfers between devices  11.2 us (62%)
  Pallas kernels  3.85 us (21%)
  waiting for transfers between devices  1.93 us (11%)
  local copies, waits for them, and re-layouts  0.89 us (5%)
    ppermute x4, starting transfers between devices, gather(): return lax.ppermute(packed, ('blk', 'band'), to)  4.84 us
    ppermute x1, starting transfers between devices, body(): lax.ppermute(far_near, 'band', [(i, (i + 1 if i % 2 else i - 1) % bands)...  3.04 us
    ppermute x1, waiting for transfers between devices, body(): lax.ppermute(far_down, 'band', [((i + 1) % bands, i) for i in range(bands)])  1.85 us
    ppermute x1, starting transfers between devices, body(): lax.ppermute(far_up, 'band', [(i, (i + 1) % bands) for i in range(bands)])  1.77 us
    pallas_call x1, Pallas kernels, body(): call(functools.partial(join_kernel, width), 'join', [parts[0], parts[0],...  0.9 us
    unnamed x10, local copies, waits for them, and re-layouts  0.89 us
    pallas_call x1, Pallas kernels, body(): pl.pallas_call(functools.partial(left_kernel, width), out_shape=[jax.Shap...  0.88 us
    ppermute x1, starting transfers between devices, body(): lax.ppermute(far_down, 'band', [((i + 1) % bands, i) for i in range(bands)])  0.88 us
  transfers between devices with their start and end apart: 8, of which 2 were waited for; matrix products, arithmetic and copies ran while one was open for 0% of the time, Pallas kernels for 16%

profile of v10, /device:TPU:1, one launch (start us, length us, event | category | flops | bytes accessed | tf_op | source)
XLA Modules:
  0.0 18.0 jit_solution(15681494181348674275)
XLA Ops:
  0.0 0.0 copy-start
  0.0 0.0 copy-start.1
  0.0 0.0 copy-start.2
  0.0 0.9 %copy-done = f32[4,64,128]{2,1,0:T(8,128)S(1)} copy-done((f32[4,64,128]{2,1,0:T(8,128)S(1)}, f32[4,64,128]{2,1,0:T(8,128)}, u32[]{:S(2)}) %copy-start) | copy-done | bytes 131096
  0.9 0.0 copy-done.1
  0.9 0.0 copy-start.3
  0.9 0.1 pack.1.packed_ref.refs_4_
  1.0 2.1 %collective-permute-start = (f32[264,128]{1,0:T(8,128)S(1)}, f32[264,128]{1,0:T(8,128)S(1)}, u32[]{:S(2)}, u32[]{:S(2)}) collective-permute-start(f32[264,128]{1,0:T(8,128)S(1)} %pack.1.packed_ref.refs_4_), channel_id=1, source_target_pairs={{0,8},{1,9},{2,10},{3,11},{4,12},{5,13},{6,14},{7,15},{8,0},{9,1},... | collective-permute-start | bytes 405512 | tf_op jit(solution)/shard_map/ppermute | solution.py:264
  3.1 1.2 %collective-permute-start.1 = (f32[264,128]{1,0:T(8,128)S(1)}, f32[264,128]{1,0:T(8,128)S(1)}, u32[]{:S(2)}, u32[]{:S(2)}) collective-permute-start(f32[264,128]{1,0:T(8,128)S(1)} %pack.1.packed_ref.refs_4_), channel_id=1, source_target_pairs={{0,16},{1,17},{2,18},{3,19},{4,20},{5,21},{6,22},{7,23},{8,24},{9,... | collective-permute-start | bytes 405512 | tf_op jit(solution)/shard_map/ppermute | solution.py:264
  4.3 0.0 collective-permute-start.2
  4.4 1.5 %collective-permute-start.3 = (f32[264,128]{1,0:T(8,128)S(1)}, f32[264,128]{1,0:T(8,128)S(1)}, u32[]{:S(2)}, u32[]{:S(2)}) collective-permute-start(f32[264,128]{1,0:T(8,128)S(1)} %pack.1.packed_ref.refs_4_), channel_id=1, source_target_pairs={{0,24},{1,3},{2,26},{3,5},{4,28},{5,7},{6,30},{7,1},{8,16},{9,11},... | collective-permute-start | bytes 405512 | tf_op jit(solution)/shard_map/ppermute | solution.py:264
  5.8 0.0 copy-done.2
  5.8 0.0 copy-done.3
  5.8 0.0 copy-done.4
  5.8 0.9 %left.1 = (bf16[4,192,256]{2,1,0:T(8,128)(2,1)S(1)}, bf16[4,192,256]{2,1,0:T(8,128)(2,1)S(1)}, f32[64,256]{1,0:T(8,128)S(1)}) custom-call(s32[4,4]{1,0:T(4,128)S(1)} %copy-done.3, s32[4,4]{1,0:T(4,128)S(1)} %copy-done.4, s32[2,4]{1,0:T(2,128)S(1)} %bitcast.4, f32[4,64,256]{2,1,0:T(8,128)S(1)} %copy-done.2, f32[264,128]{1,0:T(8,128)S(1)} %pack.1.packed_ref.refs_4_), custom_call_target="tpu_custom_call" | custom-call | flops 301989888 | bytes 2000000 | tf_op jit(solution)/shard_map/left/pallas_call | solution.py:271
  6.7 0.0 collective-permute-done.refs_0_.refs_5_
  6.7 0.4 %near.1.earlier_ref = f32[64,384]{1,0:T(8,128)S(1)} custom-call(bf16[4,192,256]{2,1,0:T(8,128)(2,1)S(1)} %get-tuple-element.11.hi_ref, bf16[4,192,256]{2,1,0:T(8,128)(2,1)S(1)} %get-tuple-element.12.lo_ref, f32[64,256]{1,0:T(8,128)S(1)} %get-tuple-element.13.own_ref, f32[264,128]{1,0:T(8,128)S(1)} %collective-permute-done.refs_0_.refs_5_), custom_call_target="tpu_custom_call" | custom-call | tf_op jit(solution)/shard_map/near/pallas_call | solution.py:296
  7.1 3.0 %collective-permute-start.4 = (f32[64,384]{1,0:T(8,128)S(1)}, f32[64,384]{1,0:T(8,128)S(1)}, u32[]{:S(2)}, u32[]{:S(2)}) collective-permute-start(f32[64,384]{1,0:T(8,128)S(1)} %near.1.earlier_ref), channel_id=1, source_target_pairs={{0,7},{1,2},{2,1},{3,4},{4,3},{5,6},{6,5},{7,0},{8,15},{9,10},{10,... | collective-permute-start | bytes 294920 | tf_op jit(solution)/shard_map/ppermute | solution.py:299
  10.2 0.0 collective-permute-done.1.refs_0_
  10.2 0.3 %rest_odd.1.found_ref.refs_0_ = f32[1,192,256]{2,1,0:T(8,128)S(1)} custom-call(f32[64,384]{1,0:T(8,128)S(1)} %near.1.earlier_ref, bf16[4,192,256]{2,1,0:T(8,128)(2,1)S(1)} %get-tuple-element.11.hi_ref, bf16[4,192,256]{2,1,0:T(8,128)(2,1)S(1)} %get-tuple-element.12.lo_ref, f32[264,128]{1,0:T(8,128)S(1)} %collective-permute-done.1.refs_0_), custom_call_target="tpu_custom_call" | custom-call | tf_op jit(solution)/shard_map/rest_odd/pallas_call | solution.py:288
  10.5 0.1 collective-permute-done.2.last_ref.refs_1_
  10.6 0.4 %far_odd.1.earlier_ref = f32[64,384]{1,0:T(8,128)S(1)} custom-call(bf16[4,192,256]{2,1,0:T(8,128)(2,1)S(1)} %get-tuple-element.11.hi_ref, bf16[4,192,256]{2,1,0:T(8,128)(2,1)S(1)} %get-tuple-element.12.lo_ref, f32[1,192,256]{2,1,0:T(8,128)S(1)} %rest_odd.1.found_ref.refs_0_, f32[264,128]{1,0:T(8,128)S(1)} %collective-permute-done.2.last_ref.refs_1_), custom_call_target="tpu_custom_call" | custom-call | tf_op jit(solution)/shard_map/far_odd/pallas_call | solution.py:294
  11.0 1.8 %collective-permute-start.5 = (f32[64,384]{1,0:T(8,128)S(1)}, f32[64,384]{1,0:T(8,128)S(1)}, u32[]{:S(2)}, u32[]{:S(2)}) collective-permute-start(f32[64,384]{1,0:T(8,128)S(1)} %far_odd.1.earlier_ref), channel_id=1, source_target_pairs={{0,1},{1,2},{2,3},{3,4},{4,5},{5,6},{6,7},{7,0},{8,9},{9,10},{10,1... | collective-permute-start | bytes 294920 | tf_op jit(solution)/shard_map/ppermute | solution.py:302
  12.7 0.0 collective-permute-done.3.last_ref.refs_3_
  12.7 0.9 %collective-permute-start.6 = (f32[64,384]{1,0:T(8,128)S(1)}, f32[64,384]{1,0:T(8,128)S(1)}, u32[]{:S(2)}, u32[]{:S(2)}) collective-permute-start(f32[64,384]{1,0:T(8,128)S(1)} %far_even.1.earlier_ref), channel_id=1, source_target_pairs={{1,0},{2,1},{3,2},{4,3},{5,4},{6,5},{7,6},{0,7},{9,8},{10,9},{11,1... | collective-permute-start | bytes 294920 | tf_op jit(solution)/shard_map/ppermute | solution.py:305
  13.6 0.9 %join.1 = (f32[64,384]{1,0:T(8,128)S(1)}, f32[64,384]{1,0:T(8,128)S(1)}, f32[128,384]{1,0:T(8,128)S(1)}) custom-call(f32[64,384]{1,0:T(8,128)S(1)} %far_even.1.earlier_ref, bf16[4,192,256]{2,1,0:T(8,128)(2,1)S(1)} %get-tuple-element.11.hi_ref, bf16[4,192,256]{2,1,0:T(8,128)(2,1)S(1)} %get-tuple-element.12.lo_ref, ...), custom_call_target="tpu_custom_call" | custom-call | tf_op jit(solution)/shard_map/join/pallas_call | solution.py:306
  14.5 0.7 %collective-permute-start.7 = (f32[128,384]{1,0:T(8,128)S(1)}, f32[128,384]{1,0:T(8,128)S(1)}, u32[]{:S(2)}, u32[]{:S(2)}) collective-permute-start(f32[128,384]{1,0:T(8,128)S(1)} %get-tuple-element.16), channel_id=1, source_target_pairs={{0,1},{1,0},{2,3},{3,2},{4,5},{5,4},{6,7},{7,6},{8,9},{9,8},{10,11... | collective-permute-start | bytes 589832 | tf_op jit(solution)/shard_map/ppermute | solution.py:312
  15.2 0.0 collective-permute-done.4.far_ref
  15.3 0.0 collective-permute-done.5.up_ref
  15.4 1.8 %collective-permute-done.6.down_ref = f32[64,384]{1,0:T(8,128)S(1)} collective-permute-done((f32[64,384]{1,0:T(8,128)S(1)}, f32[64,384]{1,0:T(8,128)S(1)}, u32[]{:S(2)}, u32[]{:S(2)}) %collective-permute-start.6) | collective-permute-done | bytes 98336 | tf_op jit(solution)/shard_map/ppermute | solution.py:305
  17.2 0.0 collective-permute-done.7.chip_ref
  17.2 0.8 %late.1 = f32[64,1280]{1,0:T(8,128)} custom-call(f32[64,1280]{1,0:T(8,128)S(1)} %early.1.early_ref, f32[64,384]{1,0:T(8,128)S(1)} %collective-permute-done.6.down_ref, f32[128,384]{1,0:T(8,128)S(1)} %collective-permute-done.7.chip_ref), custom_call_target="tpu_custom_call" | custom-call | tf_op jit(solution)/shard_map/late/pallas_call | solution.py:319
  (6 shorter events, 0.1 us)
Async XLA Ops:
  0.0 0.9 %copy-start = (f32[4,64,128]{2,1,0:T(8,128)S(1)}, f32[4,64,128]{2,1,0:T(8,128)}, u32[]{:S(2)}) copy-start(f32[4,64,128]{2,1,0:T(8,128)} %param.8) | copy-start | bytes 393220
  0.0 0.9 %copy-start.1 = (s32[4,2]{0,1:T(2,128)S(1)}, s32[4,2]{0,1:T(2,128)}, u32[]{:S(2)}) copy-start(s32[4,2]{0,1:T(2,128)} %param.9) | copy-start | bytes 100
  0.0 5.8 %copy-start.2 = (f32[4,64,256]{2,1,0:T(8,128)S(1)}, f32[4,64,256]{2,1,0:T(8,128)}, u32[]{:S(2)}) copy-start(f32[4,64,256]{2,1,0:T(8,128)} %a_ref.1) | copy-start | bytes 786436
  0.9 4.9 %copy-start.3 = (s32[4,4]{1,0:T(4,128)S(1)}, s32[4,4]{1,0:T(4,128)}, u32[]{:S(2)}) copy-start(s32[4,4]{1,0:T(4,128)} %group_ref.1) | copy-start | bytes 196
  0.9 4.9 %copy-start.4 = (s32[4,4]{1,0:T(4,128)S(1)}, s32[4,4]{1,0:T(4,128)}, u32[]{:S(2)}) copy-start(s32[4,4]{1,0:T(4,128)} %row_ref.1) | copy-start | bytes 196
  1.0 5.7 %collective-permute-start = (f32[264,128]{1,0:T(8,128)S(1)}, f32[264,128]{1,0:T(8,128)S(1)}, u32[]{:S(2)}, u32[]{:S(2)}) collective-permute-start(f32[264,128]{1,0:T(8,128)S(1)} %pack.1.packed_ref.refs_4_), channel_id=1, source_target_pairs={{0,8},{1,9},{2,10},{3,11},{4,12},{5,13},{6,14},{7,15},{8,0},{9,1},... | collective-permute-start | bytes 405512 | tf_op jit(solution)/shard_map/ppermute | solution.py:264
  3.1 7.1 %collective-permute-start.1 = (f32[264,128]{1,0:T(8,128)S(1)}, f32[264,128]{1,0:T(8,128)S(1)}, u32[]{:S(2)}, u32[]{:S(2)}) collective-permute-start(f32[264,128]{1,0:T(8,128)S(1)} %pack.1.packed_ref.refs_4_), channel_id=1, source_target_pairs={{0,16},{1,17},{2,18},{3,19},{4,20},{5,21},{6,22},{7,23},{8,24},{9,... | collective-permute-start | bytes 405512 | tf_op jit(solution)/shard_map/ppermute | solution.py:264
  4.3 6.2 %collective-permute-start.2 = (f32[264,128]{1,0:T(8,128)S(1)}, f32[264,128]{1,0:T(8,128)S(1)}, u32[]{:S(2)}, u32[]{:S(2)}) collective-permute-start(f32[264,128]{1,0:T(8,128)S(1)} %pack.1.packed_ref.refs_4_), channel_id=1, source_target_pairs={{0,8},{1,25},{2,4},{3,27},{4,6},{5,29},{6,2},{7,31},{8,0},{9,17},{... | collective-permute-start | bytes 405512 | tf_op jit(solution)/shard_map/ppermute | solution.py:264
  4.4 8.4 %collective-permute-start.3 = (f32[264,128]{1,0:T(8,128)S(1)}, f32[264,128]{1,0:T(8,128)S(1)}, u32[]{:S(2)}, u32[]{:S(2)}) collective-permute-start(f32[264,128]{1,0:T(8,128)S(1)} %pack.1.packed_ref.refs_4_), channel_id=1, source_target_pairs={{0,24},{1,3},{2,26},{3,5},{4,28},{5,7},{6,30},{7,1},{8,16},{9,11},... | collective-permute-start | bytes 405512 | tf_op jit(solution)/shard_map/ppermute | solution.py:264
  7.1 8.1 %collective-permute-start.4 = (f32[64,384]{1,0:T(8,128)S(1)}, f32[64,384]{1,0:T(8,128)S(1)}, u32[]{:S(2)}, u32[]{:S(2)}) collective-permute-start(f32[64,384]{1,0:T(8,128)S(1)} %near.1.earlier_ref), channel_id=1, source_target_pairs={{0,7},{1,2},{2,1},{3,4},{4,3},{5,6},{6,5},{7,0},{8,15},{9,10},{10,... | collective-permute-start | bytes 294920 | tf_op jit(solution)/shard_map/ppermute | solution.py:299
  11.0 4.3 %collective-permute-start.5 = (f32[64,384]{1,0:T(8,128)S(1)}, f32[64,384]{1,0:T(8,128)S(1)}, u32[]{:S(2)}, u32[]{:S(2)}) collective-permute-start(f32[64,384]{1,0:T(8,128)S(1)} %far_odd.1.earlier_ref), channel_id=1, source_target_pairs={{0,1},{1,2},{2,3},{3,4},{4,5},{5,6},{6,7},{7,0},{8,9},{9,10},{10,1... | collective-permute-start | bytes 294920 | tf_op jit(solution)/shard_map/ppermute | solution.py:302
  12.7 4.5 %collective-permute-start.6 = (f32[64,384]{1,0:T(8,128)S(1)}, f32[64,384]{1,0:T(8,128)S(1)}, u32[]{:S(2)}, u32[]{:S(2)}) collective-permute-start(f32[64,384]{1,0:T(8,128)S(1)} %far_even.1.earlier_ref), channel_id=1, source_target_pairs={{1,0},{2,1},{3,2},{4,3},{5,4},{6,5},{7,6},{0,7},{9,8},{10,9},{11,1... | collective-permute-start | bytes 294920 | tf_op jit(solution)/shard_map/ppermute | solution.py:305
  14.5 2.7 %collective-permute-start.7 = (f32[128,384]{1,0:T(8,128)S(1)}, f32[128,384]{1,0:T(8,128)S(1)}, u32[]{:S(2)}, u32[]{:S(2)}) collective-permute-start(f32[128,384]{1,0:T(8,128)S(1)} %get-tuple-element.16), channel_id=1, source_target_pairs={{0,1},{1,0},{2,3},{3,2},{4,5},{5,4},{6,7},{7,6},{8,9},{9,8},{10,11... | collective-permute-start | bytes 589832 | tf_op jit(solution)/shard_map/ppermute | solution.py:312

commit v11 on v10

--- a/solution.py
+++ b/solution.py
@@ -249,7 +249,7 @@
 
     def idle(b, r):
         if r % 2:
-            return b, (r + 2) % bands
+            return b, r ^ 2
         if r == 0:
             return b ^ 1, r
         return b, r + 2 if r + 2 < bands else 2

time: 18.1 us -> 18.1 us (level)
  no operation moved by 1% of the time
where the time goes in v11:
time: 18.1 us; the launch traced here: 18 us
  starting transfers between devices  11.2 us (62%)
  Pallas kernels  3.85 us (21%)
  waiting for transfers between devices  1.93 us (11%)
  local copies, waits for them, and re-layouts  0.89 us (5%)
    ppermute x4, starting transfers between devices, gather(): return lax.ppermute(packed, ('blk', 'band'), to)  4.84 us
    ppermute x1, starting transfers between devices, body(): lax.ppermute(far_near, 'band', [(i, (i + 1 if i % 2 else i - 1) % bands)...  3.04 us
    ppermute x1, waiting for transfers between devices, body(): lax.ppermute(far_down, 'band', [((i + 1) % bands, i) for i in range(bands)])  1.85 us
    ppermute x1, starting transfers between devices, body(): lax.ppermute(far_up, 'band', [(i, (i + 1) % bands) for i in range(bands)])  1.83 us
    pallas_call x1, Pallas kernels, body(): call(functools.partial(join_kernel, width), 'join', [parts[0], parts[0],...  0.9 us
    unnamed x10, local copies, waits for them, and re-layouts  0.89 us
    pallas_call x1, Pallas kernels, body(): pl.pallas_call(functools.partial(left_kernel, width), out_shape=[jax.Shap...  0.88 us
    ppermute x1, starting transfers between devices, body(): lax.ppermute(far_down, 'band', [((i + 1) % bands, i) for i in range(bands)])  0.81 us
  transfers between devices with their start and end apart: 8, of which 2 were waited for; matrix products, arithmetic and copies ran while one was open for 0% of the time, Pallas kernels for 16%

profile of v11, /device:TPU:1, one launch (start us, length us, event | category | flops | bytes accessed | tf_op | source)
XLA Modules:
  0.0 18.0 jit_solution(6185005744645850957)
XLA Ops:
  0.0 0.0 copy-start
  0.0 0.0 copy-start.1
  0.0 0.0 copy-start.2
  0.0 0.9 %copy-done = f32[4,64,128]{2,1,0:T(8,128)S(1)} copy-done((f32[4,64,128]{2,1,0:T(8,128)S(1)}, f32[4,64,128]{2,1,0:T(8,128)}, u32[]{:S(2)}) %copy-start) | copy-done | bytes 131096
  0.9 0.0 copy-done.1
  0.9 0.0 copy-start.3
  0.9 0.1 pack.1.packed_ref.refs_4_
  1.0 2.1 %collective-permute-start = (f32[264,128]{1,0:T(8,128)S(1)}, f32[264,128]{1,0:T(8,128)S(1)}, u32[]{:S(2)}, u32[]{:S(2)}) collective-permute-start(f32[264,128]{1,0:T(8,128)S(1)} %pack.1.packed_ref.refs_4_), channel_id=1, source_target_pairs={{0,8},{1,9},{2,10},{3,11},{4,12},{5,13},{6,14},{7,15},{8,0},{9,1},... | collective-permute-start | bytes 405512 | tf_op jit(solution)/shard_map/ppermute | solution.py:264
  3.1 1.2 %collective-permute-start.1 = (f32[264,128]{1,0:T(8,128)S(1)}, f32[264,128]{1,0:T(8,128)S(1)}, u32[]{:S(2)}, u32[]{:S(2)}) collective-permute-start(f32[264,128]{1,0:T(8,128)S(1)} %pack.1.packed_ref.refs_4_), channel_id=1, source_target_pairs={{0,16},{1,17},{2,18},{3,19},{4,20},{5,21},{6,22},{7,23},{8,24},{9,... | collective-permute-start | bytes 405512 | tf_op jit(solution)/shard_map/ppermute | solution.py:264
  4.3 0.0 collective-permute-start.2
  4.4 1.5 %collective-permute-start.3 = (f32[264,128]{1,0:T(8,128)S(1)}, f32[264,128]{1,0:T(8,128)S(1)}, u32[]{:S(2)}, u32[]{:S(2)}) collective-permute-start(f32[264,128]{1,0:T(8,128)S(1)} %pack.1.packed_ref.refs_4_), channel_id=1, source_target_pairs={{0,24},{1,3},{2,26},{3,1},{4,28},{5,7},{6,30},{7,5},{8,16},{9,11},... | collective-permute-start | bytes 405512 | tf_op jit(solution)/shard_map/ppermute | solution.py:264
  5.8 0.0 copy-done.2
  5.8 0.0 copy-done.3
  5.8 0.0 copy-done.4
  5.8 0.9 %left.1 = (bf16[4,192,256]{2,1,0:T(8,128)(2,1)S(1)}, bf16[4,192,256]{2,1,0:T(8,128)(2,1)S(1)}, f32[64,256]{1,0:T(8,128)S(1)}) custom-call(s32[4,4]{1,0:T(4,128)S(1)} %copy-done.3, s32[4,4]{1,0:T(4,128)S(1)} %copy-done.4, s32[2,4]{1,0:T(2,128)S(1)} %bitcast.4, f32[4,64,256]{2,1,0:T(8,128)S(1)} %copy-done.2, f32[264,128]{1,0:T(8,128)S(1)} %pack.1.packed_ref.refs_4_), custom_call_target="tpu_custom_call" | custom-call | flops 301989888 | bytes 2000000 | tf_op jit(solution)/shard_map/left/pallas_call | solution.py:271
  6.7 0.0 collective-permute-done.refs_0_.refs_5_
  6.7 0.4 %near.1.earlier_ref = f32[64,384]{1,0:T(8,128)S(1)} custom-call(bf16[4,192,256]{2,1,0:T(8,128)(2,1)S(1)} %get-tuple-element.11.hi_ref, bf16[4,192,256]{2,1,0:T(8,128)(2,1)S(1)} %get-tuple-element.12.lo_ref, f32[64,256]{1,0:T(8,128)S(1)} %get-tuple-element.13.own_ref, f32[264,128]{1,0:T(8,128)S(1)} %collective-permute-done.refs_0_.refs_5_), custom_call_target="tpu_custom_call" | custom-call | tf_op jit(solution)/shard_map/near/pallas_call | solution.py:296
  7.1 3.0 %collective-permute-start.4 = (f32[64,384]{1,0:T(8,128)S(1)}, f32[64,384]{1,0:T(8,128)S(1)}, u32[]{:S(2)}, u32[]{:S(2)}) collective-permute-start(f32[64,384]{1,0:T(8,128)S(1)} %near.1.earlier_ref), channel_id=1, source_target_pairs={{0,7},{1,2},{2,1},{3,4},{4,3},{5,6},{6,5},{7,0},{8,15},{9,10},{10,... | collective-permute-start | bytes 294920 | tf_op jit(solution)/shard_map/ppermute | solution.py:299
  10.2 0.0 collective-permute-done.1.refs_0_
  10.2 0.3 %rest_odd.1.found_ref.refs_0_ = f32[1,192,256]{2,1,0:T(8,128)S(1)} custom-call(f32[64,384]{1,0:T(8,128)S(1)} %near.1.earlier_ref, bf16[4,192,256]{2,1,0:T(8,128)(2,1)S(1)} %get-tuple-element.11.hi_ref, bf16[4,192,256]{2,1,0:T(8,128)(2,1)S(1)} %get-tuple-element.12.lo_ref, f32[264,128]{1,0:T(8,128)S(1)} %collective-permute-done.1.refs_0_), custom_call_target="tpu_custom_call" | custom-call | tf_op jit(solution)/shard_map/rest_odd/pallas_call | solution.py:288
  10.5 0.1 collective-permute-done.2.last_ref.refs_1_
  10.6 0.4 %far_odd.1.earlier_ref = f32[64,384]{1,0:T(8,128)S(1)} custom-call(bf16[4,192,256]{2,1,0:T(8,128)(2,1)S(1)} %get-tuple-element.11.hi_ref, bf16[4,192,256]{2,1,0:T(8,128)(2,1)S(1)} %get-tuple-element.12.lo_ref, f32[1,192,256]{2,1,0:T(8,128)S(1)} %rest_odd.1.found_ref.refs_0_, f32[264,128]{1,0:T(8,128)S(1)} %collective-permute-done.2.last_ref.refs_1_), custom_call_target="tpu_custom_call" | custom-call | tf_op jit(solution)/shard_map/far_odd/pallas_call | solution.py:294
  11.0 1.8 %collective-permute-start.5 = (f32[64,384]{1,0:T(8,128)S(1)}, f32[64,384]{1,0:T(8,128)S(1)}, u32[]{:S(2)}, u32[]{:S(2)}) collective-permute-start(f32[64,384]{1,0:T(8,128)S(1)} %far_odd.1.earlier_ref), channel_id=1, source_target_pairs={{0,1},{1,2},{2,3},{3,4},{4,5},{5,6},{6,7},{7,0},{8,9},{9,10},{10,1... | collective-permute-start | bytes 294920 | tf_op jit(solution)/shard_map/ppermute | solution.py:302
  12.8 0.0 collective-permute-done.3.last_ref.refs_3_
  12.8 0.8 %collective-permute-start.6 = (f32[64,384]{1,0:T(8,128)S(1)}, f32[64,384]{1,0:T(8,128)S(1)}, u32[]{:S(2)}, u32[]{:S(2)}) collective-permute-start(f32[64,384]{1,0:T(8,128)S(1)} %far_even.1.earlier_ref), channel_id=1, source_target_pairs={{1,0},{2,1},{3,2},{4,3},{5,4},{6,5},{7,6},{0,7},{9,8},{10,9},{11,1... | collective-permute-start | bytes 294920 | tf_op jit(solution)/shard_map/ppermute | solution.py:305
  13.6 0.9 %join.1 = (f32[64,384]{1,0:T(8,128)S(1)}, f32[64,384]{1,0:T(8,128)S(1)}, f32[128,384]{1,0:T(8,128)S(1)}) custom-call(f32[64,384]{1,0:T(8,128)S(1)} %far_even.1.earlier_ref, bf16[4,192,256]{2,1,0:T(8,128)(2,1)S(1)} %get-tuple-element.11.hi_ref, bf16[4,192,256]{2,1,0:T(8,128)(2,1)S(1)} %get-tuple-element.12.lo_ref, ...), custom_call_target="tpu_custom_call" | custom-call | tf_op jit(solution)/shard_map/join/pallas_call | solution.py:306
  14.5 0.7 %collective-permute-start.7 = (f32[128,384]{1,0:T(8,128)S(1)}, f32[128,384]{1,0:T(8,128)S(1)}, u32[]{:S(2)}, u32[]{:S(2)}) collective-permute-start(f32[128,384]{1,0:T(8,128)S(1)} %get-tuple-element.16), channel_id=1, source_target_pairs={{0,1},{1,0},{2,3},{3,2},{4,5},{5,4},{6,7},{7,6},{8,9},{9,8},{10,11... | collective-permute-start | bytes 589832 | tf_op jit(solution)/shard_map/ppermute | solution.py:312
  15.2 0.0 collective-permute-done.4.far_ref
  15.3 0.0 collective-permute-done.5.up_ref
  15.4 1.8 %collective-permute-done.6.down_ref = f32[64,384]{1,0:T(8,128)S(1)} collective-permute-done((f32[64,384]{1,0:T(8,128)S(1)}, f32[64,384]{1,0:T(8,128)S(1)}, u32[]{:S(2)}, u32[]{:S(2)}) %collective-permute-start.6) | collective-permute-done | bytes 98336 | tf_op jit(solution)/shard_map/ppermute | solution.py:305
  17.2 0.0 collective-permute-done.7.chip_ref
  17.2 0.8 %late.1 = f32[64,1280]{1,0:T(8,128)} custom-call(f32[64,1280]{1,0:T(8,128)S(1)} %early.1.early_ref, f32[64,384]{1,0:T(8,128)S(1)} %collective-permute-done.6.down_ref, f32[128,384]{1,0:T(8,128)S(1)} %collective-permute-done.7.chip_ref), custom_call_target="tpu_custom_call" | custom-call | tf_op jit(solution)/shard_map/late/pallas_call | solution.py:319
  (6 shorter events, 0.1 us)
Async XLA Ops:
  0.0 0.9 %copy-start = (f32[4,64,128]{2,1,0:T(8,128)S(1)}, f32[4,64,128]{2,1,0:T(8,128)}, u32[]{:S(2)}) copy-start(f32[4,64,128]{2,1,0:T(8,128)} %param.8) | copy-start | bytes 393220
  0.0 0.9 %copy-start.1 = (s32[4,2]{0,1:T(2,128)S(1)}, s32[4,2]{0,1:T(2,128)}, u32[]{:S(2)}) copy-start(s32[4,2]{0,1:T(2,128)} %param.9) | copy-start | bytes 100
  0.0 5.8 %copy-start.2 = (f32[4,64,256]{2,1,0:T(8,128)S(1)}, f32[4,64,256]{2,1,0:T(8,128)}, u32[]{:S(2)}) copy-start(f32[4,64,256]{2,1,0:T(8,128)} %a_ref.1) | copy-start | bytes 786436
  0.9 4.9 %copy-start.3 = (s32[4,4]{1,0:T(4,128)S(1)}, s32[4,4]{1,0:T(4,128)}, u32[]{:S(2)}) copy-start(s32[4,4]{1,0:T(4,128)} %group_ref.1) | copy-start | bytes 196
  0.9 4.9 %copy-start.4 = (s32[4,4]{1,0:T(4,128)S(1)}, s32[4,4]{1,0:T(4,128)}, u32[]{:S(2)}) copy-start(s32[4,4]{1,0:T(4,128)} %row_ref.1) | copy-start | bytes 196
  1.0 5.7 %collective-permute-start = (f32[264,128]{1,0:T(8,128)S(1)}, f32[264,128]{1,0:T(8,128)S(1)}, u32[]{:S(2)}, u32[]{:S(2)}) collective-permute-start(f32[264,128]{1,0:T(8,128)S(1)} %pack.1.packed_ref.refs_4_), channel_id=1, source_target_pairs={{0,8},{1,9},{2,10},{3,11},{4,12},{5,13},{6,14},{7,15},{8,0},{9,1},... | collective-permute-start | bytes 405512 | tf_op jit(solution)/shard_map/ppermute | solution.py:264
  3.1 7.1 %collective-permute-start.1 = (f32[264,128]{1,0:T(8,128)S(1)}, f32[264,128]{1,0:T(8,128)S(1)}, u32[]{:S(2)}, u32[]{:S(2)}) collective-permute-start(f32[264,128]{1,0:T(8,128)S(1)} %pack.1.packed_ref.refs_4_), channel_id=1, source_target_pairs={{0,16},{1,17},{2,18},{3,19},{4,20},{5,21},{6,22},{7,23},{8,24},{9,... | collective-permute-start | bytes 405512 | tf_op jit(solution)/shard_map/ppermute | solution.py:264
  4.3 6.2 %collective-permute-start.2 = (f32[264,128]{1,0:T(8,128)S(1)}, f32[264,128]{1,0:T(8,128)S(1)}, u32[]{:S(2)}, u32[]{:S(2)}) collective-permute-start(f32[264,128]{1,0:T(8,128)S(1)} %pack.1.packed_ref.refs_4_), channel_id=1, source_target_pairs={{0,8},{1,25},{2,4},{3,27},{4,6},{5,29},{6,2},{7,31},{8,0},{9,17},{... | collective-permute-start | bytes 405512 | tf_op jit(solution)/shard_map/ppermute | solution.py:264
  4.4 8.4 %collective-permute-start.3 = (f32[264,128]{1,0:T(8,128)S(1)}, f32[264,128]{1,0:T(8,128)S(1)}, u32[]{:S(2)}, u32[]{:S(2)}) collective-permute-start(f32[264,128]{1,0:T(8,128)S(1)} %pack.1.packed_ref.refs_4_), channel_id=1, source_target_pairs={{0,24},{1,3},{2,26},{3,1},{4,28},{5,7},{6,30},{7,5},{8,16},{9,11},... | collective-permute-start | bytes 405512 | tf_op jit(solution)/shard_map/ppermute | solution.py:264
  7.1 8.1 %collective-permute-start.4 = (f32[64,384]{1,0:T(8,128)S(1)}, f32[64,384]{1,0:T(8,128)S(1)}, u32[]{:S(2)}, u32[]{:S(2)}) collective-permute-start(f32[64,384]{1,0:T(8,128)S(1)} %near.1.earlier_ref), channel_id=1, source_target_pairs={{0,7},{1,2},{2,1},{3,4},{4,3},{5,6},{6,5},{7,0},{8,15},{9,10},{10,... | collective-permute-start | bytes 294920 | tf_op jit(solution)/shard_map/ppermute | solution.py:299
  11.0 4.3 %collective-permute-start.5 = (f32[64,384]{1,0:T(8,128)S(1)}, f32[64,384]{1,0:T(8,128)S(1)}, u32[]{:S(2)}, u32[]{:S(2)}) collective-permute-start(f32[64,384]{1,0:T(8,128)S(1)} %far_odd.1.earlier_ref), channel_id=1, source_target_pairs={{0,1},{1,2},{2,3},{3,4},{4,5},{5,6},{6,7},{7,0},{8,9},{9,10},{10,1... | collective-permute-start | bytes 294920 | tf_op jit(solution)/shard_map/ppermute | solution.py:302
  12.8 4.4 %collective-permute-start.6 = (f32[64,384]{1,0:T(8,128)S(1)}, f32[64,384]{1,0:T(8,128)S(1)}, u32[]{:S(2)}, u32[]{:S(2)}) collective-permute-start(f32[64,384]{1,0:T(8,128)S(1)} %far_even.1.earlier_ref), channel_id=1, source_target_pairs={{1,0},{2,1},{3,2},{4,3},{5,4},{6,5},{7,6},{0,7},{9,8},{10,9},{11,1... | collective-permute-start | bytes 294920 | tf_op jit(solution)/shard_map/ppermute | solution.py:305
  14.5 2.7 %collective-permute-start.7 = (f32[128,384]{1,0:T(8,128)S(1)}, f32[128,384]{1,0:T(8,128)S(1)}, u32[]{:S(2)}, u32[]{:S(2)}) collective-permute-start(f32[128,384]{1,0:T(8,128)S(1)} %get-tuple-element.16), channel_id=1, source_target_pairs={{0,1},{1,0},{2,3},{3,2},{4,5},{5,4},{6,7},{7,6},{8,9},{9,8},{10,11... | collective-permute-start | bytes 589832 | tf_op jit(solution)/shard_map/ppermute | solution.py:312

commit v12 on v11

--- a/solution.py
+++ b/solution.py
@@ -250,9 +250,9 @@
     def idle(b, r):
         if r % 2:
             return b, r ^ 2
-        if r == 0:
+        if r in (0, 2):
             return b ^ 1, r
-        return b, r + 2 if r + 2 < bands else 2
+        return b, r + 2 if r % 4 == 0 else r - 2
 
     def gather(offsets):
         to = []

time: 18.1 us -> 18.1 us (level)
    ppermute x1, starting transfers between devices: 0.81 us -> 1.58 us  [body(): lax.ppermute(far_down, 'band', [((i + 1) % bands, i) for i in range(bands)])]
    ppermute x1, starting transfers between devices: 1.83 us -> 1.07 us  [body(): lax.ppermute(far_up, 'band', [(i, (i + 1) % bands) for i in range(bands)])]
where the time goes in v12:
time: 18.1 us; the launch traced here: 18 us
  starting transfers between devices  11.1 us (61%)
  Pallas kernels  3.85 us (21%)
  waiting for transfers between devices  2.02 us (11%)
  local copies, waits for them, and re-layouts  0.89 us (5%)
    ppermute x4, starting transfers between devices, gather(): return lax.ppermute(packed, ('blk', 'band'), to)  4.84 us
    ppermute x1, starting transfers between devices, body(): lax.ppermute(far_near, 'band', [(i, (i + 1 if i % 2 else i - 1) % bands)...  2.96 us
    ppermute x1, waiting for transfers between devices, body(): lax.ppermute(far_down, 'band', [((i + 1) % bands, i) for i in range(bands)])  1.85 us
    ppermute x1, starting transfers between devices, body(): lax.ppermute(far_down, 'band', [((i + 1) % bands, i) for i in range(bands)])  1.58 us
    ppermute x1, starting transfers between devices, body(): lax.ppermute(far_up, 'band', [(i, (i + 1) % bands) for i in range(bands)])  1.07 us
    pallas_call x1, Pallas kernels, body(): call(functools.partial(join_kernel, width), 'join', [parts[0], parts[0],...  0.9 us
    unnamed x10, local copies, waits for them, and re-layouts  0.89 us
    pallas_call x1, Pallas kernels, body(): pl.pallas_call(functools.partial(left_kernel, width), out_shape=[jax.Shap...  0.88 us
  transfers between devices with their start and end apart: 8, of which 2 were waited for; matrix products, arithmetic and copies ran while one was open for 0% of the time, Pallas kernels for 16%

profile of v12, /device:TPU:1, one launch (start us, length us, event | category | flops | bytes accessed | tf_op | source)
XLA Modules:
  0.0 18.0 jit_solution(15370599722301372922)
XLA Ops:
  0.0 0.0 copy-start
  0.0 0.0 copy-start.1
  0.0 0.0 copy-start.2
  0.0 0.9 %copy-done = f32[4,64,128]{2,1,0:T(8,128)S(1)} copy-done((f32[4,64,128]{2,1,0:T(8,128)S(1)}, f32[4,64,128]{2,1,0:T(8,128)}, u32[]{:S(2)}) %copy-start) | copy-done | bytes 131096
  0.9 0.0 copy-done.1
  0.9 0.0 copy-start.3
  0.9 0.1 pack.1.packed_ref.refs_4_
  1.0 2.1 %collective-permute-start = (f32[264,128]{1,0:T(8,128)S(1)}, f32[264,128]{1,0:T(8,128)S(1)}, u32[]{:S(2)}, u32[]{:S(2)}) collective-permute-start(f32[264,128]{1,0:T(8,128)S(1)} %pack.1.packed_ref.refs_4_), channel_id=1, source_target_pairs={{0,8},{1,9},{2,10},{3,11},{4,12},{5,13},{6,14},{7,15},{8,0},{9,1},... | collective-permute-start | bytes 405512 | tf_op jit(solution)/shard_map/ppermute | solution.py:264
  3.1 1.2 %collective-permute-start.1 = (f32[264,128]{1,0:T(8,128)S(1)}, f32[264,128]{1,0:T(8,128)S(1)}, u32[]{:S(2)}, u32[]{:S(2)}) collective-permute-start(f32[264,128]{1,0:T(8,128)S(1)} %pack.1.packed_ref.refs_4_), channel_id=1, source_target_pairs={{0,16},{1,17},{2,18},{3,19},{4,20},{5,21},{6,22},{7,23},{8,24},{9,... | collective-permute-start | bytes 405512 | tf_op jit(solution)/shard_map/ppermute | solution.py:264
  4.3 0.0 collective-permute-start.2
  4.4 1.5 %collective-permute-start.3 = (f32[264,128]{1,0:T(8,128)S(1)}, f32[264,128]{1,0:T(8,128)S(1)}, u32[]{:S(2)}, u32[]{:S(2)}) collective-permute-start(f32[264,128]{1,0:T(8,128)S(1)} %pack.1.packed_ref.refs_4_), channel_id=1, source_target_pairs={{0,24},{1,3},{2,26},{3,1},{4,28},{5,7},{6,30},{7,5},{8,16},{9,11},... | collective-permute-start | bytes 405512 | tf_op jit(solution)/shard_map/ppermute | solution.py:264
  5.8 0.0 copy-done.2
  5.8 0.0 copy-done.3
  5.8 0.0 copy-done.4
  5.8 0.9 %left.1 = (bf16[4,192,256]{2,1,0:T(8,128)(2,1)S(1)}, bf16[4,192,256]{2,1,0:T(8,128)(2,1)S(1)}, f32[64,256]{1,0:T(8,128)S(1)}) custom-call(s32[4,4]{1,0:T(4,128)S(1)} %copy-done.3, s32[4,4]{1,0:T(4,128)S(1)} %copy-done.4, s32[2,4]{1,0:T(2,128)S(1)} %bitcast.4, f32[4,64,256]{2,1,0:T(8,128)S(1)} %copy-done.2, f32[264,128]{1,0:T(8,128)S(1)} %pack.1.packed_ref.refs_4_), custom_call_target="tpu_custom_call" | custom-call | flops 301989888 | bytes 2000000 | tf_op jit(solution)/shard_map/left/pallas_call | solution.py:271
  6.7 0.0 collective-permute-done.refs_0_.refs_5_
  6.7 0.4 %near.1.earlier_ref = f32[64,384]{1,0:T(8,128)S(1)} custom-call(bf16[4,192,256]{2,1,0:T(8,128)(2,1)S(1)} %get-tuple-element.11.hi_ref, bf16[4,192,256]{2,1,0:T(8,128)(2,1)S(1)} %get-tuple-element.12.lo_ref, f32[64,256]{1,0:T(8,128)S(1)} %get-tuple-element.13.own_ref, f32[264,128]{1,0:T(8,128)S(1)} %collective-permute-done.refs_0_.refs_5_), custom_call_target="tpu_custom_call" | custom-call | tf_op jit(solution)/shard_map/near/pallas_call | solution.py:296
  7.1 3.0 %collective-permute-start.4 = (f32[64,384]{1,0:T(8,128)S(1)}, f32[64,384]{1,0:T(8,128)S(1)}, u32[]{:S(2)}, u32[]{:S(2)}) collective-permute-start(f32[64,384]{1,0:T(8,128)S(1)} %near.1.earlier_ref), channel_id=1, source_target_pairs={{0,7},{1,2},{2,1},{3,4},{4,3},{5,6},{6,5},{7,0},{8,15},{9,10},{10,... | collective-permute-start | bytes 294920 | tf_op jit(solution)/shard_map/ppermute | solution.py:299
  10.1 0.0 collective-permute-done.1.refs_0_
  10.1 0.3 %rest_odd.1.found_ref.refs_0_ = f32[1,192,256]{2,1,0:T(8,128)S(1)} custom-call(f32[64,384]{1,0:T(8,128)S(1)} %near.1.earlier_ref, bf16[4,192,256]{2,1,0:T(8,128)(2,1)S(1)} %get-tuple-element.11.hi_ref, bf16[4,192,256]{2,1,0:T(8,128)(2,1)S(1)} %get-tuple-element.12.lo_ref, f32[264,128]{1,0:T(8,128)S(1)} %collective-permute-done.1.refs_0_), custom_call_target="tpu_custom_call" | custom-call | tf_op jit(solution)/shard_map/rest_odd/pallas_call | solution.py:288
  10.4 0.2 collective-permute-done.2.last_ref.refs_1_
  10.6 0.4 %far_odd.1.earlier_ref = f32[64,384]{1,0:T(8,128)S(1)} custom-call(bf16[4,192,256]{2,1,0:T(8,128)(2,1)S(1)} %get-tuple-element.11.hi_ref, bf16[4,192,256]{2,1,0:T(8,128)(2,1)S(1)} %get-tuple-element.12.lo_ref, f32[1,192,256]{2,1,0:T(8,128)S(1)} %rest_odd.1.found_ref.refs_0_, f32[264,128]{1,0:T(8,128)S(1)} %collective-permute-done.2.last_ref.refs_1_), custom_call_target="tpu_custom_call" | custom-call | tf_op jit(solution)/shard_map/far_odd/pallas_call | solution.py:294
  11.0 1.1 %collective-permute-start.5 = (f32[64,384]{1,0:T(8,128)S(1)}, f32[64,384]{1,0:T(8,128)S(1)}, u32[]{:S(2)}, u32[]{:S(2)}) collective-permute-start(f32[64,384]{1,0:T(8,128)S(1)} %far_odd.1.earlier_ref), channel_id=1, source_target_pairs={{0,1},{1,2},{2,3},{3,4},{4,5},{5,6},{6,7},{7,0},{8,9},{9,10},{10,1... | collective-permute-start | bytes 294920 | tf_op jit(solution)/shard_map/ppermute | solution.py:302
  12.0 0.0 collective-permute-done.3.last_ref.refs_3_
  12.0 1.6 %collective-permute-start.6 = (f32[64,384]{1,0:T(8,128)S(1)}, f32[64,384]{1,0:T(8,128)S(1)}, u32[]{:S(2)}, u32[]{:S(2)}) collective-permute-start(f32[64,384]{1,0:T(8,128)S(1)} %far_even.1.earlier_ref), channel_id=1, source_target_pairs={{1,0},{2,1},{3,2},{4,3},{5,4},{6,5},{7,6},{0,7},{9,8},{10,9},{11,1... | collective-permute-start | bytes 294920 | tf_op jit(solution)/shard_map/ppermute | solution.py:305
  13.6 0.9 %join.1 = (f32[64,384]{1,0:T(8,128)S(1)}, f32[64,384]{1,0:T(8,128)S(1)}, f32[128,384]{1,0:T(8,128)S(1)}) custom-call(f32[64,384]{1,0:T(8,128)S(1)} %far_even.1.earlier_ref, bf16[4,192,256]{2,1,0:T(8,128)(2,1)S(1)} %get-tuple-element.11.hi_ref, bf16[4,192,256]{2,1,0:T(8,128)(2,1)S(1)} %get-tuple-element.12.lo_ref, ...), custom_call_target="tpu_custom_call" | custom-call | tf_op jit(solution)/shard_map/join/pallas_call | solution.py:306
  14.5 0.7 %collective-permute-start.7 = (f32[128,384]{1,0:T(8,128)S(1)}, f32[128,384]{1,0:T(8,128)S(1)}, u32[]{:S(2)}, u32[]{:S(2)}) collective-permute-start(f32[128,384]{1,0:T(8,128)S(1)} %get-tuple-element.16), channel_id=1, source_target_pairs={{0,1},{1,0},{2,3},{3,2},{4,5},{5,4},{6,7},{7,6},{8,9},{9,8},{10,11... | collective-permute-start | bytes 589832 | tf_op jit(solution)/shard_map/ppermute | solution.py:312
  15.2 0.0 collective-permute-done.4.far_ref
  15.3 0.0 collective-permute-done.5.up_ref
  15.4 1.8 %collective-permute-done.6.down_ref = f32[64,384]{1,0:T(8,128)S(1)} collective-permute-done((f32[64,384]{1,0:T(8,128)S(1)}, f32[64,384]{1,0:T(8,128)S(1)}, u32[]{:S(2)}, u32[]{:S(2)}) %collective-permute-start.6) | collective-permute-done | bytes 98336 | tf_op jit(solution)/shard_map/ppermute | solution.py:305
  17.2 0.0 collective-permute-done.7.chip_ref
  17.2 0.8 %late.1 = f32[64,1280]{1,0:T(8,128)} custom-call(f32[64,1280]{1,0:T(8,128)S(1)} %early.1.early_ref, f32[64,384]{1,0:T(8,128)S(1)} %collective-permute-done.6.down_ref, f32[128,384]{1,0:T(8,128)S(1)} %collective-permute-done.7.chip_ref), custom_call_target="tpu_custom_call" | custom-call | tf_op jit(solution)/shard_map/late/pallas_call | solution.py:319
  (6 shorter events, 0.1 us)
Async XLA Ops:
  0.0 0.9 %copy-start = (f32[4,64,128]{2,1,0:T(8,128)S(1)}, f32[4,64,128]{2,1,0:T(8,128)}, u32[]{:S(2)}) copy-start(f32[4,64,128]{2,1,0:T(8,128)} %param.8) | copy-start | bytes 393220
  0.0 0.9 %copy-start.1 = (s32[4,2]{0,1:T(2,128)S(1)}, s32[4,2]{0,1:T(2,128)}, u32[]{:S(2)}) copy-start(s32[4,2]{0,1:T(2,128)} %param.9) | copy-start | bytes 100
  0.0 5.8 %copy-start.2 = (f32[4,64,256]{2,1,0:T(8,128)S(1)}, f32[4,64,256]{2,1,0:T(8,128)}, u32[]{:S(2)}) copy-start(f32[4,64,256]{2,1,0:T(8,128)} %a_ref.1) | copy-start | bytes 786436
  0.9 4.9 %copy-start.3 = (s32[4,4]{1,0:T(4,128)S(1)}, s32[4,4]{1,0:T(4,128)}, u32[]{:S(2)}) copy-start(s32[4,4]{1,0:T(4,128)} %group_ref.1) | copy-start | bytes 196
  0.9 4.9 %copy-start.4 = (s32[4,4]{1,0:T(4,128)S(1)}, s32[4,4]{1,0:T(4,128)}, u32[]{:S(2)}) copy-start(s32[4,4]{1,0:T(4,128)} %row_ref.1) | copy-start | bytes 196
  1.0 5.7 %collective-permute-start = (f32[264,128]{1,0:T(8,128)S(1)}, f32[264,128]{1,0:T(8,128)S(1)}, u32[]{:S(2)}, u32[]{:S(2)}) collective-permute-start(f32[264,128]{1,0:T(8,128)S(1)} %pack.1.packed_ref.refs_4_), channel_id=1, source_target_pairs={{0,8},{1,9},{2,10},{3,11},{4,12},{5,13},{6,14},{7,15},{8,0},{9,1},... | collective-permute-start | bytes 405512 | tf_op jit(solution)/shard_map/ppermute | solution.py:264
  3.1 7.0 %collective-permute-start.1 = (f32[264,128]{1,0:T(8,128)S(1)}, f32[264,128]{1,0:T(8,128)S(1)}, u32[]{:S(2)}, u32[]{:S(2)}) collective-permute-start(f32[264,128]{1,0:T(8,128)S(1)} %pack.1.packed_ref.refs_4_), channel_id=1, source_target_pairs={{0,16},{1,17},{2,18},{3,19},{4,20},{5,21},{6,22},{7,23},{8,24},{9,... | collective-permute-start | bytes 405512 | tf_op jit(solution)/shard_map/ppermute | solution.py:264
  4.3 6.2 %collective-permute-start.2 = (f32[264,128]{1,0:T(8,128)S(1)}, f32[264,128]{1,0:T(8,128)S(1)}, u32[]{:S(2)}, u32[]{:S(2)}) collective-permute-start(f32[264,128]{1,0:T(8,128)S(1)} %pack.1.packed_ref.refs_4_), channel_id=1, source_target_pairs={{0,8},{1,25},{2,10},{3,27},{4,6},{5,29},{6,4},{7,31},{8,0},{9,17},... | collective-permute-start | bytes 405512 | tf_op jit(solution)/shard_map/ppermute | solution.py:264
  4.4 7.7 %collective-permute-start.3 = (f32[264,128]{1,0:T(8,128)S(1)}, f32[264,128]{1,0:T(8,128)S(1)}, u32[]{:S(2)}, u32[]{:S(2)}) collective-permute-start(f32[264,128]{1,0:T(8,128)S(1)} %pack.1.packed_ref.refs_4_), channel_id=1, source_target_pairs={{0,24},{1,3},{2,26},{3,1},{4,28},{5,7},{6,30},{7,5},{8,16},{9,11},... | collective-permute-start | bytes 405512 | tf_op jit(solution)/shard_map/ppermute | solution.py:264
  7.1 8.1 %collective-permute-start.4 = (f32[64,384]{1,0:T(8,128)S(1)}, f32[64,384]{1,0:T(8,128)S(1)}, u32[]{:S(2)}, u32[]{:S(2)}) collective-permute-start(f32[64,384]{1,0:T(8,128)S(1)} %near.1.earlier_ref), channel_id=1, source_target_pairs={{0,7},{1,2},{2,1},{3,4},{4,3},{5,6},{6,5},{7,0},{8,15},{9,10},{10,... | collective-permute-start | bytes 294920 | tf_op jit(solution)/shard_map/ppermute | solution.py:299
  11.0 4.3 %collective-permute-start.5 = (f32[64,384]{1,0:T(8,128)S(1)}, f32[64,384]{1,0:T(8,128)S(1)}, u32[]{:S(2)}, u32[]{:S(2)}) collective-permute-start(f32[64,384]{1,0:T(8,128)S(1)} %far_odd.1.earlier_ref), channel_id=1, source_target_pairs={{0,1},{1,2},{2,3},{3,4},{4,5},{5,6},{6,7},{7,0},{8,9},{9,10},{10,1... | collective-permute-start | bytes 294920 | tf_op jit(solution)/shard_map/ppermute | solution.py:302
  12.0 5.2 %collective-permute-start.6 = (f32[64,384]{1,0:T(8,128)S(1)}, f32[64,384]{1,0:T(8,128)S(1)}, u32[]{:S(2)}, u32[]{:S(2)}) collective-permute-start(f32[64,384]{1,0:T(8,128)S(1)} %far_even.1.earlier_ref), channel_id=1, source_target_pairs={{1,0},{2,1},{3,2},{4,3},{5,4},{6,5},{7,6},{0,7},{9,8},{10,9},{11,1... | collective-permute-start | bytes 294920 | tf_op jit(solution)/shard_map/ppermute | solution.py:305
  14.5 2.7 %collective-permute-start.7 = (f32[128,384]{1,0:T(8,128)S(1)}, f32[128,384]{1,0:T(8,128)S(1)}, u32[]{:S(2)}, u32[]{:S(2)}) collective-permute-start(f32[128,384]{1,0:T(8,128)S(1)} %get-tuple-element.16), channel_id=1, source_target_pairs={{0,1},{1,0},{2,3},{3,2},{4,5},{5,4},{6,7},{7,6},{8,9},{9,8},{10,11... | collective-permute-start | bytes 589832 | tf_op jit(solution)/shard_map/ppermute | solution.py:312

commit v13 on v11

--- a/solution.py
+++ b/solution.py
@@ -26,7 +26,9 @@
 
 
 def dot3(a_hi, a_lo, b_hi, b_lo):
-    return dot(a_hi, b_hi) + (dot(a_hi, b_lo) + dot(a_lo, b_hi))
+    height = a_hi.shape[0]
+    both = dot(jnp.concatenate([a_hi, a_lo], axis=0), b_hi)
+    return both[:height] + (dot(a_hi, b_lo) + both[height:])
 
 
 def lanes_kernel(out_ref):

time: 18.1 us -> 18 us (level)
  no operation moved by 1% of the time
where the time goes in v13:
time: 18 us; the launch traced here: 17.9 us
  starting transfers between devices  11.2 us (62%)
  Pallas kernels  3.7 us (21%)
  waiting for transfers between devices  1.96 us (11%)
  local copies, waits for them, and re-layouts  0.89 us (5%)
    ppermute x4, starting transfers between devices, gather(): return lax.ppermute(packed, ('blk', 'band'), to)  4.84 us
    ppermute x1, starting transfers between devices, body(): lax.ppermute(far_near, 'band', [(i, (i + 1 if i % 2 else i - 1) % bands)...  3.04 us
    ppermute x1, starting transfers between devices, body(): lax.ppermute(far_up, 'band', [(i, (i + 1) % bands) for i in range(bands)])  1.85 us
    ppermute x1, waiting for transfers between devices, body(): lax.ppermute(far_down, 'band', [((i + 1) % bands, i) for i in range(bands)])  1.76 us
    unnamed x10, local copies, waits for them, and re-layouts  0.89 us
    pallas_call x1, Pallas kernels, body(): call(functools.partial(join_kernel, width), 'join', [parts[0], parts[0],...  0.89 us
    ppermute x1, starting transfers between devices, body(): lax.ppermute(far_down, 'band', [((i + 1) % bands, i) for i in range(bands)])  0.8 us
    pallas_call x1, Pallas kernels, body(): call(functools.partial(late_kernel, groups), 'late', whole, inputs=3)  0.79 us
  transfers between devices with their start and end apart: 8, of which 2 were waited for; matrix products, arithmetic and copies ran while one was open for 0% of the time, Pallas kernels for 16%

profile of v13, /device:TPU:1, one launch (start us, length us, event | category | flops | bytes accessed | tf_op | source)
XLA Modules:
  0.0 17.9 jit_solution(13144351368984913947)
XLA Ops:
  0.0 0.0 copy-start
  0.0 0.0 copy-start.1
  0.0 0.0 copy-start.2
  0.0 0.9 %copy-done = f32[4,64,128]{2,1,0:T(8,128)S(1)} copy-done((f32[4,64,128]{2,1,0:T(8,128)S(1)}, f32[4,64,128]{2,1,0:T(8,128)}, u32[]{:S(2)}) %copy-start) | copy-done | bytes 131096
  0.9 0.0 copy-done.1
  0.9 0.0 copy-start.4
  0.9 0.1 pack.1.packed_ref.refs_4_
  1.0 2.1 %collective-permute-start = (f32[264,128]{1,0:T(8,128)S(1)}, f32[264,128]{1,0:T(8,128)S(1)}, u32[]{:S(2)}, u32[]{:S(2)}) collective-permute-start(f32[264,128]{1,0:T(8,128)S(1)} %pack.1.packed_ref.refs_4_), channel_id=1, source_target_pairs={{0,8},{1,9},{2,10},{3,11},{4,12},{5,13},{6,14},{7,15},{8,0},{9,1},... | collective-permute-start | bytes 405512 | tf_op jit(solution)/shard_map/ppermute | solution.py:266
  3.1 1.2 %collective-permute-start.1 = (f32[264,128]{1,0:T(8,128)S(1)}, f32[264,128]{1,0:T(8,128)S(1)}, u32[]{:S(2)}, u32[]{:S(2)}) collective-permute-start(f32[264,128]{1,0:T(8,128)S(1)} %pack.1.packed_ref.refs_4_), channel_id=1, source_target_pairs={{0,16},{1,17},{2,18},{3,19},{4,20},{5,21},{6,22},{7,23},{8,24},{9,... | collective-permute-start | bytes 405512 | tf_op jit(solution)/shard_map/ppermute | solution.py:266
  4.3 0.0 collective-permute-start.2
  4.4 1.5 %collective-permute-start.3 = (f32[264,128]{1,0:T(8,128)S(1)}, f32[264,128]{1,0:T(8,128)S(1)}, u32[]{:S(2)}, u32[]{:S(2)}) collective-permute-start(f32[264,128]{1,0:T(8,128)S(1)} %pack.1.packed_ref.refs_4_), channel_id=1, source_target_pairs={{0,24},{1,3},{2,26},{3,1},{4,28},{5,7},{6,30},{7,5},{8,16},{9,11},... | collective-permute-start | bytes 405512 | tf_op jit(solution)/shard_map/ppermute | solution.py:266
  5.8 0.0 copy-done.2
  5.8 0.0 copy-done.3
  5.8 0.0 copy-done.4
  5.8 0.8 %left.1 = (bf16[4,192,256]{2,1,0:T(8,128)(2,1)S(1)}, bf16[4,192,256]{2,1,0:T(8,128)(2,1)S(1)}, f32[64,256]{1,0:T(8,128)S(1)}) custom-call(s32[4,4]{1,0:T(4,128)S(1)} %copy-done.3, s32[4,4]{1,0:T(4,128)S(1)} %copy-done.4, s32[2,4]{1,0:T(2,128)S(1)} %bitcast.4, f32[4,64,256]{2,1,0:T(8,128)S(1)} %copy-done.2, f32[264,128]{1,0:T(8,128)S(1)} %pack.1.packed_ref.refs_4_), custom_call_target="tpu_custom_call" | custom-call | flops 301989888 | bytes 2000000 | tf_op jit(solution)/shard_map/left/pallas_call | solution.py:273
  6.6 0.0 collective-permute-done.refs_0_.refs_5_
  6.7 0.4 %near.1.earlier_ref = f32[64,384]{1,0:T(8,128)S(1)} custom-call(bf16[4,192,256]{2,1,0:T(8,128)(2,1)S(1)} %get-tuple-element.11.hi_ref, bf16[4,192,256]{2,1,0:T(8,128)(2,1)S(1)} %get-tuple-element.12.lo_ref, f32[64,256]{1,0:T(8,128)S(1)} %get-tuple-element.13.own_ref, f32[264,128]{1,0:T(8,128)S(1)} %collective-permute-done.refs_0_.refs_5_), custom_call_target="tpu_custom_call" | custom-call | tf_op jit(solution)/shard_map/near/pallas_call | solution.py:298
  7.0 3.0 %collective-permute-start.4 = (f32[64,384]{1,0:T(8,128)S(1)}, f32[64,384]{1,0:T(8,128)S(1)}, u32[]{:S(2)}, u32[]{:S(2)}) collective-permute-start(f32[64,384]{1,0:T(8,128)S(1)} %near.1.earlier_ref), channel_id=1, source_target_pairs={{0,7},{1,2},{2,1},{3,4},{4,3},{5,6},{6,5},{7,0},{8,15},{9,10},{10,... | collective-permute-start | bytes 294920 | tf_op jit(solution)/shard_map/ppermute | solution.py:301
  10.1 0.0 collective-permute-done.1.refs_0_
  10.1 0.3 %rest_odd.1.found_ref.refs_0_ = f32[1,192,256]{2,1,0:T(8,128)S(1)} custom-call(f32[64,384]{1,0:T(8,128)S(1)} %near.1.earlier_ref, bf16[4,192,256]{2,1,0:T(8,128)(2,1)S(1)} %get-tuple-element.11.hi_ref, bf16[4,192,256]{2,1,0:T(8,128)(2,1)S(1)} %get-tuple-element.12.lo_ref, f32[264,128]{1,0:T(8,128)S(1)} %collective-permute-done.1.refs_0_), custom_call_target="tpu_custom_call" | custom-call | tf_op jit(solution)/shard_map/rest_odd/pallas_call | solution.py:290
  10.4 0.2 %collective-permute-done.2.last_ref.refs_1_ = f32[264,128]{1,0:T(8,128)S(1)} collective-permute-done((f32[264,128]{1,0:T(8,128)S(1)}, f32[264,128]{1,0:T(8,128)S(1)}, u32[]{:S(2)}, u32[]{:S(2)}) %collective-permute-start.2) | collective-permute-done | bytes 135200 | tf_op jit(solution)/shard_map/ppermute | solution.py:266
  10.6 0.4 %far_odd.1.earlier_ref = f32[64,384]{1,0:T(8,128)S(1)} custom-call(bf16[4,192,256]{2,1,0:T(8,128)(2,1)S(1)} %get-tuple-element.11.hi_ref, bf16[4,192,256]{2,1,0:T(8,128)(2,1)S(1)} %get-tuple-element.12.lo_ref, f32[1,192,256]{2,1,0:T(8,128)S(1)} %rest_odd.1.found_ref.refs_0_, f32[264,128]{1,0:T(8,128)S(1)} %collective-permute-done.2.last_ref.refs_1_), custom_call_target="tpu_custom_call" | custom-call | tf_op jit(solution)/shard_map/far_odd/pallas_call | solution.py:296
  10.9 1.9 %collective-permute-start.5 = (f32[64,384]{1,0:T(8,128)S(1)}, f32[64,384]{1,0:T(8,128)S(1)}, u32[]{:S(2)}, u32[]{:S(2)}) collective-permute-start(f32[64,384]{1,0:T(8,128)S(1)} %far_odd.1.earlier_ref), channel_id=1, source_target_pairs={{0,1},{1,2},{2,3},{3,4},{4,5},{5,6},{6,7},{7,0},{8,9},{9,10},{10,1... | collective-permute-start | bytes 294920 | tf_op jit(solution)/shard_map/ppermute | solution.py:304
  12.8 0.0 collective-permute-done.3.last_ref.refs_3_
  12.8 0.8 %collective-permute-start.6 = (f32[64,384]{1,0:T(8,128)S(1)}, f32[64,384]{1,0:T(8,128)S(1)}, u32[]{:S(2)}, u32[]{:S(2)}) collective-permute-start(f32[64,384]{1,0:T(8,128)S(1)} %far_even.1.earlier_ref), channel_id=1, source_target_pairs={{1,0},{2,1},{3,2},{4,3},{5,4},{6,5},{7,6},{0,7},{9,8},{10,9},{11,1... | collective-permute-start | bytes 294920 | tf_op jit(solution)/shard_map/ppermute | solution.py:307
  13.6 0.9 %join.1 = (f32[64,384]{1,0:T(8,128)S(1)}, f32[64,384]{1,0:T(8,128)S(1)}, f32[128,384]{1,0:T(8,128)S(1)}) custom-call(f32[64,384]{1,0:T(8,128)S(1)} %far_even.1.earlier_ref, bf16[4,192,256]{2,1,0:T(8,128)(2,1)S(1)} %get-tuple-element.11.hi_ref, bf16[4,192,256]{2,1,0:T(8,128)(2,1)S(1)} %get-tuple-element.12.lo_ref, ...), custom_call_target="tpu_custom_call" | custom-call | tf_op jit(solution)/shard_map/join/pallas_call | solution.py:308
  14.5 0.7 %collective-permute-start.7 = (f32[128,384]{1,0:T(8,128)S(1)}, f32[128,384]{1,0:T(8,128)S(1)}, u32[]{:S(2)}, u32[]{:S(2)}) collective-permute-start(f32[128,384]{1,0:T(8,128)S(1)} %get-tuple-element.16), channel_id=1, source_target_pairs={{0,1},{1,0},{2,3},{3,2},{4,5},{5,4},{6,7},{7,6},{8,9},{9,8},{10,11... | collective-permute-start | bytes 589832 | tf_op jit(solution)/shard_map/ppermute | solution.py:314
  15.2 0.0 collective-permute-done.4.far_ref
  15.3 0.0 collective-permute-done.5.up_ref
  15.3 1.8 %collective-permute-done.6.down_ref = f32[64,384]{1,0:T(8,128)S(1)} collective-permute-done((f32[64,384]{1,0:T(8,128)S(1)}, f32[64,384]{1,0:T(8,128)S(1)}, u32[]{:S(2)}, u32[]{:S(2)}) %collective-permute-start.6) | collective-permute-done | bytes 98336 | tf_op jit(solution)/shard_map/ppermute | solution.py:307
  17.1 0.0 collective-permute-done.7.chip_ref
  17.1 0.8 %late.1 = f32[64,1280]{1,0:T(8,128)} custom-call(f32[64,1280]{1,0:T(8,128)S(1)} %early.1.early_ref, f32[64,384]{1,0:T(8,128)S(1)} %collective-permute-done.6.down_ref, f32[128,384]{1,0:T(8,128)S(1)} %collective-permute-done.7.chip_ref), custom_call_target="tpu_custom_call" | custom-call | tf_op jit(solution)/shard_map/late/pallas_call | solution.py:321
  (6 shorter events, 0.1 us)
Async XLA Ops:
  0.0 0.9 %copy-start = (f32[4,64,128]{2,1,0:T(8,128)S(1)}, f32[4,64,128]{2,1,0:T(8,128)}, u32[]{:S(2)}) copy-start(f32[4,64,128]{2,1,0:T(8,128)} %param.8) | copy-start | bytes 393220
  0.0 0.9 %copy-start.1 = (s32[4,2]{0,1:T(2,128)S(1)}, s32[4,2]{0,1:T(2,128)}, u32[]{:S(2)}) copy-start(s32[4,2]{0,1:T(2,128)} %param.9) | copy-start | bytes 100
  0.0 5.8 %copy-start.2 = (f32[4,64,256]{2,1,0:T(8,128)S(1)}, f32[4,64,256]{2,1,0:T(8,128)}, u32[]{:S(2)}) copy-start(f32[4,64,256]{2,1,0:T(8,128)} %a_ref.1) | copy-start | bytes 786436
  0.9 4.9 %copy-start.3 = (s32[4,4]{1,0:T(4,128)S(1)}, s32[4,4]{1,0:T(4,128)}, u32[]{:S(2)}) copy-start(s32[4,4]{1,0:T(4,128)} %group_ref.1) | copy-start | bytes 196
  0.9 4.9 %copy-start.4 = (s32[4,4]{1,0:T(4,128)S(1)}, s32[4,4]{1,0:T(4,128)}, u32[]{:S(2)}) copy-start(s32[4,4]{1,0:T(4,128)} %row_ref.1) | copy-start | bytes 196
  1.0 5.7 %collective-permute-start = (f32[264,128]{1,0:T(8,128)S(1)}, f32[264,128]{1,0:T(8,128)S(1)}, u32[]{:S(2)}, u32[]{:S(2)}) collective-permute-start(f32[264,128]{1,0:T(8,128)S(1)} %pack.1.packed_ref.refs_4_), channel_id=1, source_target_pairs={{0,8},{1,9},{2,10},{3,11},{4,12},{5,13},{6,14},{7,15},{8,0},{9,1},... | collective-permute-start | bytes 405512 | tf_op jit(solution)/shard_map/ppermute | solution.py:266
  3.1 7.0 %collective-permute-start.1 = (f32[264,128]{1,0:T(8,128)S(1)}, f32[264,128]{1,0:T(8,128)S(1)}, u32[]{:S(2)}, u32[]{:S(2)}) collective-permute-start(f32[264,128]{1,0:T(8,128)S(1)} %pack.1.packed_ref.refs_4_), channel_id=1, source_target_pairs={{0,16},{1,17},{2,18},{3,19},{4,20},{5,21},{6,22},{7,23},{8,24},{9,... | collective-permute-start | bytes 405512 | tf_op jit(solution)/shard_map/ppermute | solution.py:266
  4.3 6.2 %collective-permute-start.2 = (f32[264,128]{1,0:T(8,128)S(1)}, f32[264,128]{1,0:T(8,128)S(1)}, u32[]{:S(2)}, u32[]{:S(2)}) collective-permute-start(f32[264,128]{1,0:T(8,128)S(1)} %pack.1.packed_ref.refs_4_), channel_id=1, source_target_pairs={{0,8},{1,25},{2,4},{3,27},{4,6},{5,29},{6,2},{7,31},{8,0},{9,17},{... | collective-permute-start | bytes 405512 | tf_op jit(solution)/shard_map/ppermute | solution.py:266
  4.4 8.4 %collective-permute-start.3 = (f32[264,128]{1,0:T(8,128)S(1)}, f32[264,128]{1,0:T(8,128)S(1)}, u32[]{:S(2)}, u32[]{:S(2)}) collective-permute-start(f32[264,128]{1,0:T(8,128)S(1)} %pack.1.packed_ref.refs_4_), channel_id=1, source_target_pairs={{0,24},{1,3},{2,26},{3,1},{4,28},{5,7},{6,30},{7,5},{8,16},{9,11},... | collective-permute-start | bytes 405512 | tf_op jit(solution)/shard_map/ppermute | solution.py:266
  7.0 8.2 %collective-permute-start.4 = (f32[64,384]{1,0:T(8,128)S(1)}, f32[64,384]{1,0:T(8,128)S(1)}, u32[]{:S(2)}, u32[]{:S(2)}) collective-permute-start(f32[64,384]{1,0:T(8,128)S(1)} %near.1.earlier_ref), channel_id=1, source_target_pairs={{0,7},{1,2},{2,1},{3,4},{4,3},{5,6},{6,5},{7,0},{8,15},{9,10},{10,... | collective-permute-start | bytes 294920 | tf_op jit(solution)/shard_map/ppermute | solution.py:301
  10.9 4.3 %collective-permute-start.5 = (f32[64,384]{1,0:T(8,128)S(1)}, f32[64,384]{1,0:T(8,128)S(1)}, u32[]{:S(2)}, u32[]{:S(2)}) collective-permute-start(f32[64,384]{1,0:T(8,128)S(1)} %far_odd.1.earlier_ref), channel_id=1, source_target_pairs={{0,1},{1,2},{2,3},{3,4},{4,5},{5,6},{6,7},{7,0},{8,9},{9,10},{10,1... | collective-permute-start | bytes 294920 | tf_op jit(solution)/shard_map/ppermute | solution.py:304
  12.8 4.3 %collective-permute-start.6 = (f32[64,384]{1,0:T(8,128)S(1)}, f32[64,384]{1,0:T(8,128)S(1)}, u32[]{:S(2)}, u32[]{:S(2)}) collective-permute-start(f32[64,384]{1,0:T(8,128)S(1)} %far_even.1.earlier_ref), channel_id=1, source_target_pairs={{1,0},{2,1},{3,2},{4,3},{5,4},{6,5},{7,6},{0,7},{9,8},{10,9},{11,1... | collective-permute-start | bytes 294920 | tf_op jit(solution)/shard_map/ppermute | solution.py:307
  14.5 2.6 %collective-permute-start.7 = (f32[128,384]{1,0:T(8,128)S(1)}, f32[128,384]{1,0:T(8,128)S(1)}, u32[]{:S(2)}, u32[]{:S(2)}) collective-permute-start(f32[128,384]{1,0:T(8,128)S(1)} %get-tuple-element.16), channel_id=1, source_target_pairs={{0,1},{1,0},{2,3},{3,2},{4,5},{5,4},{6,7},{7,6},{8,9},{9,8},{10,11... | collective-permute-start | bytes 589832 | tf_op jit(solution)/shard_map/ppermute | solution.py:314
